TPU v7x, 256 devices: a whole 4x4x8 slice. The times are simulated.
256 devices in a mesh: seq: 16 (over y_hi, z), tp: 2 (over y_lo), head: 8 (over x, core).
Axes of the slice: x: 4, y: 4 (y_hi: 2, y_lo: 2; y = y_hi * 2 + y_lo), z: 8, core: 2. Of those that a mesh axis runs over, the one named last changes fastest.
Arguments:
- tokens: bfloat16 [81920, 8192], P(('seq', 'head')), may hold values from -60 to 60
- kv_weight: bfloat16 [8192, 2048], P('seq', 'tp'), may hold values from -0.0625 to 0.0625
- lengths: int32 [2], replicated, may hold values from 20480 to 40960, as said below
- page_table: int32 [320], P(('seq', 'tp')), may hold values from 0 to 9, as said below
- queries: bfloat16 [2, 64, 8192], P(None, None, 'head'), may hold values from -180 to 180
- new_keys: bfloat16 [2, 64, 1024], P(None, None, 'head'), may hold values from -6 to 6
- new_values: bfloat16 [2, 64, 1024], P(None, None, 'head'), may hold values from -6 to 6
- positions: int32 [2, 64], replicated, may hold values from 1 to 40960
Outputs:
- kv_cache: bfloat16 [2, 320, 256, 1024], P(None, ('seq', 'tp'), None, 'head')
- scales: float32 [2, 1024], replicated
- attended: bfloat16 [2, 64, 8192], P(None, None, 'head')
Inputs may be any that keep to these rules, and one draw needn't show every extreme that they name: `lengths`: one of the two prompts has all 40960 tokens valid, the other at least half of them. `page_table`: each aligned group of 10 entries is a permutation of 0 to 9.
All inputs are finite; a program needn't handle non-finite values.
Results may differ from a plain program's by a relative error of at most 0.0041.
The roundings to bfloat16 on the way count: a program that leaves them out, or rounds other values in their place, can miss the bound.
Values may be sent and summed in bfloat16 or wider, within the bound.
No kernel may reach another device: no remote copies, remote signals or barrier semaphores. Data moves between devices by JAX's collectives and lax.ppermute only.
A program may use at most 128 MiB of HBM per device.

v0:
```python
import jax
import jax.numpy as jnp
from jax import lax
from jax.sharding import PartitionSpec as P

HD = 128
PAGE = 256
ROWS = 64


eps = 1e-05
clip_level = 2.5
masked_fill = -1e30


def body(tokens, kv_weight, lengths, page_table, queries, new_keys, new_values, positions):
    tok_rows = tokens.shape[0]
    n_seq = lax.axis_size("seq")
    n_head = lax.axis_size("head")
    n_tp = lax.axis_size("tp")
    full_weight = lax.all_gather(kv_weight, "seq", axis=0, tiled=True)
    proj = jnp.dot(tokens, full_weight, preferred_element_type=jnp.float32)
    prompt_size = tok_rows * n_seq * n_head // 2
    source = lax.axis_index("seq") * n_head + lax.axis_index("head")
    token_ids = source * tok_rows + jnp.arange(tok_rows, dtype=jnp.int32)
    prompt_of = token_ids // prompt_size
    limit = jnp.where(prompt_of == 0, lengths[0], lengths[1])
    valid = token_ids % prompt_size < limit
    local_squares = jnp.sum(jnp.where(valid[:, None], proj * proj, 0.0), axis=0)
    side = lax.axis_index("tp")
    placed = jnp.where(jnp.arange(2, dtype=jnp.int32)[:, None] == side, local_squares[None, :], 0.0)
    squares = lax.psum(placed, ("seq", "tp", "head"))
    count = (lengths[0] + lengths[1]).astype(jnp.float32)
    scales = jnp.sqrt(squares / count + eps)
    own_scale = lax.dynamic_index_in_dim(scales, side, 0, keepdims=False)
    quant = jnp.clip(proj / own_scale[None, :], -clip_level, clip_level).astype(jnp.bfloat16)
    moved = lax.all_to_all(
        lax.all_to_all(quant[None], "head", split_axis=2, concat_axis=1, tiled=True),
        "tp",
        split_axis=1,
        concat_axis=0,
        tiled=True,
    )
    local_tokens = moved.shape[1]
    head_width = moved.shape[2]
    heads_dev = head_width // HD
    pages_here = local_tokens // PAGE
    blocks = moved.reshape(2, pages_here, PAGE, head_width)
    kv_cache = jnp.zeros_like(blocks).at[:, page_table].set(blocks)
    group_index = lax.axis_index("seq") * n_tp + lax.axis_index("tp")
    key_ids = group_index * local_tokens + jnp.arange(local_tokens, dtype=jnp.int32)
    key_prompt = key_ids // prompt_size
    key_place = key_ids % prompt_size
    total_rows = queries.shape[0] * queries.shape[1]
    group_size = queries.shape[2] // head_width
    row_pos = positions.reshape(total_rows)
    row_prompt = jnp.arange(total_rows, dtype=jnp.int32) % ROWS // (ROWS // 2)
    mask = (key_prompt[None, :] == row_prompt[:, None]) & (key_place[None, :] < row_pos[:, None])
    channel_start = lax.axis_index("head") * head_width
    head_scales = lax.dynamic_slice_in_dim(scales, channel_start, head_width, 1).reshape(
        2, heads_dev, HD
    )
    query_rows = queries.reshape(total_rows, heads_dev, group_size, HD)
    scaled = (query_rows.astype(jnp.float32) * head_scales[0][None, :, None, :]).astype(
        jnp.bfloat16
    )
    keys_here = moved[0].reshape(local_tokens, heads_dev, HD)
    values_here = moved[1].reshape(local_tokens, heads_dev, HD)
    inverse = 1.0 / jnp.sqrt(jnp.float32(HD))
    score = (
        jnp.einsum("rhgd,khd->hrgk", scaled, keys_here, preferred_element_type=jnp.float32)
        * inverse
    )
    wide_mask = mask[None, :, None, :]
    local_top = jnp.max(jnp.where(wide_mask, score, masked_fill), axis=-1)
    weight = jnp.where(wide_mask, jnp.exp(score - local_top[..., None]), 0.0)
    local_total = jnp.sum(weight, axis=-1)
    local_sum = jnp.einsum(
        "hrgk,khd->hrgd",
        weight.astype(jnp.bfloat16),
        values_here,
        preferred_element_type=jnp.float32,
    )
    top = lax.pmax(local_top, ("seq", "tp"))
    factor = jnp.exp(local_top - top)
    total, summed = lax.psum((local_total * factor, local_sum * factor[..., None]), ("seq", "tp"))
    own_keys = new_keys.reshape(total_rows, heads_dev, HD)
    own_values = new_values.reshape(total_rows, heads_dev, HD)
    own = (
        jnp.einsum("rhgd,rhd->hrg", query_rows, own_keys, preferred_element_type=jnp.float32)
        * inverse
    )
    overall = jnp.maximum(top, own)
    cached_factor = jnp.exp(top - overall)
    own_weight = jnp.exp(own - overall)
    denominator = total * cached_factor + own_weight
    value_part = summed * cached_factor[..., None] * head_scales[1][:, None, None, :]
    own_part = own_weight[..., None] * jnp.transpose(own_values, (1, 0, 2))[:, :, None, :].astype(
        jnp.float32
    )
    result = (value_part + own_part) / denominator[..., None]
    attended = jnp.transpose(result, (1, 0, 2, 3)).reshape(queries.shape).astype(jnp.bfloat16)
    return (kv_cache, scales, attended)


def solution(mesh):
    in_specs = (
        P(("seq", "head"), None),
        P("seq", "tp"),
        P(),
        P(("seq", "tp")),
        P(None, None, "head"),
        P(None, None, "head"),
        P(None, None, "head"),
        P(),
    )
    out_specs = (P(None, ("seq", "tp"), None, "head"), P(), P(None, None, "head"))
    return jax.shard_map(body, mesh=mesh, in_specs=in_specs, out_specs=out_specs, check_vma=False)
```

profile of v0, /device:TPU:6, one launch (start us, length us, event | category | flops | bytes accessed | tf_op | source)
XLA Modules:
  0.0 678.7 jit_solution(5218652826180324995)
XLA Ops:
  7.2 0.0 copy-start
  7.2 0.0 all-gather.2.cloned.1.call-start
  7.2 0.7 all-gather.2.cloned.1.call-update
  7.9 1.3 fusion.36
  10.6 1.3 fusion.23
  11.9 226.7 %all-gather.2.cloned.1.call-done = bf16[8192,1024]{1,0:T(8,128)(2,1)} async-done(((bf16[512,1024]{1,0:T(8,128)(2,1)}), bf16[8192,1024]{1,0:T(8,128)(2,1)}) %all-gather.2.cloned.1.call-update) | async-done | bytes 16777232 | tf_op jit(solution)/shard_map/all_gather | solution.py:21
  238.6 17.8 %select_reduce_fusion.1 = (f32[1024]{0:T(1024)S(1)}, f32[640,1024]{1,0:T(8,128)S(1)}) fusion(pred[640]{0:T(1024)(128)(4,1)S(1)} %fusion.23, bf16[640,8192]{1,0:T(8,128)(2,1)} %param.8, bf16[8192,1024]{1,0:T(8,128)(2,1)} %all-gather.2.cloned.1.call-done), kind=kOutput, calls=%fused_computation.8 | convolution fusion | flops 10739383296 | bytes 29889152 | tf_op jit(solution)/shard_map/dot_general | solution.py:22
  256.4 0.1 broadcast_select_fusion
  256.5 74.1 %psum.21 = f32[2,1024]{1,0:T(2,128)S(1)} all-reduce(f32[2,1024]{1,0:T(2,128)S(1)} %broadcast_select_fusion), channel_id=1, replica_groups=mesh['seq'=16,'tp'=2,'head'=8] {'seq','tp','head'}, use_global_device_ids=true, to_apply=%region_1.2 | all-reduce | flops 2048 | bytes 16384 | tf_op jit(solution)/shard_map/psum | solution.py:32
  330.6 0.0 copy-start.6
  330.6 1.4 fusion.5
  332.0 5.0 copy.25
  337.0 0.5 broadcast.237
  337.5 9.7 %reduce.4 = bf16[1024,640]{1,0:T(8,128)(2,1)} reduce(bf16[1024,1,640]{2,1,0:T(2,128)(2,1)S(1)} %bitcast.94, bf16[]{:T(256)} %broadcast.237), dimensions={1}, to_apply=%bitcast.80.reduce_sub_computation | reduce | bytes 2621442
  347.2 4.1 reshape.247
  351.3 5.4 all-to-all-start
  356.7 0.1 lt.61
  356.9 0.3 fusion.14
  357.2 0.3 compare_and_fusion
  357.6 15.9 %all-to-all-done = bf16[8,2,40960]{2,1,0:T(2,128)(2,1)} async-done(((bf16[8,2,40960]{2,1,0:T(2,128)(2,1)}), bf16[8,2,40960]{2,1,0:T(2,128)(2,1)}, u32[]{:S(2)}, u32[]{:S(2)}) %all-to-all-start) | async-done | bytes 1310752 | tf_op jit(solution)/shard_map/all_to_all | solution.py:38
  373.5 4.5 reshape.248
  378.0 1.3 copy.35
  379.3 2.4 copy.26
  381.7 4.1 copy.54
  385.8 28.9 %reduce.5 = bf16[5120,128]{1,0:T(8,128)(2,1)} reduce(bf16[5120,1,128]{2,1,0:T(2,128)(2,1)S(1)} %bitcast.95, bf16[]{:T(256)} %broadcast.237), dimensions={1}, to_apply=%bitcast.90.reduce_sub_computation | reduce | bytes 2621442
  414.7 2.3 reshape.249
  417.0 4.5 all-to-all-start.1
  421.5 0.3 all-reduce.2.cloned.1.call-start
  422.0 16.1 %all-to-all-done.1 = bf16[2,2,163840]{2,1,0:T(2,128)(2,1)} async-done(((bf16[2,2,163840]{2,1,0:T(2,128)(2,1)}), bf16[2,2,163840]{2,1,0:T(2,128)(2,1)}, u32[]{:S(2)}, u32[]{:S(2)}) %all-to-all-start.1) | async-done | bytes 1310752 | tf_op jit(solution)/shard_map/all_to_all | solution.py:37
  438.1 2.2 reshape.250
  440.3 3.5 fusion.35
  443.9 2.1 select_reduce_fusion
  446.0 2.6 fusion
  448.6 1.4 copy-done.2
  450.0 70.4 %pmax.7 = f32[1,128,8]{1,2,0:T(8,128)S(1)} all-reduce(f32[1,128,8]{1,2,0:T(8,128)S(1)} %bitcast.104), channel_id=1, replica_groups=mesh['seq'=16,'tp'=2,'head'=8] {'seq','tp'}, use_global_device_ids=true, to_apply=%region_4.5 | all-reduce | flops 1024 | bytes 8192 | tf_op jit(solution)/shard_map/pmax | solution.py:84
  520.4 0.0 copy-start.5
  520.4 7.1 %fusion.9 = f32[1,128,8,128]{3,1,2,0:T(8,128)} fusion(f32[128,8,2560]{2,0,1:T(8,128)} %copy-done.2, f32[128,8]{0,1:T(8,128)S(1)} %get-tuple-element.16, pred[128,2560]{1,0:T(8,128)(4,1)S(1)} %compare_and_fusion, bf16[1,2560,128]{2,0,1:T(2,128)(2,1)} %get-tuple-element.3, f32[128,8]{0,1:T(8,128)S(1)} %get-tuple-element.9), kind=kOutput, calls=%fused_computation.12 | convolution fusion | flops 681705472 | bytes 12001280 | tf_op jit(solution)/shard_map/hrgk,khd->hrgd/dot_general | solution.py:78
  527.5 0.0 all-reduce.2.cloned.1.call-update
  527.7 0.2 copy.36
  527.8 0.1 copy.28
  527.9 0.3 broadcast_in_dim.80
  528.2 1.5 scatter_fusion
  529.7 0.0 copy-start.3
  529.7 71.0 %psum.23 = f32[1,128,8]{1,2,0:T(8,128)S(1)} all-reduce(f32[1,128,8]{1,2,0:T(8,128)S(1)} %get-tuple-element.8), channel_id=1, replica_groups=mesh['seq'=16,'tp'=2,'head'=8] {'seq','tp'}, use_global_device_ids=true, to_apply=%region_7.8 | all-reduce | flops 1024 | bytes 8192 | tf_op jit(solution)/shard_map/psum | solution.py:86
  600.8 68.5 %all-reduce.2.cloned.1.call-done = f32[1,128,8,128]{3,1,2,0:T(8,128)} async-done(((f32[1,128,8,128]{3,1,2,0:T(8,128)}), f32[1,128,8,128]{3,1,2,0:T(8,128)}) %all-reduce.2.cloned.1.call-update) | async-done | bytes 524304 | tf_op jit(solution)/shard_map/psum | solution.py:86
  669.3 1.5 divide_convert_fusion
  670.8 0.2 copy.32
  671.0 0.8 convert_element_type.52
  (29 shorter events, 0.3 us)
Async XLA Ops:
  7.2 349.7 %copy-start = (bf16[2,64,128]{2,1,0:T(8,128)(2,1)S(1)}, bf16[2,64,128]{2,1,0:T(8,128)(2,1)}, u32[]{:S(2)}) copy-start(bf16[2,64,128]{2,1,0:T(8,128)(2,1)} %param.13) | copy-start | bytes 98308
  7.2 231.4 %all-gather.2.cloned.1.call-start = ((), (), s32[]{:S(2)}) async-start(), calls=%async_computation.2 | async-start | bytes 17825792 | tf_op jit(solution)/shard_map/all_gather | solution.py:21
  330.6 26.9 %copy-start.6 = (f32[2,1024]{1,0:T(2,128)}, f32[2,1024]{1,0:T(2,128)S(1)}, u32[]{:S(2)}) copy-start(f32[2,1024]{1,0:T(2,128)S(1)} %add_sqrt_fusion) | copy-start | bytes 24580
  347.2 9.5 %copy-start.7 = (s32[2,64]{1,0:T(2,128)S(1)}, s32[2,64]{1,0:T(2,128)}, u32[]{:S(2)}) copy-start(s32[2,64]{1,0:T(2,128)} %param.15) | copy-start | bytes 1540
  347.2 9.6 %copy-start.4 = (bf16[2,64,1024]{2,1,0:T(8,128)(2,1)S(1)}, bf16[2,64,1024]{2,1,0:T(8,128)(2,1)}, u32[]{:S(2)}) copy-start(bf16[2,64,1024]{2,1,0:T(8,128)(2,1)} %param.12) | copy-start | bytes 786436
  351.3 22.2 %all-to-all-start = ((bf16[8,2,40960]{2,1,0:T(2,128)(2,1)}), bf16[8,2,40960]{2,1,0:T(2,128)(2,1)}, u32[]{:S(2)}, u32[]{:S(2)}) async-start(bf16[8,2,40960]{2,1,0:T(2,128)(2,1)} %reshape.247), calls=%async_computation | async-start | bytes 2621440 | tf_op jit(solution)/shard_map/all_to_all | solution.py:38
  417.0 21.1 %all-to-all-start.1 = ((bf16[2,2,163840]{2,1,0:T(2,128)(2,1)}), bf16[2,2,163840]{2,1,0:T(2,128)(2,1)}, u32[]{:S(2)}, u32[]{:S(2)}) async-start(bf16[2,2,163840]{2,1,0:T(2,128)(2,1)} %reshape.249), calls=%async_computation.1 | async-start | bytes 2621440 | tf_op jit(solution)/shard_map/all_to_all | solution.py:37
  421.5 247.8 %all-reduce.2.cloned.1.call-start = ((), (), s32[]{:S(2)}) async-start(), calls=%async_computation.3 | async-start | bytes 1048576 | tf_op jit(solution)/shard_map/psum | solution.py:86
  446.0 4.0 copy-start.2
  520.4 7.2 %copy-start.8 = (s32[10]{0:T(128)S(1)}, s32[10]{0:T(128)}, u32[]{:S(2)}) copy-start(s32[10]{0:T(128)} %param.11) | copy-start | bytes 124
  520.4 7.2 %copy-start.5 = (bf16[2,64,128]{2,1,0:T(8,128)(2,1)S(1)}, bf16[2,64,128]{2,1,0:T(8,128)(2,1)}, u32[]{:S(2)}) copy-start(bf16[2,64,128]{2,1,0:T(8,128)(2,1)} %param.14) | copy-start | bytes 98308
  527.9 143.9 %copy-start.1 = (bf16[2,64,128]{2,1,0:T(8,128)(2,1)S(1)}, bf16[2,64,128]{2,1,0:T(8,128)(2,1)}, u32[]{:S(2)}) copy-start(bf16[2,64,128]{2,1,0:T(8,128)(2,1)} %param.13) | copy-start | bytes 98308
  529.7 142.1 %copy-start.3 = (bf16[2,10,256,128]{3,2,1,0:T(8,128)(2,1)}, bf16[2,10,256,128]{3,2,1,0:T(8,128)(2,1)S(1)}, u32[]{:S(2)}) copy-start(bf16[2,10,256,128]{3,2,1,0:T(8,128)(2,1)S(1)} %scatter_fusion) | copy-start | bytes 3932164
Sparse Core Ops, SparseCore 0:
  10.6 227.9 all-gather.1
  527.7 141.5 all-reduce.1
where the time goes:
time: 679 us
  waiting for transfers between devices  328 us (48%)
  blocking collectives  215 us (32%)
  other arithmetic  46 us (7%)
  local copies, waits for them, and re-layouts  35.9 us (5%)
  matrix products  27.3 us (4%)
  between operations  15.7 us (2%)
  starting transfers between devices  10.3 us (2%)
    all_gather x1, waiting for transfers between devices, body(): full_weight = lax.all_gather(kv_weight, 'seq', axis=0, tiled=True)  227 us
    psum x1, blocking collectives, body(): squares = lax.psum(placed, ('seq', 'tp', 'head'))  74.1 us
    psum x1, blocking collectives, body(): lax.psum((local_total * factor, local_sum * factor[..., None]), ('seq', '...  71 us
    pmax x1, blocking collectives, body(): top = lax.pmax(local_top, ('seq', 'tp'))  70.4 us
    psum x1, waiting for transfers between devices, body(): lax.psum((local_total * factor, local_sum * factor[..., None]), ('seq', '...  68.5 us
    unnamed x2, other arithmetic  38.6 us
    dot_general x1, matrix products, body(): proj = jnp.dot(tokens, full_weight, preferred_element_type=jnp.float32)  17.8 us
    unnamed x27, local copies, waits for them, and re-layouts  16.6 us
  transfers between devices with their start and end apart: 4, of which 4 were waited for; matrix products, arithmetic and copies ran while one was open for 1% of the time, Pallas kernels for 0%

commit v1 on v0

v1 whole, which is shorter than its diff:
```python
import functools
import math

import jax
import jax.numpy as jnp
from jax import lax
from jax.experimental import pallas as pl
from jax.experimental.pallas import tpu as pltpu
from jax.sharding import Mesh, PartitionSpec as P

HD = 128
PAGE = 256
PIECE = 256
TILE = 320
GROUP = 8
MIB = 1024 * 1024
VMEM = 60 * MIB
SHARED = 16 * MIB

eps = 1e-05
clip_level = 2.5
masked_fill = -1e30
inverse = 1.0 / (float(HD) ** 0.5)

SIZES = {"yh": 2, "z": 8, "tp": 2, "x": 4, "core": 2}
ANYWHERE = pl.BlockSpec(memory_space=pl.ANY)
WHOLE = pl.BlockSpec(memory_space=pltpu.VMEM)
SCALAR = pl.BlockSpec(memory_space=pltpu.SMEM)


def params(limit):
    return pltpu.CompilerParams(vmem_limit_bytes=limit)


def cost(flops=0, size=0, exps=0):
    return pl.CostEstimate(flops=flops, bytes_accessed=size, transcendentals=exps)


def send(value, **steps):
    names = tuple(steps)
    sizes = [SIZES[name] for name in names]
    pairs = []
    for i in range(math.prod(sizes)):
        target, rest = 0, i
        place = []
        for n in reversed(sizes):
            place.insert(0, rest % n)
            rest //= n
        for at, n, name in zip(place, sizes, names):
            target = target * n + (at + steps[name]) % n
        pairs.append((i, target))
    return lax.ppermute(value, names if len(names) > 1 else names[0], pairs)


def gate_kernel(*refs):
    pass


def gate(values, after):
    args = [pltpu.with_memory_space_constraint(v, pltpu.HBM) for v in values]
    return pl.pallas_call(
        gate_kernel,
        in_specs=[ANYWHERE] * (len(args) + 1),
        out_specs=[ANYWHERE] * len(args),
        out_shape=[jax.ShapeDtypeStruct(v.shape, v.dtype) for v in values],
        input_output_aliases={i: i for i in range(len(args))},
        compiler_params=params(SHARED),
        cost_estimate=cost(),
    )(*args, after)


def keep_kernel(source, target, sem):
    copy = pltpu.make_async_copy(source, target, sem)
    copy.start()
    copy.wait()


def keep(value):
    return pl.pallas_call(
        keep_kernel,
        in_specs=[ANYWHERE],
        out_specs=ANYWHERE,
        out_shape=pltpu.VMEM(value.shape, value.dtype),
        scratch_shapes=[pltpu.SemaphoreType.DMA],
        compiler_params=params(SHARED),
        cost_estimate=cost(size=2 * value.size * value.dtype.itemsize),
    )(value)


def take_kernel(weight, out, sems):
    core, half = lax.axis_index("core"), lax.axis_index("x") % 2
    copies = []
    for i in range(4):
        copies.append(
            pltpu.make_async_copy(
                weight.at[
                    pl.ds(pl.multiple_of(half * PIECE, PIECE), PIECE),
                    pl.ds(pl.multiple_of((2 * i + core) * HD, HD), HD),
                ],
                out.at[:, pl.ds(i * HD, HD)],
                sems.at[i],
            )
        )
    for copy in copies:
        copy.start()
    for copy in copies:
        copy.wait()


def take(weight):
    return pl.pallas_call(
        take_kernel,
        in_specs=[ANYWHERE],
        out_specs=ANYWHERE,
        out_shape=pltpu.HBM((PIECE, 4 * HD), weight.dtype),
        scratch_shapes=[pltpu.SemaphoreType.DMA((4,))],
        compiler_params=params(SHARED),
        cost_estimate=cost(size=MIB),
    )(weight)


def project_kernel(names, has_acc, last, own, sib, *refs):
    arrays = len(names)
    sources, refs = refs[:arrays], refs[arrays:]
    acc = lengths = None
    if has_acc:
        acc, refs = refs[0], refs[1:]
    if last:
        lengths, refs = refs[0], refs[1:]
    outs, (held, sems) = refs[:-2], refs[-2:]
    yh, z, x = lax.axis_index("yh"), lax.axis_index("z"), lax.axis_index("x")
    core = lax.axis_index("core")
    width = held.shape[1]
    copies, columns, sem = [], [], 0
    for i, pieces in enumerate(names):
        at = len(columns) * PIECE
        if pieces is None:
            pieces = [(0, 0, None), (0, 0, None)]
            some = [
                pltpu.make_async_copy(
                    sources[i].at[:, pl.ds(pl.multiple_of((2 * j + core) * HD, HD), HD)],
                    held.at[pl.ds(at, 2 * PIECE), pl.ds(j * HD, HD)],
                    sems.at[sem + j],
                )
                for j in range(4)
            ]
        else:
            some = [
                pltpu.make_async_copy(
                    sources[i], held.at[pl.ds(at, len(pieces) * PIECE)], sems.at[sem]
                )
            ]
        sem += len(some)
        for j, (other, dz, mine) in enumerate(pieces):
            half = j if mine is None else (x + (0 if mine else 1)) % 2
            shard = ((yh + other) % 2) * 8 + (z + dz + 8) % 8
            columns.append(pl.multiple_of((shard * 2 + half) * PIECE, PIECE))
            copies.append(some if j == 0 else [])
    for some in copies:
        for copy in some:
            copy.start()
    rows = own.shape[0]
    total = refs[-3] if last else outs[0]
    for piece, column in enumerate(columns):
        for copy in copies[piece]:
            copy.wait()
        weight = held[piece * PIECE : (piece + 1) * PIECE]
        for side, tokens in enumerate((own, sib)):
            for row in range(0, rows, TILE):
                value = jnp.dot(
                    tokens[pl.ds(row, TILE), pl.ds(column, PIECE)],
                    weight,
                    preferred_element_type=jnp.float32,
                )
                here = pl.ds(side * rows + row, TILE)
                if piece > 0:
                    total[here] += value
                elif has_acc:
                    total[here] = acc[here] + value
                else:
                    total[here] = value
    if not last:
        return
    squares = outs[1]
    part = jnp.zeros((1, width), jnp.float32)
    limit = jnp.where(yh == 0, lengths[0], lengths[1])
    for row in range(0, 2 * rows, TILE):
        value = total[row : row + TILE]
        goes = pl.multiple_of((row + core * rows) % (2 * rows), TILE)
        place = (z * 4 + x) * 2 * rows + goes + lax.broadcasted_iota(jnp.int32, value.shape, 0)
        kept = jnp.where(place < limit, value * value, 0.0)
        part = part + jnp.sum(kept, axis=0, keepdims=True)
        outs[0][pl.ds(goes, TILE)] = value
    squares[...] = jnp.broadcast_to(part[None], squares.shape)


def project(own, sib, pieces, acc=None, lengths=None):
    names = [ids for _, ids in pieces]
    n = sum(2 if ids is None else len(ids) for ids in names)
    rows, width = own.shape[0], 4 * HD
    last = lengths is not None
    in_specs = [WHOLE, WHOLE] + [ANYWHERE] * len(pieces)
    args = [pltpu.with_memory_space_constraint(value, pltpu.VMEM) for value in (own, sib)]
    args += [pltpu.with_memory_space_constraint(value, pltpu.HBM) for value, _ in pieces]
    aliases = {}
    if acc is not None:
        in_specs.append(WHOLE)
        if not last:
            aliases = {len(args): 0}
        args.append(acc)
    scratch = [
        pltpu.VMEM((n * PIECE, width), jnp.bfloat16),
        pltpu.SemaphoreType.DMA((len(pieces) + 3,)),
    ]
    if not last:
        out_shape = [pltpu.VMEM((2 * rows, width), jnp.float32)]
    else:
        in_specs.append(SCALAR)
        args.append(lengths)
        out_shape = [pltpu.VMEM((2 * rows, width), jnp.float32)]
        out_shape.append(jax.ShapeDtypeStruct((64, 1, width), jnp.float32))
        scratch.insert(0, pltpu.VMEM((2 * rows, width), jnp.float32))
    return pl.pallas_call(
        functools.partial(project_kernel, names, acc is not None, last),
        in_specs=in_specs,
        out_specs=[WHOLE] * len(out_shape),
        scratch_shapes=scratch,
        out_shape=out_shape,
        input_output_aliases=aliases,
        compiler_params=params(SHARED),
        cost_estimate=cost(4 * rows * PIECE * n * width, n * PIECE * width * 2),
    )(*args)


def quantize_kernel(proj, squares, lengths, *outs):
    x, tp = lax.axis_index("x"), lax.axis_index("tp")
    count = (lengths[0] + lengths[1]).astype(jnp.float32)
    scale = jnp.sqrt(jnp.sum(squares[:, 0, :], axis=0, keepdims=True) / count + eps)
    outs[4][...] = scale
    for k in range(4):
        head = pl.ds(pl.multiple_of(((x + k + 2 * tp) % 4) * HD, HD), HD)
        value = proj[:, head] * (1.0 / outs[4][:, head])
        outs[k][...] = jnp.clip(value, -clip_level, clip_level).astype(jnp.bfloat16)


def quantize(proj, squares, lengths):
    rows, width = proj.shape
    return pl.pallas_call(
        quantize_kernel,
        in_specs=[WHOLE, WHOLE, SCALAR],
        out_specs=[WHOLE] * 5,
        out_shape=[jax.ShapeDtypeStruct((rows, HD), jnp.bfloat16)] * 4
        + [jax.ShapeDtypeStruct((1, width), jnp.float32)],
        compiler_params=params(54 * MIB),
        cost_estimate=cost(4 * rows * width, 6 * rows * width),
    )(proj, squares, lengths)


def head_scale(own, other, side):
    here = pl.ds(pl.multiple_of(lax.axis_index("x") * HD, HD), HD)
    return jnp.where(lax.axis_index("tp") == side, own[:, here], other[:, here])


def attend_kernel(
    pages, r0, r1, r2, r3, query, limits, own_scale, other_scale, cache, part, held, tops, totals, sems
):
    yh, z, x, tp = [lax.axis_index(name) for name in ("yh", "z", "x", "tp")]
    got = (r0, r1, r2, r3)
    rows = r0.shape[0]
    scales = [head_scale(own_scale, other_scale, side) for side in range(2)]
    first = (x - 2 * tp + 4) % 4
    for m in range(4):

        @pl.when(first == m)
        def _(m=m):
            for j in range(4):
                held[j // 2, pl.ds((j % 2) * rows, rows)] = got[(m - j) % 4][...]

    count = 2 * rows // PAGE
    copies = []
    for j in range(2):
        for b in range(count):
            copies.append(
                pltpu.make_async_copy(
                    held.at[j, pl.ds(b * PAGE, PAGE)], cache.at[j, pages[b]], sems.at[j, b]
                )
            )
    for copy in copies:
        copy.start()
    keys, values = held[0], held[1]
    seen = pl.multiple_of(yh * 32, 32)
    limit = jnp.concatenate([limits[pl.ds(s * 64 + seen, 32)] for s in range(2)], axis=0)
    limit = jnp.concatenate([limit, limit], axis=0)
    base = (z * 2 + tp) * 2 * rows
    for pair in range(GROUP // 2):
        asked = [
            query[s, pl.ds(seen, 32), g * HD : (g + 1) * HD]
            for g in (2 * pair, 2 * pair + 1)
            for s in range(2)
        ]
        asked = jnp.concatenate(asked, axis=0)
        scaled = (asked.astype(jnp.float32) * scales[0]).astype(jnp.bfloat16)
        score = (
            lax.dot_general(
                scaled, keys, (((1,), (1,)), ((), ())), preferred_element_type=jnp.float32
            )
            * inverse
        )
        mask = base + lax.broadcasted_iota(jnp.int32, score.shape, 1) < limit
        top = jnp.max(jnp.where(mask, score, masked_fill), axis=1, keepdims=True)
        weight = jnp.where(mask, jnp.exp(score - top), 0.0)
        total = jnp.sum(weight, axis=1, keepdims=True)
        summed = jnp.dot(weight.astype(jnp.bfloat16), values, preferred_element_type=jnp.float32)
        for side in range(2):
            g = 2 * pair + side
            for block in range(8):
                source = slice(side * 64 + block * 8, side * 64 + block * 8 + 8)
                target = 2 * block + g // 4, slice((g % 4) * 8, (g % 4) * 8 + 8)
                part[target] = summed[source]
                tops[target], totals[target] = [
                    jnp.broadcast_to(value[source], (8, HD)) for value in (top, total)
                ]
    here = lax.broadcasted_iota(jnp.int32, (32, HD), 0) == lax.broadcasted_iota(
        jnp.int32, (32, HD), 1
    )
    for share in range(16):
        for at, column in enumerate((tops, totals)):
            part[share, 32 + at : 33 + at] = jnp.sum(
                jnp.where(here, column[share], 0.0), axis=0, keepdims=True
            )
    for copy in copies:
        copy.wait()


def attend(received, query, limits, own_scale, other_scale, page_table):
    rows = received[0].shape[0]
    pages = 2 * rows // PAGE
    heads = 512
    return pl.pallas_call(
        attend_kernel,
        in_specs=[SCALAR] + [WHOLE] * 8,
        out_specs=[ANYWHERE, WHOLE],
        scratch_shapes=[
            pltpu.VMEM((2, 2 * rows, HD), jnp.bfloat16),
            pltpu.VMEM((16, 32, HD), jnp.float32),
            pltpu.VMEM((16, 32, HD), jnp.float32),
            pltpu.SemaphoreType.DMA((2, pages)),
        ],
        out_shape=[
            jax.ShapeDtypeStruct((2, pages, PAGE, HD), jnp.bfloat16),
            jax.ShapeDtypeStruct((16, 40, HD), jnp.float32),
        ],
        compiler_params=params(VMEM),
        cost_estimate=cost(8 * heads * rows * HD, 16 * rows * HD, 2 * heads * rows),
    )(page_table, *received, query, limits, own_scale, other_scale)


def merge_kernel(parts, query, new_key, new_value, own_scale, other_scale, out, rows):
    yh, z, tp = [lax.axis_index(name) for name in ("yh", "z", "tp")]
    seen = pl.multiple_of(yh * 32, 32)
    step, at = z // 4, pl.multiple_of((z % 4) * 8, 8)
    half = 4 * HD
    rows[:, :half] = query[step, pl.ds(seen, 32), pl.ds(pl.multiple_of(tp * half, half), half)].astype(
        jnp.float32
    )
    rows[:, half : half + HD] = new_key[step, pl.ds(seen, 32)].astype(jnp.float32)
    rows[:, half + HD :] = new_value[step, pl.ds(seen, 32)].astype(jnp.float32)
    key = rows[pl.ds(at, 8), half : half + HD]
    value = rows[pl.ds(at, 8), half + HD :]
    scale = head_scale(own_scale, other_scale, 1)
    own = [
        jnp.sum(rows[pl.ds(at, 8), g * HD : (g + 1) * HD] * key, axis=1, keepdims=True) * inverse
        for g in range(4)
    ]
    own = jnp.concatenate(own, axis=0)
    value = jnp.concatenate([value] * 4, axis=0)
    here = lax.broadcasted_iota(jnp.int32, (1, 32, HD), 1) == lax.broadcasted_iota(
        jnp.int32, (1, 32, HD), 2
    )
    top, total = [
        jnp.sum(jnp.where(here, parts[:, at : at + 1, :], 0.0), axis=2, keepdims=True)
        for at in (32, 33)
    ]
    overall = jnp.maximum(jnp.max(top, axis=0), own)
    factor = jnp.exp(top - overall[None])
    own_weight = jnp.exp(own - overall)
    denominator = jnp.sum(total * factor, axis=0) + own_weight
    summed = jnp.sum(parts[:, :32, :] * factor, axis=0)
    result = (summed * scale + own_weight * value) / denominator
    out[...] = jnp.broadcast_to(result.astype(out.dtype)[None], out.shape)


def merge(parts, query, new_key, new_value, own_scale, other_scale):
    return pl.pallas_call(
        merge_kernel,
        in_specs=[WHOLE] * 6,
        out_specs=WHOLE,
        out_shape=jax.ShapeDtypeStruct((32, 32, HD), jnp.bfloat16),
        scratch_shapes=[pltpu.VMEM((32, 6 * HD), jnp.float32)],
        compiler_params=params(VMEM),
        cost_estimate=cost(1 << 18, 1 << 19, 512),
    )(parts, query, new_key, new_value, own_scale, other_scale)


def finish_kernel(whole, both, far, attended, scales):
    for yh in range(2):
        for step in range(2):
            for side in range(2):
                blocks = [
                    whole[yh * 16 + 2 * (step * 4 + part) + side].astype(jnp.float32)
                    for part in range(4)
                ]
                for g in range(4):
                    value = jnp.concatenate([b[g * 8 : g * 8 + 8] for b in blocks], axis=0)
                    head = side * 4 + g
                    attended[step, yh * 32 : yh * 32 + 32, head * HD : (head + 1) * HD] = (
                        value.astype(attended.dtype)
                    )
    tp, core = lax.axis_index("tp"), lax.axis_index("core")
    for side in range(2):
        for i in range(4):
            lanes = slice(i * HD, (i + 1) * HD)
            for c in range(2):
                own = jnp.where(core == c, both[0:1, lanes], far[0:1, lanes])
                other = jnp.where(core == c, both[1:2, lanes], far[1:2, lanes])
                scales[side : side + 1, (2 * i + c) * HD : (2 * i + c + 1) * HD] = jnp.where(
                    tp == side, own, other
                )


def finish(whole, both, far):
    return pl.pallas_call(
        finish_kernel,
        in_specs=[WHOLE] * 3,
        out_specs=[WHOLE] * 2,
        out_shape=[
            jax.ShapeDtypeStruct((2, 64, GROUP * HD), jnp.bfloat16),
            jax.ShapeDtypeStruct((2, 8 * HD), jnp.float32),
        ],
        compiler_params=params(VMEM),
        cost_estimate=cost(0, MIB // 2),
    )(whole, both, far)


def body(tokens, kv_weight, lengths, page_table, queries, new_keys, new_values, positions):
    sibling = send(tokens, core=1)
    own = keep(pltpu.with_memory_space_constraint(tokens, pltpu.HBM))

    def joined(*values):
        return jnp.concatenate(values, axis=0)

    def swapped(ids):
        return [(other, dz, False) for other, dz, _ in ids]

    first = take(kv_weight)
    cross = send(first, yh=1)
    up, down = send(first, z=1), send(first, z=-1)
    up_far, down_far = send(first, yh=1, z=1), send(first, yh=1, z=-1)
    cross, up, up_far, down, down_far = gate([cross, up, up_far, down, down_far], own)
    up, down = joined(up, up_far), joined(down, down_far)
    at = lambda dz: [(0, dz, True), (1, dz, True)]

    sides = send(cross, x=1), send(up, x=-1), send(down, x=1)
    next_up, next_down = send(up, z=1), send(down, z=-1)
    sib = keep(sibling)
    next_up, next_down, *sides = gate([next_up, next_down, *sides], sib)
    wave = [(kv_weight, None), (cross, [(1, 0, True)]), (up, at(-1)), (down, at(1))]
    wave += [(sides[0], [(1, 0, False)]), (sides[1], swapped(at(-1))), (sides[2], swapped(at(1)))]
    wave += [(next_up, at(-2)), (next_down, at(2))]
    up, down = next_up, next_down

    acc = project(own, sib, wave)[0]
    sides = send(up, x=-1), send(down, x=1)
    next_up, next_down = send(up, z=1), send(down, z=-1)
    next_up, next_down, *sides = gate([next_up, next_down, *sides], acc)
    wave = [(next_up, at(-3)), (next_down, at(3))]
    wave += [(sides[0], swapped(at(-2))), (sides[1], swapped(at(2)))]
    up, down = next_up, next_down

    near, far = up[:PIECE], down[PIECE:]
    wave_last = [(send(near, z=1), at(-4)[:1]), (send(far, z=-1), at(4)[1:])]
    wave_last += [(send(up, x=-1), swapped(at(-3))), (send(down, x=1), swapped(at(3)))]
    wave_last += [(send(near, z=1, x=-1), swapped(at(-4)[:1]))]
    wave_last += [(send(far, z=-1, x=1), swapped(at(4)[1:]))]
    acc = project(own, sib, wave, acc)[0]
    proj, squares = project(own, sib, wave_last, acc, lengths)
    squares = lax.all_to_all(squares, ("yh", "z", "x"), 0, 0, tiled=True)
    *sent, scale = quantize(proj, squares, lengths)

    received = []
    for k in range(4):
        pairs = []
        for t in range(2):
            for a in range(4):
                pairs.append((t * 4 + a, (a // 2) * 4 + (a + k + 2 * t) % 4))
        received.append(lax.ppermute(sent[k], ("tp", "x"), pairs))

    other_scale = send(scale, tp=1)
    both = joined(scale, other_scale)
    far = send(both, core=1)

    kv_cache, part = attend(
        received, queries, positions.reshape(128, 1), scale, other_scale, page_table
    )
    parts = lax.all_to_all(part, ("z", "tp"), 0, 0, tiled=True)
    result = merge(parts, queries, new_keys, new_values, scale, other_scale)
    whole = lax.all_to_all(result, ("yh", "z", "tp"), 0, 0, tiled=True)
    attended, scales = finish(whole, both, far)
    return (kv_cache, scales, attended)


def solution(mesh):
    names = tuple(SIZES)
    fine = Mesh(mesh.devices.reshape(tuple(SIZES.values())), names)
    seq, head = ("yh", "z"), ("x", "core")
    in_specs = (
        P(seq + head, None),
        P(seq, "tp"),
        P(),
        P(seq + ("tp",)),
        P(None, None, head),
        P(None, None, head),
        P(None, None, head),
        P(),
    )
    out_specs = (P(None, seq + ("tp",), None, head), P(), P(None, None, head))
    return jax.shard_map(body, mesh=fine, in_specs=in_specs, out_specs=out_specs, check_vma=False)
```

time: 679 us -> 192 us (0.28)
  waiting for transfers between devices: 328 us -> 44.4 us
  blocking collectives: 215 us -> 39 us
  other arithmetic: 46 us -> 0.7 us
  starting transfers between devices: 10.3 us -> 53.6 us
  Pallas kernels: 0 us -> 36.2 us
  matrix products: 27.3 us -> 0 us
  local copies, waits for them, and re-layouts: 35.9 us -> 16.7 us
  between operations: 15.7 us -> 1.07 us
    all_gather x1 -> x0, waiting for transfers between devices: 227 us -> none  [body(): full_weight = lax.all_gather(kv_weight, 'seq', axis=0, tiled=True)]
    psum x2 -> x0, blocking collectives: 145 us -> none  [the longest x1 74.1 us: body(): squares = lax.psum(placed, ('seq', 'tp', 'head'))]
    pmax x1 -> x0, blocking collectives: 70.4 us -> none  [body(): top = lax.pmax(local_top, ('seq', 'tp'))]
    psum x1 -> x0, waiting for transfers between devices: 68.5 us -> none  [body(): lax.psum((local_total * factor, local_sum * factor[..., None]), ('seq', '...]
    ppermute x0 -> x27, starting transfers between devices: none -> 49.8 us  [the longest x23 41.4 us: send(): return lax.ppermute(value, names if len(names) > 1 else names[0], pairs)]
    all_to_all x0 -> x2, blocking collectives: none -> 39 us  [the longest x1 23.4 us: body(): squares = lax.all_to_all(squares, ('yh', 'z', 'x'), 0, 0, tiled=True)]
    unnamed x2 -> x0, other arithmetic: 38.6 us -> none
    pallas_call x0 -> x13, Pallas kernels: none -> 36.2 us  [the longest x3 18 us: project(): pl.pallas_call(functools.partial(project_kernel, names, acc is not None,...]
  transfers between devices with their start and end apart: 4 -> 28, of which waited for: 4 -> 13; matrix products, arithmetic and copies ran while one was open for 1% -> 3% of each run, Pallas kernels for 0% -> 9%
where the time goes in v1:
time: 192 us
  starting transfers between devices  53.6 us (28%)
  waiting for transfers between devices  44.4 us (23%)
  blocking collectives  39 us (20%)
  Pallas kernels  36.2 us (19%)
  local copies, waits for them, and re-layouts  16.7 us (9%)
    ppermute x23, starting transfers between devices, send(): return lax.ppermute(value, names if len(names) > 1 else names[0], pairs)  41.4 us
    ppermute x23, waiting for transfers between devices, send(): return lax.ppermute(value, names if len(names) > 1 else names[0], pairs)  26.4 us
    all_to_all x1, blocking collectives, body(): squares = lax.all_to_all(squares, ('yh', 'z', 'x'), 0, 0, tiled=True)  23.4 us
    pallas_call x3, Pallas kernels, project(): pl.pallas_call(functools.partial(project_kernel, names, acc is not None,...  18 us
    all_to_all x1, blocking collectives, body(): parts = lax.all_to_all(part, ('z', 'tp'), 0, 0, tiled=True)  15.5 us
    unnamed x70, local copies, waits for them, and re-layouts  12 us
    all_to_all x1, waiting for transfers between devices, body(): whole = lax.all_to_all(result, ('yh', 'z', 'tp'), 0, 0, tiled=True)  10.5 us
    ppermute x4, starting transfers between devices, body(): received.append(lax.ppermute(sent[k], ('tp', 'x'), pairs))  8.4 us
  transfers between devices with their start and end apart: 28, of which 13 were waited for; matrix products, arithmetic and copies ran while one was open for 3% of the time, Pallas kernels for 9%

profile of v1, /device:TPU:6, one launch (start us, length us, event | category | flops | bytes accessed | tf_op | source)
XLA Modules:
  0.0 191.7 jit_solution(5384139409646691743)
XLA Ops:
  0.7 1.2 copy-done
  2.7 3.3 %collective-permute-start.1 = (bf16[256,512]{1,0:T(8,128)(2,1)}, bf16[256,512]{1,0:T(8,128)(2,1)S(1)}, u32[]{:S(2)}, u32[]{:S(2)}) collective-permute-start(bf16[256,512]{1,0:T(8,128)(2,1)} %shard_map.105), channel_id=1, source_target_pairs={{0,128},{128,0},{1,129},{129,1},{2,130},{130,2},{3,131},{131,3},{4... | collective-permute-start | bytes 786440 | tf_op jit(solution)/shard_map/ppermute | solution.py:52
  6.0 1.9 %collective-permute-start.2 = (bf16[256,512]{1,0:T(8,128)(2,1)}, bf16[256,512]{1,0:T(8,128)(2,1)S(1)}, u32[]{:S(2)}, u32[]{:S(2)}) collective-permute-start(bf16[256,512]{1,0:T(8,128)(2,1)} %shard_map.105), channel_id=1, source_target_pairs={{0,16},{16,32},{32,48},{48,64},{64,80},{80,96},{96,112},{112,0},{1... | collective-permute-start | bytes 786440 | tf_op jit(solution)/shard_map/ppermute | solution.py:52
  7.9 1.7 collective-permute-start.3
  9.6 2.3 %collective-permute-start.4 = (bf16[256,512]{1,0:T(8,128)(2,1)}, bf16[256,512]{1,0:T(8,128)(2,1)S(1)}, u32[]{:S(2)}, u32[]{:S(2)}) collective-permute-start(bf16[256,512]{1,0:T(8,128)(2,1)} %shard_map.105), channel_id=1, source_target_pairs={{0,112},{16,0},{32,16},{48,32},{64,48},{80,64},{96,80},{112,96},{1... | collective-permute-start | bytes 786440 | tf_op jit(solution)/shard_map/ppermute | solution.py:52
  11.8 1.4 collective-permute-done.1.refs_0_
  13.2 8.5 %collective-permute-start.5 = (bf16[256,512]{1,0:T(8,128)(2,1)}, bf16[256,512]{1,0:T(8,128)(2,1)S(1)}, u32[]{:S(2)}, u32[]{:S(2)}) collective-permute-start(bf16[256,512]{1,0:T(8,128)(2,1)} %shard_map.105), channel_id=1, source_target_pairs={{0,240},{16,128},{32,144},{48,160},{64,176},{80,192},{96,208},{112... | collective-permute-start | bytes 786440 | tf_op jit(solution)/shard_map/ppermute | solution.py:52
  21.7 4.0 %shard_map.103.refs_5_.own = bf16[640,8192]{1,0:T(8,128)(2,1)S(1)} custom-call(bf16[640,8192]{1,0:T(8,128)(2,1)} %source.1), custom_call_target="tpu_custom_call" | custom-call | bytes 20971520 | tf_op jit(solution)/shard_map/pallas_call | solution.py:79
  25.7 1.4 collective-permute-done.3.refs_2_
  27.1 2.7 %collective-permute-done.5.refs_4_ = bf16[256,512]{1,0:T(8,128)(2,1)S(1)} collective-permute-done((bf16[256,512]{1,0:T(8,128)(2,1)}, bf16[256,512]{1,0:T(8,128)(2,1)S(1)}, u32[]{:S(2)}, u32[]{:S(2)}) %collective-permute-start.5) | collective-permute-done | bytes 262176 | tf_op jit(solution)/shard_map/ppermute | solution.py:52
  30.5 1.0 constant_dynamic-update-slice_fusion.1
  31.5 1.0 constant_dynamic-update-slice_fusion.refs_2_
  32.6 1.1 constant_dynamic-update-slice_fusion.3
  33.6 1.0 constant_dynamic-update-slice_fusion.2.refs_3_
  34.6 3.2 %collective-permute-start.7 = (bf16[512,512]{1,0:T(8,128)(2,1)S(1)}, bf16[512,512]{1,0:T(8,128)(2,1)S(1)}, u32[]{:S(2)}, u32[]{:S(2)}) collective-permute-start(bf16[512,512]{1,0:T(8,128)(2,1)S(1)} %constant_dynamic-update-slice_fusion.2.refs_3_), channel_id=1, source_target_pairs={{0,112},{16,0},{32,16},{48,32},{64,48},{80,64},{96,80},{112,96},{1... | collective-permute-start | bytes 1572872 | tf_op jit(solution)/shard_map/ppermute | solution.py:52
  37.8 0.8 collective-permute-start.9
  38.6 2.4 %collective-permute-start.10 = (bf16[512,512]{1,0:T(8,128)(2,1)S(1)}, bf16[512,512]{1,0:T(8,128)(2,1)S(1)}, u32[]{:S(2)}, u32[]{:S(2)}) collective-permute-start(bf16[512,512]{1,0:T(8,128)(2,1)S(1)} %constant_dynamic-update-slice_fusion.2.refs_3_), channel_id=1, source_target_pairs={{0,2},{2,4},{4,6},{6,0},{1,3},{3,5},{5,7},{7,1},{8,10},{10,12},{12... | collective-permute-start | bytes 1572872 | tf_op jit(solution)/shard_map/ppermute | solution.py:52
  41.8 14.4 %collective-permute-done.8.refs_2_ = bf16[256,512]{1,0:T(8,128)(2,1)S(1)} collective-permute-done((bf16[256,512]{1,0:T(8,128)(2,1)}, bf16[256,512]{1,0:T(8,128)(2,1)S(1)}, u32[]{:S(2)}, u32[]{:S(2)}) %collective-permute-start.8) | collective-permute-done | bytes 262176 | tf_op jit(solution)/shard_map/ppermute | solution.py:52
  58.2 3.2 %collective-permute-start.12 = (bf16[512,512]{1,0:T(8,128)(2,1)}, bf16[512,512]{1,0:T(8,128)(2,1)S(1)}, u32[]{:S(2)}, u32[]{:S(2)}) collective-permute-start(bf16[512,512]{1,0:T(8,128)(2,1)} %get-tuple-element.34.refs_8_), channel_id=1, source_target_pairs={{0,112},{16,0},{32,16},{48,32},{64,48},{80,64},{96,80},{112,96},{1... | collective-permute-start | bytes 1572872 | tf_op jit(solution)/shard_map/ppermute | solution.py:52
  62.0 3.1 %collective-permute-start.14 = (bf16[512,512]{1,0:T(8,128)(2,1)}, bf16[512,512]{1,0:T(8,128)(2,1)S(1)}, u32[]{:S(2)}, u32[]{:S(2)}) collective-permute-start(bf16[512,512]{1,0:T(8,128)(2,1)} %get-tuple-element.34.refs_8_), channel_id=1, source_target_pairs={{0,2},{2,4},{4,6},{6,0},{1,3},{3,5},{5,7},{7,1},{8,10},{10,12},{12... | collective-permute-start | bytes 1572872 | tf_op jit(solution)/shard_map/ppermute | solution.py:52
  65.1 7.8 %shard_map.108.refs_4_ = f32[1280,512]{1,0:T(8,128)S(1)} custom-call(bf16[640,8192]{1,0:T(8,128)(2,1)S(1)} %shard_map.103.refs_5_.own, bf16[640,8192]{1,0:T(8,128)(2,1)S(1)} %shard_map.104.refs_5_.sib, bf16[512,1024]{1,0:T(8,128)(2,1)} %refs_0_.1, bf16[256,512]{1,0:T(8,128)(2,1)} %get-tuple-element.32.refs_1_, bf16[512,512]{1,0:T(8,128)(2,1)} %copy-done.11, ...), custom_call_target="tpu_custom_call" | custom-call | flops 5368709120 | bytes 4194304 | tf_op jit(solution)/shard_map/pallas_call | solution.py:223
  72.9 1.1 collective-permute-done.13.refs_2_
  75.6 1.0 slice.6
  77.1 2.9 %collective-permute-start.18 = (bf16[512,512]{1,0:T(8,128)(2,1)}, bf16[512,512]{1,0:T(8,128)(2,1)S(1)}, u32[]{:S(2)}, u32[]{:S(2)}) collective-permute-start(bf16[512,512]{1,0:T(8,128)(2,1)} %get-tuple-element.39.refs_1_), channel_id=1, source_target_pairs={{0,2},{2,4},{4,6},{6,0},{1,3},{3,5},{5,7},{7,1},{8,10},{10,12},{12... | collective-permute-start | bytes 1572872 | tf_op jit(solution)/shard_map/ppermute | solution.py:52
  79.9 1.0 slice.7
  81.0 3.2 %collective-permute-start.16 = (bf16[256,512]{1,0:T(8,128)(2,1)S(1)}, bf16[256,512]{1,0:T(8,128)(2,1)S(1)}, u32[]{:S(2)}, u32[]{:S(2)}) collective-permute-start(bf16[256,512]{1,0:T(8,128)(2,1)S(1)} %slice.7), channel_id=1, source_target_pairs={{0,112},{16,0},{32,16},{48,32},{64,48},{80,64},{96,80},{112,96},{1... | collective-permute-start | bytes 786440 | tf_op jit(solution)/shard_map/ppermute | solution.py:52
  84.3 1.5 collective-permute-done.15.refs_0_
  85.8 2.5 %collective-permute-start.20 = (bf16[256,512]{1,0:T(8,128)(2,1)S(1)}, bf16[256,512]{1,0:T(8,128)(2,1)S(1)}, u32[]{:S(2)}, u32[]{:S(2)}) collective-permute-start(bf16[256,512]{1,0:T(8,128)(2,1)S(1)} %slice.7), channel_id=1, source_target_pairs={{0,114},{2,116},{4,118},{6,112},{16,2},{18,4},{20,6},{22,0},{32,18... | collective-permute-start | bytes 786440 | tf_op jit(solution)/shard_map/ppermute | solution.py:52
  88.3 4.7 %shard_map.110.refs_6_ = f32[1280,512]{1,0:T(8,128)S(1)} custom-call(bf16[640,8192]{1,0:T(8,128)(2,1)S(1)} %shard_map.103.refs_5_.own, bf16[640,8192]{1,0:T(8,128)(2,1)S(1)} %shard_map.104.refs_5_.sib, bf16[512,512]{1,0:T(8,128)(2,1)} %get-tuple-element.38.refs_0_, bf16[512,512]{1,0:T(8,128)(2,1)} %get-tuple-element.39.refs_1_, ...), custom_call_target="tpu_custom_call", output_to_operand_aliasing={{}: (6, {})} | custom-call | flops 2684354560 | bytes 2097152 | tf_op jit(solution)/shard_map/pallas_call | solution.py:223
  95.1 5.6 %shard_map.111 = (f32[1280,512]{1,0:T(8,128)S(1)}, f32[64,1,512]{2,1,0:T(1,128)S(1)}) custom-call(bf16[640,8192]{1,0:T(8,128)(2,1)S(1)} %shard_map.103.refs_5_.own, bf16[640,8192]{1,0:T(8,128)(2,1)S(1)} %shard_map.104.refs_5_.sib, bf16[256,512]{1,0:T(8,128)(2,1)} %copy-done.22, bf16[256,512]{1,0:T(8,128)(2,1)} %copy-done.24, bf16[512,512]{1,0:T(8,128)(2,1)} %copy-done.20, ...), custom_call_target="tpu_custom_call" | custom-call | flops 2684354560 | bytes 2097152 | tf_op jit(solution)/shard_map/pallas_call | solution.py:223
  100.7 1.5 copy-done.1
  102.2 23.4 %all_to_all.15.squares = f32[64,1,512]{2,1,0:T(1,128)} all-to-all(f32[64,1,512]{2,1,0:T(1,128)S(1)} %get-tuple-element.43), channel_id=1, replica_groups=mesh['yh'=2,'z'=8,'tp'=2,'x'=4,'core'=2] {'yh','z','x'}, dimensions={0} | all-to-all | bytes 262144 | tf_op jit(solution)/shard_map/all_to_all | solution.py:487
  125.6 3.0 %shard_map.112 = (bf16[1280,128]{1,0:T(8,128)(2,1)}, bf16[1280,128]{1,0:T(8,128)(2,1)}, bf16[1280,128]{1,0:T(8,128)(2,1)}, bf16[1280,128]{1,0:T(8,128)(2,1)}, f32[1,512]{1,0:T(1,128)}) custom-call(f32[1280,512]{1,0:T(8,128)} %copy-done.1, f32[64,1,512]{2,1,0:T(1,128)} %all_to_all.15.squares, s32[2]{0:T(128)} %lengths.1), custom_call_target="tpu_custom_call" | custom-call | flops 2621440 | bytes 3932160 | tf_op jit(solution)/shard_map/pallas_call | solution.py:248
  128.6 2.6 %collective-permute-start.21 = (bf16[1280,128]{1,0:T(8,128)(2,1)}, bf16[1280,128]{1,0:T(8,128)(2,1)S(1)}, u32[]{:S(2)}, u32[]{:S(2)}) collective-permute-start(bf16[1280,128]{1,0:T(8,128)(2,1)} %get-tuple-element.44), channel_id=1, source_target_pairs={{0,0},{2,2},{4,12},{6,14},{8,4},{10,6},{12,8},{14,10},{1,1},{3,3},... | collective-permute-start | bytes 983048 | tf_op jit(solution)/shard_map/ppermute | solution.py:496
  131.2 3.2 %collective-permute-start.22 = (bf16[1280,128]{1,0:T(8,128)(2,1)}, bf16[1280,128]{1,0:T(8,128)(2,1)S(1)}, u32[]{:S(2)}, u32[]{:S(2)}) collective-permute-start(bf16[1280,128]{1,0:T(8,128)(2,1)} %get-tuple-element.45), channel_id=1, source_target_pairs={{0,2},{2,4},{4,14},{6,8},{8,6},{10,0},{12,10},{14,12},{1,3},{3,5},... | collective-permute-start | bytes 983048 | tf_op jit(solution)/shard_map/ppermute | solution.py:496
  134.4 2.5 %collective-permute-start.23 = (bf16[1280,128]{1,0:T(8,128)(2,1)}, bf16[1280,128]{1,0:T(8,128)(2,1)S(1)}, u32[]{:S(2)}, u32[]{:S(2)}) collective-permute-start(bf16[1280,128]{1,0:T(8,128)(2,1)} %get-tuple-element.46), channel_id=1, source_target_pairs={{0,4},{2,6},{4,8},{6,10},{8,0},{10,2},{12,12},{14,14},{1,5},{3,7},... | collective-permute-start | bytes 983048 | tf_op jit(solution)/shard_map/ppermute | solution.py:496
  137.0 0.9 collective-permute-start.25
  138.7 2.4 %collective-permute-done.25.other_scale = f32[1,512]{1,0:T(1,128)S(1)} collective-permute-done((f32[1,512]{1,0:T(1,128)}, f32[1,512]{1,0:T(1,128)S(1)}, u32[]{:S(2)}, u32[]{:S(2)}) %collective-permute-start.25) | collective-permute-done | bytes 2080 | tf_op jit(solution)/shard_map/ppermute | solution.py:52
  141.1 2.6 %collective-permute-done.22.r1 = bf16[1280,128]{1,0:T(8,128)(2,1)S(1)} collective-permute-done((bf16[1280,128]{1,0:T(8,128)(2,1)}, bf16[1280,128]{1,0:T(8,128)(2,1)S(1)}, u32[]{:S(2)}, u32[]{:S(2)}) %collective-permute-start.22) | collective-permute-done | bytes 327712 | tf_op jit(solution)/shard_map/ppermute | solution.py:496
  143.7 1.5 collective-permute-done.23.r2
  145.2 3.4 %collective-permute-done.24.r3 = bf16[1280,128]{1,0:T(8,128)(2,1)S(1)} collective-permute-done((bf16[1280,128]{1,0:T(8,128)(2,1)}, bf16[1280,128]{1,0:T(8,128)(2,1)S(1)}, u32[]{:S(2)}, u32[]{:S(2)}) %collective-permute-start.24) | collective-permute-done | bytes 327712 | tf_op jit(solution)/shard_map/ppermute | solution.py:496
  149.3 5.9 %shard_map.113 = (bf16[2,10,256,128]{3,2,1,0:T(8,128)(2,1)}, f32[16,40,128]{2,1,0:T(8,128)}) custom-call(s32[10]{0:T(128)} %pages.1, bf16[1280,128]{1,0:T(8,128)(2,1)} %copy-done.30, bf16[1280,128]{1,0:T(8,128)(2,1)} %copy-done.31, bf16[1280,128]{1,0:T(8,128)(2,1)} %copy-done.32, bf16[1280,128]{1,0:T(8,128)(2,1)} %copy-done.33, bf16[2,64,1024]{2,1,0:T(8,128)(2,1)} %query.3, ...), custom_call_target="tpu_custom_call" | custom-call | flops 671088640 | bytes 2621440 | tf_op jit(solution)/shard_map/pallas_call | solution.py:339
  155.3 15.5 %all_to_all.16.parts = f32[16,40,128]{2,1,0:T(8,128)} all-to-all(f32[16,40,128]{2,1,0:T(8,128)} %get-tuple-element.50), channel_id=1, replica_groups=mesh['yh'=2,'z'=8,'tp'=2,'x'=4,'core'=2] {'z','tp'}, dimensions={0} | all-to-all | bytes 655360 | tf_op jit(solution)/shard_map/all_to_all | solution.py:505
  170.8 2.1 %shard_map.114 = bf16[32,32,128]{2,1,0:T(8,128)(2,1)} custom-call(f32[16,40,128]{2,1,0:T(8,128)} %all_to_all.16.parts, bf16[2,64,1024]{2,1,0:T(8,128)(2,1)} %query.3, bf16[2,64,128]{2,1,0:T(8,128)(2,1)} %new_key.1, bf16[2,64,128]{2,1,0:T(8,128)(2,1)} %new_value.1, f32[1,512]{1,0:T(1,128)} %get-tuple-element.48.own_scale, f32[1,512]{1,0:T(1,128)} %copy-done.27), custom_call_target="tpu_custom_call" | custom-call | flops 262144 | bytes 524288 | tf_op jit(solution)/shard_map/pallas_call | solution.py:394
  172.9 3.9 %all-to-all-start.2 = ((bf16[32,32,128]{2,1,0:T(8,128)(2,1)}), bf16[32,32,128]{2,1,0:T(8,128)(2,1)S(1)}, u32[]{:S(2)}, u32[]{:S(2)}) async-start(bf16[32,32,128]{2,1,0:T(8,128)(2,1)} %shard_map.114), calls=%async_computation.2 | async-start | bytes 524288 | tf_op jit(solution)/shard_map/all_to_all | solution.py:507
  177.6 1.2 collective-permute-done.26.far
  178.8 10.5 %all-to-all-done.2.whole = bf16[32,32,128]{2,1,0:T(8,128)(2,1)S(1)} async-done(((bf16[32,32,128]{2,1,0:T(8,128)(2,1)}), bf16[32,32,128]{2,1,0:T(8,128)(2,1)S(1)}, u32[]{:S(2)}, u32[]{:S(2)}) %all-to-all-start.2) | async-done | bytes 262176 | tf_op jit(solution)/shard_map/all_to_all | solution.py:507
  189.9 1.7 shard_map.115
  (99 shorter events, 12.2 us)
Async XLA Ops:
  0.6 40.4 %collective-permute-start = (bf16[640,8192]{1,0:T(8,128)(2,1)}, bf16[640,8192]{1,0:T(8,128)(2,1)S(1)}, u32[]{:S(2)}, u32[]{:S(2)}) collective-permute-start(bf16[640,8192]{1,0:T(8,128)(2,1)} %source.1), channel_id=1, source_target_pairs={{0,1},{1,0},{2,3},{3,2},{4,5},{5,4},{6,7},{7,6},{8,9},{9,8},{10,11... | collective-permute-start | bytes 31457288 | tf_op jit(solution)/shard_map/ppermute | solution.py:52
  0.7 1.2 copy-start
  2.7 10.5 %collective-permute-start.1 = (bf16[256,512]{1,0:T(8,128)(2,1)}, bf16[256,512]{1,0:T(8,128)(2,1)S(1)}, u32[]{:S(2)}, u32[]{:S(2)}) collective-permute-start(bf16[256,512]{1,0:T(8,128)(2,1)} %shard_map.105), channel_id=1, source_target_pairs={{0,128},{128,0},{1,129},{129,1},{2,130},{130,2},{3,131},{131,3},{4... | collective-permute-start | bytes 786440 | tf_op jit(solution)/shard_map/ppermute | solution.py:52
  6.0 19.7 %collective-permute-start.2 = (bf16[256,512]{1,0:T(8,128)(2,1)}, bf16[256,512]{1,0:T(8,128)(2,1)S(1)}, u32[]{:S(2)}, u32[]{:S(2)}) collective-permute-start(bf16[256,512]{1,0:T(8,128)(2,1)} %shard_map.105), channel_id=1, source_target_pairs={{0,16},{16,32},{32,48},{48,64},{64,80},{80,96},{96,112},{112,0},{1... | collective-permute-start | bytes 786440 | tf_op jit(solution)/shard_map/ppermute | solution.py:52
  7.9 19.2 %collective-permute-start.3 = (bf16[256,512]{1,0:T(8,128)(2,1)}, bf16[256,512]{1,0:T(8,128)(2,1)S(1)}, u32[]{:S(2)}, u32[]{:S(2)}) collective-permute-start(bf16[256,512]{1,0:T(8,128)(2,1)} %shard_map.105), channel_id=1, source_target_pairs={{0,144},{16,160},{32,176},{48,192},{64,208},{80,224},{96,240},{112... | collective-permute-start | bytes 786440 | tf_op jit(solution)/shard_map/ppermute | solution.py:52
  9.6 17.6 %collective-permute-start.4 = (bf16[256,512]{1,0:T(8,128)(2,1)}, bf16[256,512]{1,0:T(8,128)(2,1)S(1)}, u32[]{:S(2)}, u32[]{:S(2)}) collective-permute-start(bf16[256,512]{1,0:T(8,128)(2,1)} %shard_map.105), channel_id=1, source_target_pairs={{0,112},{16,0},{32,16},{48,32},{64,48},{80,64},{96,80},{112,96},{1... | collective-permute-start | bytes 786440 | tf_op jit(solution)/shard_map/ppermute | solution.py:52
  13.2 12.5 %copy-start.13 = (bf16[256,512]{1,0:T(8,128)(2,1)}, bf16[256,512]{1,0:T(8,128)(2,1)S(1)}, u32[]{:S(2)}) copy-start(bf16[256,512]{1,0:T(8,128)(2,1)S(1)} %collective-permute-done.1.refs_0_) | copy-start | bytes 786436
  13.2 16.6 %collective-permute-start.5 = (bf16[256,512]{1,0:T(8,128)(2,1)}, bf16[256,512]{1,0:T(8,128)(2,1)S(1)}, u32[]{:S(2)}, u32[]{:S(2)}) collective-permute-start(bf16[256,512]{1,0:T(8,128)(2,1)} %shard_map.105), channel_id=1, source_target_pairs={{0,240},{16,128},{32,144},{48,160},{64,176},{80,192},{96,208},{112... | collective-permute-start | bytes 786440 | tf_op jit(solution)/shard_map/ppermute | solution.py:52
  25.7 4.1 %copy-start.15 = (bf16[256,512]{1,0:T(8,128)(2,1)}, bf16[256,512]{1,0:T(8,128)(2,1)S(1)}, u32[]{:S(2)}) copy-start(bf16[256,512]{1,0:T(8,128)(2,1)S(1)} %collective-permute-done.2.refs_1_) | copy-start | bytes 786436
  27.1 2.7 %copy-start.16 = (bf16[256,512]{1,0:T(8,128)(2,1)}, bf16[256,512]{1,0:T(8,128)(2,1)S(1)}, u32[]{:S(2)}) copy-start(bf16[256,512]{1,0:T(8,128)(2,1)S(1)} %collective-permute-done.3.refs_2_) | copy-start | bytes 786436
  27.1 2.7 %copy-start.17 = (bf16[256,512]{1,0:T(8,128)(2,1)}, bf16[256,512]{1,0:T(8,128)(2,1)S(1)}, u32[]{:S(2)}) copy-start(bf16[256,512]{1,0:T(8,128)(2,1)S(1)} %collective-permute-done.4.refs_3_) | copy-start | bytes 786436
  32.5 9.3 %copy-start.11 = (bf16[512,512]{1,0:T(8,128)(2,1)}, bf16[512,512]{1,0:T(8,128)(2,1)S(1)}, u32[]{:S(2)}) copy-start(bf16[512,512]{1,0:T(8,128)(2,1)S(1)} %constant_dynamic-update-slice_fusion.refs_2_) | copy-start | bytes 1572868
  32.5 23.8 %collective-permute-start.6 = (bf16[512,512]{1,0:T(8,128)(2,1)S(1)}, bf16[512,512]{1,0:T(8,128)(2,1)S(1)}, u32[]{:S(2)}, u32[]{:S(2)}) collective-permute-start(bf16[512,512]{1,0:T(8,128)(2,1)S(1)} %constant_dynamic-update-slice_fusion.refs_2_), channel_id=1, source_target_pairs={{0,16},{16,32},{32,48},{48,64},{64,80},{80,96},{96,112},{112,0},{1... | collective-permute-start | bytes 1572872 | tf_op jit(solution)/shard_map/ppermute | solution.py:52
  34.6 7.2 %copy-start.12 = (bf16[512,512]{1,0:T(8,128)(2,1)}, bf16[512,512]{1,0:T(8,128)(2,1)S(1)}, u32[]{:S(2)}) copy-start(bf16[512,512]{1,0:T(8,128)(2,1)S(1)} %constant_dynamic-update-slice_fusion.2.refs_3_) | copy-start | bytes 1572868
  34.6 21.6 %collective-permute-start.7 = (bf16[512,512]{1,0:T(8,128)(2,1)S(1)}, bf16[512,512]{1,0:T(8,128)(2,1)S(1)}, u32[]{:S(2)}, u32[]{:S(2)}) collective-permute-start(bf16[512,512]{1,0:T(8,128)(2,1)S(1)} %constant_dynamic-update-slice_fusion.2.refs_3_), channel_id=1, source_target_pairs={{0,112},{16,0},{32,16},{48,32},{64,48},{80,64},{96,80},{112,96},{1... | collective-permute-start | bytes 1572872 | tf_op jit(solution)/shard_map/ppermute | solution.py:52
  37.8 18.4 %collective-permute-start.9 = (bf16[512,512]{1,0:T(8,128)(2,1)S(1)}, bf16[512,512]{1,0:T(8,128)(2,1)S(1)}, u32[]{:S(2)}, u32[]{:S(2)}) collective-permute-start(bf16[512,512]{1,0:T(8,128)(2,1)S(1)} %constant_dynamic-update-slice_fusion.refs_2_), channel_id=1, source_target_pairs={{0,6},{2,0},{4,2},{6,4},{1,7},{3,1},{5,3},{7,5},{8,14},{10,8},{12,... | collective-permute-start | bytes 1572872 | tf_op jit(solution)/shard_map/ppermute | solution.py:52
  38.6 17.6 %collective-permute-start.10 = (bf16[512,512]{1,0:T(8,128)(2,1)S(1)}, bf16[512,512]{1,0:T(8,128)(2,1)S(1)}, u32[]{:S(2)}, u32[]{:S(2)}) collective-permute-start(bf16[512,512]{1,0:T(8,128)(2,1)S(1)} %constant_dynamic-update-slice_fusion.2.refs_3_), channel_id=1, source_target_pairs={{0,2},{2,4},{4,6},{6,0},{1,3},{3,5},{5,7},{7,1},{8,10},{10,12},{12... | collective-permute-start | bytes 1572872 | tf_op jit(solution)/shard_map/ppermute | solution.py:52
  41.1 15.2 %collective-permute-start.8 = (bf16[256,512]{1,0:T(8,128)(2,1)}, bf16[256,512]{1,0:T(8,128)(2,1)S(1)}, u32[]{:S(2)}, u32[]{:S(2)}) collective-permute-start(bf16[256,512]{1,0:T(8,128)(2,1)} %get-tuple-element.32.refs_1_), channel_id=1, source_target_pairs={{0,2},{2,4},{4,6},{6,0},{1,3},{3,5},{5,7},{7,1},{8,10},{10,12},{12... | collective-permute-start | bytes 786440 | tf_op jit(solution)/shard_map/ppermute | solution.py:52
  56.3 1.2 copy-start.7
  58.2 14.6 %collective-permute-start.11 = (bf16[512,512]{1,0:T(8,128)(2,1)}, bf16[512,512]{1,0:T(8,128)(2,1)S(1)}, u32[]{:S(2)}, u32[]{:S(2)}) collective-permute-start(bf16[512,512]{1,0:T(8,128)(2,1)} %get-tuple-element.33.refs_7_), channel_id=1, source_target_pairs={{0,16},{16,32},{32,48},{48,64},{64,80},{80,96},{96,112},{112,0},{1... | collective-permute-start | bytes 1572872 | tf_op jit(solution)/shard_map/ppermute | solution.py:52
  58.2 14.6 %collective-permute-start.12 = (bf16[512,512]{1,0:T(8,128)(2,1)}, bf16[512,512]{1,0:T(8,128)(2,1)S(1)}, u32[]{:S(2)}, u32[]{:S(2)}) collective-permute-start(bf16[512,512]{1,0:T(8,128)(2,1)} %get-tuple-element.34.refs_8_), channel_id=1, source_target_pairs={{0,112},{16,0},{32,16},{48,32},{64,48},{80,64},{96,80},{112,96},{1... | collective-permute-start | bytes 1572872 | tf_op jit(solution)/shard_map/ppermute | solution.py:52
  61.5 12.5 %collective-permute-start.13 = (bf16[512,512]{1,0:T(8,128)(2,1)}, bf16[512,512]{1,0:T(8,128)(2,1)S(1)}, u32[]{:S(2)}, u32[]{:S(2)}) collective-permute-start(bf16[512,512]{1,0:T(8,128)(2,1)} %get-tuple-element.33.refs_7_), channel_id=1, source_target_pairs={{0,6},{2,0},{4,2},{6,4},{1,7},{3,1},{5,3},{7,5},{8,14},{10,8},{12,... | collective-permute-start | bytes 1572872 | tf_op jit(solution)/shard_map/ppermute | solution.py:52
  62.0 12.0 %collective-permute-start.14 = (bf16[512,512]{1,0:T(8,128)(2,1)}, bf16[512,512]{1,0:T(8,128)(2,1)S(1)}, u32[]{:S(2)}, u32[]{:S(2)}) collective-permute-start(bf16[512,512]{1,0:T(8,128)(2,1)} %get-tuple-element.34.refs_8_), channel_id=1, source_target_pairs={{0,2},{2,4},{4,6},{6,0},{1,3},{3,5},{5,7},{7,1},{8,10},{10,12},{12... | collective-permute-start | bytes 1572872 | tf_op jit(solution)/shard_map/ppermute | solution.py:52
  72.9 1.1 copy-start.3
  72.9 1.1 copy-start.4
  76.5 9.2 %collective-permute-start.15 = (bf16[256,512]{1,0:T(8,128)(2,1)S(1)}, bf16[256,512]{1,0:T(8,128)(2,1)S(1)}, u32[]{:S(2)}, u32[]{:S(2)}) collective-permute-start(bf16[256,512]{1,0:T(8,128)(2,1)S(1)} %slice.6), channel_id=1, source_target_pairs={{0,16},{16,32},{32,48},{48,64},{64,80},{80,96},{96,112},{112,0},{1... | collective-permute-start | bytes 786440 | tf_op jit(solution)/shard_map/ppermute | solution.py:52
  76.6 16.9 %collective-permute-start.17 = (bf16[512,512]{1,0:T(8,128)(2,1)}, bf16[512,512]{1,0:T(8,128)(2,1)S(1)}, u32[]{:S(2)}, u32[]{:S(2)}) collective-permute-start(bf16[512,512]{1,0:T(8,128)(2,1)} %get-tuple-element.38.refs_0_), channel_id=1, source_target_pairs={{0,6},{2,0},{4,2},{6,4},{1,7},{3,1},{5,3},{7,5},{8,14},{10,8},{12,... | collective-permute-start | bytes 1572872 | tf_op jit(solution)/shard_map/ppermute | solution.py:52
  77.1 16.5 %collective-permute-start.18 = (bf16[512,512]{1,0:T(8,128)(2,1)}, bf16[512,512]{1,0:T(8,128)(2,1)S(1)}, u32[]{:S(2)}, u32[]{:S(2)}) collective-permute-start(bf16[512,512]{1,0:T(8,128)(2,1)} %get-tuple-element.39.refs_1_), channel_id=1, source_target_pairs={{0,2},{2,4},{4,6},{6,0},{1,3},{3,5},{5,7},{7,1},{8,10},{10,12},{12... | collective-permute-start | bytes 1572872 | tf_op jit(solution)/shard_map/ppermute | solution.py:52
  80.9 12.1 %collective-permute-start.19 = (bf16[256,512]{1,0:T(8,128)(2,1)S(1)}, bf16[256,512]{1,0:T(8,128)(2,1)S(1)}, u32[]{:S(2)}, u32[]{:S(2)}) collective-permute-start(bf16[256,512]{1,0:T(8,128)(2,1)S(1)} %slice.6), channel_id=1, source_target_pairs={{0,22},{2,16},{4,18},{6,20},{16,38},{18,32},{20,34},{22,36},{32,54... | collective-permute-start | bytes 786440 | tf_op jit(solution)/shard_map/ppermute | solution.py:52
  81.0 12.0 %collective-permute-start.16 = (bf16[256,512]{1,0:T(8,128)(2,1)S(1)}, bf16[256,512]{1,0:T(8,128)(2,1)S(1)}, u32[]{:S(2)}, u32[]{:S(2)}) collective-permute-start(bf16[256,512]{1,0:T(8,128)(2,1)S(1)} %slice.7), channel_id=1, source_target_pairs={{0,112},{16,0},{32,16},{48,32},{64,48},{80,64},{96,80},{112,96},{1... | collective-permute-start | bytes 786440 | tf_op jit(solution)/shard_map/ppermute | solution.py:52
  85.8 7.3 %copy-start.22 = (bf16[256,512]{1,0:T(8,128)(2,1)}, bf16[256,512]{1,0:T(8,128)(2,1)S(1)}, u32[]{:S(2)}) copy-start(bf16[256,512]{1,0:T(8,128)(2,1)S(1)} %collective-permute-done.15.refs_0_) | copy-start | bytes 786436
  85.8 7.3 %collective-permute-start.20 = (bf16[256,512]{1,0:T(8,128)(2,1)S(1)}, bf16[256,512]{1,0:T(8,128)(2,1)S(1)}, u32[]{:S(2)}, u32[]{:S(2)}) collective-permute-start(bf16[256,512]{1,0:T(8,128)(2,1)S(1)} %slice.7), channel_id=1, source_target_pairs={{0,114},{2,116},{4,118},{6,112},{16,2},{18,4},{20,6},{22,0},{32,18... | collective-permute-start | bytes 786440 | tf_op jit(solution)/shard_map/ppermute | solution.py:52
  88.3 6.8 %copy-start.2 = (s32[2]{0:T(128)S(1)}, s32[2]{0:T(128)}, u32[]{:S(2)}) copy-start(s32[2]{0:T(128)} %lengths.1) | copy-start | bytes 28
  93.0 44.9 %copy-start.29 = (s32[2,64]{1,0:T(2,128)S(1)}, s32[2,64]{1,0:T(2,128)}, u32[]{:S(2)}) copy-start(s32[2,64]{1,0:T(2,128)} %param.15) | copy-start | bytes 1540
  100.7 1.5 copy-start.1
  128.6 12.5 %collective-permute-start.21 = (bf16[1280,128]{1,0:T(8,128)(2,1)}, bf16[1280,128]{1,0:T(8,128)(2,1)S(1)}, u32[]{:S(2)}, u32[]{:S(2)}) collective-permute-start(bf16[1280,128]{1,0:T(8,128)(2,1)} %get-tuple-element.44), channel_id=1, source_target_pairs={{0,0},{2,2},{4,12},{6,14},{8,4},{10,6},{12,8},{14,10},{1,1},{3,3},... | collective-permute-start | bytes 983048 | tf_op jit(solution)/shard_map/ppermute | solution.py:496
  131.2 12.5 %collective-permute-start.22 = (bf16[1280,128]{1,0:T(8,128)(2,1)}, bf16[1280,128]{1,0:T(8,128)(2,1)S(1)}, u32[]{:S(2)}, u32[]{:S(2)}) collective-permute-start(bf16[1280,128]{1,0:T(8,128)(2,1)} %get-tuple-element.45), channel_id=1, source_target_pairs={{0,2},{2,4},{4,14},{6,8},{8,6},{10,0},{12,10},{14,12},{1,3},{3,5},... | collective-permute-start | bytes 983048 | tf_op jit(solution)/shard_map/ppermute | solution.py:496
  134.4 10.8 %collective-permute-start.23 = (bf16[1280,128]{1,0:T(8,128)(2,1)}, bf16[1280,128]{1,0:T(8,128)(2,1)S(1)}, u32[]{:S(2)}, u32[]{:S(2)}) collective-permute-start(bf16[1280,128]{1,0:T(8,128)(2,1)} %get-tuple-element.46), channel_id=1, source_target_pairs={{0,4},{2,6},{4,8},{6,10},{8,0},{10,2},{12,12},{14,14},{1,5},{3,7},... | collective-permute-start | bytes 983048 | tf_op jit(solution)/shard_map/ppermute | solution.py:496
  136.9 11.7 %collective-permute-start.24 = (bf16[1280,128]{1,0:T(8,128)(2,1)}, bf16[1280,128]{1,0:T(8,128)(2,1)S(1)}, u32[]{:S(2)}, u32[]{:S(2)}) collective-permute-start(bf16[1280,128]{1,0:T(8,128)(2,1)} %get-tuple-element.47), channel_id=1, source_target_pairs={{0,6},{2,0},{4,10},{6,12},{8,2},{10,4},{12,14},{14,8},{1,7},{3,1},... | collective-permute-start | bytes 983048 | tf_op jit(solution)/shard_map/ppermute | solution.py:496
  137.0 4.1 %collective-permute-start.25 = (f32[1,512]{1,0:T(1,128)}, f32[1,512]{1,0:T(1,128)S(1)}, u32[]{:S(2)}, u32[]{:S(2)}) collective-permute-start(f32[1,512]{1,0:T(1,128)} %get-tuple-element.48.own_scale), channel_id=1, source_target_pairs={{0,8},{8,0},{1,9},{9,1},{2,10},{10,2},{3,11},{11,3},{4,12},{12,4},... | collective-permute-start | bytes 6152 | tf_op jit(solution)/shard_map/ppermute | solution.py:52
  141.1 7.5 %copy-start.27 = (f32[1,512]{1,0:T(1,128)}, f32[1,512]{1,0:T(1,128)S(1)}, u32[]{:S(2)}) copy-start(f32[1,512]{1,0:T(1,128)S(1)} %collective-permute-done.25.other_scale) | copy-start | bytes 6148
  141.1 7.5 %copy-start.30 = (bf16[1280,128]{1,0:T(8,128)(2,1)}, bf16[1280,128]{1,0:T(8,128)(2,1)S(1)}, u32[]{:S(2)}) copy-start(bf16[1280,128]{1,0:T(8,128)(2,1)S(1)} %collective-permute-done.21.r0) | copy-start | bytes 983044
  143.7 4.9 %copy-start.31 = (bf16[1280,128]{1,0:T(8,128)(2,1)}, bf16[1280,128]{1,0:T(8,128)(2,1)S(1)}, u32[]{:S(2)}) copy-start(bf16[1280,128]{1,0:T(8,128)(2,1)S(1)} %collective-permute-done.22.r1) | copy-start | bytes 983044
  145.2 3.4 %copy-start.32 = (bf16[1280,128]{1,0:T(8,128)(2,1)}, bf16[1280,128]{1,0:T(8,128)(2,1)S(1)}, u32[]{:S(2)}) copy-start(bf16[1280,128]{1,0:T(8,128)(2,1)S(1)} %collective-permute-done.23.r2) | copy-start | bytes 983044
  172.9 16.3 %all-to-all-start.2 = ((bf16[32,32,128]{2,1,0:T(8,128)(2,1)}), bf16[32,32,128]{2,1,0:T(8,128)(2,1)S(1)}, u32[]{:S(2)}, u32[]{:S(2)}) async-start(bf16[32,32,128]{2,1,0:T(8,128)(2,1)} %shard_map.114), calls=%async_computation.2 | async-start | bytes 524288 | tf_op jit(solution)/shard_map/all_to_all | solution.py:507
  177.5 11.7 %copy-start.26 = (f32[2,512]{1,0:T(2,128)}, f32[2,512]{1,0:T(2,128)S(1)}, u32[]{:S(2)}) copy-start(f32[2,512]{1,0:T(2,128)S(1)} %pad_maximum_fusion.both) | copy-start | bytes 12292
  177.5 1.3 collective-permute-start.26
  178.8 10.5 %copy-start.28 = (f32[2,512]{1,0:T(2,128)}, f32[2,512]{1,0:T(2,128)S(1)}, u32[]{:S(2)}) copy-start(f32[2,512]{1,0:T(2,128)S(1)} %collective-permute-done.26.far) | copy-start | bytes 12292
  (14 other events, 11.0 us)

commit v2 on v1

--- a/solution.py
+++ b/solution.py
@@ -14,7 +14,7 @@
 TILE = 320
 GROUP = 8
 MIB = 1024 * 1024
-VMEM = 60 * MIB
+VMEM = 20 * MIB
 SHARED = 16 * MIB
 
 eps = 1e-05
@@ -52,18 +52,43 @@
     return lax.ppermute(value, names if len(names) > 1 else names[0], pairs)
 
 
-def gate_kernel(*refs):
-    pass
-
-
-def gate(values, after):
-    args = [pltpu.with_memory_space_constraint(v, pltpu.HBM) for v in values]
-    return pl.pallas_call(
-        gate_kernel,
+def in_vmem(values):
+    return [pltpu.with_memory_space_constraint(value, pltpu.VMEM) for value in values]
+
+
+def relay_kernel(count, picks, *refs):
+    sources, outs, sems = refs[:count], refs[count + 1 + count : -1], refs[-1]
+    copies = []
+    for out, parts in zip(outs, picks):
+        at = 0
+        for i, start, rows in parts:
+            copies.append(
+                pltpu.make_async_copy(
+                    sources[i].at[pl.ds(start, rows)], out.at[pl.ds(at, rows)], sems.at[len(copies)]
+                )
+            )
+            at += rows
+    for copy in copies:
+        copy.start()
+    for copy in copies:
+        copy.wait()
+
+
+def relay(values, after, picks=()):
+    args = in_vmem(values)
+    shapes = [jax.ShapeDtypeStruct(v.shape, v.dtype) for v in values]
+    for parts in picks:
+        shape = (sum(rows for _, _, rows in parts), values[0].shape[1])
+        shapes.append(pltpu.VMEM(shape, values[0].dtype))
+    return pl.pallas_call(
+        functools.partial(relay_kernel, len(args), picks),
         in_specs=[ANYWHERE] * (len(args) + 1),
-        out_specs=[ANYWHERE] * len(args),
-        out_shape=[jax.ShapeDtypeStruct(v.shape, v.dtype) for v in values],
+        out_specs=[ANYWHERE] * len(shapes),
+        out_shape=shapes,
         input_output_aliases={i: i for i in range(len(args))},
+        scratch_shapes=[
+            pltpu.SemaphoreType.DMA((max(1, sum(len(p) for p in picks)),)),
+        ],
         compiler_params=params(SHARED),
         cost_estimate=cost(),
     )(*args, after)
@@ -112,7 +137,7 @@
         take_kernel,
         in_specs=[ANYWHERE],
         out_specs=ANYWHERE,
-        out_shape=pltpu.HBM((PIECE, 4 * HD), weight.dtype),
+        out_shape=pltpu.VMEM((PIECE, 4 * HD), weight.dtype),
         scratch_shapes=[pltpu.SemaphoreType.DMA((4,))],
         compiler_params=params(SHARED),
         cost_estimate=cost(size=MIB),
@@ -130,41 +155,32 @@
     outs, (held, sems) = refs[:-2], refs[-2:]
     yh, z, x = lax.axis_index("yh"), lax.axis_index("z"), lax.axis_index("x")
     core = lax.axis_index("core")
-    width = held.shape[1]
-    copies, columns, sem = [], [], 0
-    for i, pieces in enumerate(names):
-        at = len(columns) * PIECE
+    width = 4 * HD
+    copies, columns, weights = [], [], []
+    for source, pieces in zip(sources, names):
         if pieces is None:
             pieces = [(0, 0, None), (0, 0, None)]
-            some = [
-                pltpu.make_async_copy(
-                    sources[i].at[:, pl.ds(pl.multiple_of((2 * j + core) * HD, HD), HD)],
-                    held.at[pl.ds(at, 2 * PIECE), pl.ds(j * HD, HD)],
-                    sems.at[sem + j],
+            for j in range(4):
+                lanes = pl.ds(pl.multiple_of((2 * j + core) * HD, HD), HD)
+                copies.append(
+                    pltpu.make_async_copy(
+                        source.at[:, lanes], held.at[:, pl.ds(j * HD, HD)], sems.at[j]
+                    )
                 )
-                for j in range(4)
-            ]
-        else:
-            some = [
-                pltpu.make_async_copy(
-                    sources[i], held.at[pl.ds(at, len(pieces) * PIECE)], sems.at[sem]
-                )
-            ]
-        sem += len(some)
+            source = held
         for j, (other, dz, mine) in enumerate(pieces):
             half = j if mine is None else (x + (0 if mine else 1)) % 2
             shard = ((yh + other) % 2) * 8 + (z + dz + 8) % 8
             columns.append(pl.multiple_of((shard * 2 + half) * PIECE, PIECE))
-            copies.append(some if j == 0 else [])
-    for some in copies:
-        for copy in some:
-            copy.start()
+            weights.append((source, j * PIECE))
+    for copy in copies:
+        copy.start()
+    for copy in copies:
+        copy.wait()
     rows = own.shape[0]
     total = refs[-3] if last else outs[0]
-    for piece, column in enumerate(columns):
-        for copy in copies[piece]:
-            copy.wait()
-        weight = held[piece * PIECE : (piece + 1) * PIECE]
+    for piece, (column, (source, start)) in enumerate(zip(columns, weights)):
+        weight = source[start : start + PIECE]
         for side, tokens in enumerate((own, sib)):
             for row in range(0, rows, TILE):
                 value = jnp.dot(
@@ -199,9 +215,12 @@
     n = sum(2 if ids is None else len(ids) for ids in names)
     rows, width = own.shape[0], 4 * HD
     last = lengths is not None
-    in_specs = [WHOLE, WHOLE] + [ANYWHERE] * len(pieces)
-    args = [pltpu.with_memory_space_constraint(value, pltpu.VMEM) for value in (own, sib)]
-    args += [pltpu.with_memory_space_constraint(value, pltpu.HBM) for value, _ in pieces]
+    in_specs = [WHOLE, WHOLE] + [ANYWHERE if ids is None else WHOLE for ids in names]
+    args = [own, sib] + [value for value, _ in pieces]
+    args = [
+        value if spec is ANYWHERE else pltpu.with_memory_space_constraint(value, pltpu.VMEM)
+        for value, spec in zip(args, in_specs)
+    ]
     aliases = {}
     if acc is not None:
         in_specs.append(WHOLE)
@@ -209,8 +228,8 @@
             aliases = {len(args): 0}
         args.append(acc)
     scratch = [
-        pltpu.VMEM((n * PIECE, width), jnp.bfloat16),
-        pltpu.SemaphoreType.DMA((len(pieces) + 3,)),
+        pltpu.VMEM((2 * PIECE, width), jnp.bfloat16),
+        pltpu.SemaphoreType.DMA((4,)),
     ]
     if not last:
         out_shape = [pltpu.VMEM((2 * rows, width), jnp.float32)]
@@ -249,11 +268,11 @@
         quantize_kernel,
         in_specs=[WHOLE, WHOLE, SCALAR],
         out_specs=[WHOLE] * 5,
-        out_shape=[jax.ShapeDtypeStruct((rows, HD), jnp.bfloat16)] * 4
+        out_shape=[pltpu.VMEM((rows, HD), jnp.bfloat16)] * 4
         + [jax.ShapeDtypeStruct((1, width), jnp.float32)],
-        compiler_params=params(54 * MIB),
+        compiler_params=params(VMEM),
         cost_estimate=cost(4 * rows * width, 6 * rows * width),
-    )(proj, squares, lengths)
+    )(pltpu.with_memory_space_constraint(proj, pltpu.VMEM), squares, lengths)
 
 
 def head_scale(own, other, side):
@@ -352,7 +371,7 @@
         ],
         compiler_params=params(VMEM),
         cost_estimate=cost(8 * heads * rows * HD, 16 * rows * HD, 2 * heads * rows),
-    )(page_table, *received, query, limits, own_scale, other_scale)
+    )(page_table, *in_vmem(received), query, limits, own_scale, other_scale)
 
 
 def merge_kernel(parts, query, new_key, new_value, own_scale, other_scale, out, rows):
@@ -399,7 +418,7 @@
         scratch_shapes=[pltpu.VMEM((32, 6 * HD), jnp.float32)],
         compiler_params=params(VMEM),
         cost_estimate=cost(1 << 18, 1 << 19, 512),
-    )(parts, query, new_key, new_value, own_scale, other_scale)
+    )(*in_vmem([parts]), query, new_key, new_value, own_scale, other_scale)
 
 
 def finish_kernel(whole, both, far, attended, scales):
@@ -439,51 +458,53 @@
         ],
         compiler_params=params(VMEM),
         cost_estimate=cost(0, MIB // 2),
-    )(whole, both, far)
+    )(*in_vmem([whole]), both, far)
 
 
 def body(tokens, kv_weight, lengths, page_table, queries, new_keys, new_values, positions):
     sibling = send(tokens, core=1)
     own = keep(pltpu.with_memory_space_constraint(tokens, pltpu.HBM))
 
-    def joined(*values):
-        return jnp.concatenate(values, axis=0)
-
     def swapped(ids):
         return [(other, dz, False) for other, dz, _ in ids]
 
+    at = lambda dz: [(0, dz, True), (1, dz - (1 if dz > 0 else -1), True)]
+    near, far = lambda dz: [(0, dz, True)], lambda dz: [(1, dz, True)]
+    part = lambda i: (i, 0, PIECE)
+
     first = take(kv_weight)
-    cross = send(first, yh=1)
-    up, down = send(first, z=1), send(first, z=-1)
-    up_far, down_far = send(first, yh=1, z=1), send(first, yh=1, z=-1)
-    cross, up, up_far, down, down_far = gate([cross, up, up_far, down, down_far], own)
-    up, down = joined(up, up_far), joined(down, down_far)
-    at = lambda dz: [(0, dz, True), (1, dz, True)]
-
-    sides = send(cross, x=1), send(up, x=-1), send(down, x=1)
+    cross, up, down = send(first, yh=1), send(first, z=1), send(first, z=-1)
+    cross, up, down, both_up, both_down = relay(
+        [cross, up, down], own, [[part(1), part(0)], [part(2), part(0)]]
+    )
+    wave = [(kv_weight, None), (both_up, at(-1)), (down, near(1))]
+
+    over, under = send(both_up, x=-1), send(down, x=1)
+    up, down = send(both_up, z=1), send(both_down, z=-1)
+    sib = keep(sibling)
+    up, down, over, under = relay([up, down, over, under], sib)
+    wave += [(over, swapped(at(-1))), (under, swapped(near(1))), (up, at(-2)), (down, at(2))]
+
+    over, under = send(up, x=-1), send(down, x=1)
     next_up, next_down = send(up, z=1), send(down, z=-1)
-    sib = keep(sibling)
-    next_up, next_down, *sides = gate([next_up, next_down, *sides], sib)
-    wave = [(kv_weight, None), (cross, [(1, 0, True)]), (up, at(-1)), (down, at(1))]
-    wave += [(sides[0], [(1, 0, False)]), (sides[1], swapped(at(-1))), (sides[2], swapped(at(1)))]
-    wave += [(next_up, at(-2)), (next_down, at(2))]
-    up, down = next_up, next_down
-
     acc = project(own, sib, wave)[0]
-    sides = send(up, x=-1), send(down, x=1)
-    next_up, next_down = send(up, z=1), send(down, z=-1)
-    next_up, next_down, *sides = gate([next_up, next_down, *sides], acc)
-    wave = [(next_up, at(-3)), (next_down, at(3))]
-    wave += [(sides[0], swapped(at(-2))), (sides[1], swapped(at(2)))]
-    up, down = next_up, next_down
-
-    near, far = up[:PIECE], down[PIECE:]
-    wave_last = [(send(near, z=1), at(-4)[:1]), (send(far, z=-1), at(4)[1:])]
-    wave_last += [(send(up, x=-1), swapped(at(-3))), (send(down, x=1), swapped(at(3)))]
-    wave_last += [(send(near, z=1, x=-1), swapped(at(-4)[:1]))]
-    wave_last += [(send(far, z=-1, x=1), swapped(at(4)[1:]))]
+    up, down, over, under, last = relay(
+        [next_up, next_down, over, under], acc, [[(1, PIECE, PIECE)]]
+    )
+    wave = [(up, at(-3)), (down, at(3)), (over, swapped(at(-2))), (under, swapped(at(2)))]
+
+    over, under = send(up, x=-1), send(down, x=1)
+    next_up, next_down = send(up, z=1), send(last, z=-1)
     acc = project(own, sib, wave, acc)[0]
-    proj, squares = project(own, sib, wave_last, acc, lengths)
+    up, down, over, under, last = relay([next_up, next_down, over, under], acc, [[part(0)]])
+    wave = [(up, at(-4)), (down, far(3)), (over, swapped(at(-3))), (under, swapped(at(3)))]
+
+    over, under = send(up, x=-1), send(down, x=1)
+    cross, corner = send(last, yh=1), send(last, yh=1, x=1)
+    acc = project(own, sib, wave, acc)[0]
+    wave = [(over, swapped(at(-4))), (under, swapped(far(3)))]
+    wave += [(cross, far(-4)), (corner, swapped(far(-4)))]
+    proj, squares = project(own, sib, wave, acc, lengths)
     squares = lax.all_to_all(squares, ("yh", "z", "x"), 0, 0, tiled=True)
     *sent, scale = quantize(proj, squares, lengths)
 
@@ -496,7 +517,7 @@
         received.append(lax.ppermute(sent[k], ("tp", "x"), pairs))
 
     other_scale = send(scale, tp=1)
-    both = joined(scale, other_scale)
+    both = jnp.concatenate([scale, other_scale], axis=0)
     far = send(both, core=1)
 
     kv_cache, part = attend(

time: 192 us -> 159 us (0.83)
  local copies, waits for them, and re-layouts: 16.7 us -> 1.38 us
  Pallas kernels: 36.2 us -> 24.9 us
  blocking collectives: 39 us -> 34.6 us
  starting transfers between devices: 53.6 us -> 50.1 us
  waiting for transfers between devices: 44.4 us -> 47 us
    unnamed x70 -> x14, local copies, waits for them, and re-layouts: 12 us -> 1.25 us
    pallas_call x3 -> x4, Pallas kernels: 18 us -> 13 us  [project(): pl.pallas_call(functools.partial(project_kernel, names, acc is not None,...]
    ppermute x23 -> x22, starting transfers between devices: 41.4 us -> 37.8 us  [send(): return lax.ppermute(value, names if len(names) > 1 else names[0], pairs)]
    all_to_all x1, blocking collectives: 23.4 us -> 20.6 us  [body(): squares = lax.all_to_all(squares, ('yh', 'z', 'x'), 0, 0, tiled=True)]
    ppermute x23 -> x22, waiting for transfers between devices: 26.4 us -> 28.4 us  [send(): return lax.ppermute(value, names if len(names) > 1 else names[0], pairs)]
    slice x2 -> x0, local copies, waits for them, and re-layouts: 1.97 us -> none  [body(): near, far = (up[:PIECE], down[PIECE:])]
    concatenate x2 -> x0, local copies, waits for them, and re-layouts: 1.94 us -> none  [joined(): return jnp.concatenate(values, axis=0)]
    pallas_call x1, Pallas kernels: 2.99 us -> 1.06 us  [quantize(): pl.pallas_call(quantize_kernel, in_specs=[WHOLE, WHOLE, SCALAR], out_spec...]
  transfers between devices with their start and end apart: 28 -> 27, of which waited for: 13 -> 16; matrix products, arithmetic and copies ran while one was open for 3% -> 0% of each run, Pallas kernels for 9% -> 10%
where the time goes in v2:
time: 159 us
  starting transfers between devices  50.1 us (32%)
  waiting for transfers between devices  47 us (30%)
  blocking collectives  34.6 us (22%)
  Pallas kernels  24.9 us (16%)
    ppermute x22, starting transfers between devices, send(): return lax.ppermute(value, names if len(names) > 1 else names[0], pairs)  37.8 us
    ppermute x22, waiting for transfers between devices, send(): return lax.ppermute(value, names if len(names) > 1 else names[0], pairs)  28.4 us
    all_to_all x1, blocking collectives, body(): squares = lax.all_to_all(squares, ('yh', 'z', 'x'), 0, 0, tiled=True)  20.6 us
    all_to_all x1, blocking collectives, body(): parts = lax.all_to_all(part, ('z', 'tp'), 0, 0, tiled=True)  14 us
    pallas_call x4, Pallas kernels, project(): pl.pallas_call(functools.partial(project_kernel, names, acc is not None,...  13 us
    all_to_all x1, waiting for transfers between devices, body(): whole = lax.all_to_all(result, ('yh', 'z', 'tp'), 0, 0, tiled=True)  11.1 us
    ppermute x4, starting transfers between devices, body(): received.append(lax.ppermute(sent[k], ('tp', 'x'), pairs))  8.42 us
    ppermute x4, waiting for transfers between devices, body(): received.append(lax.ppermute(sent[k], ('tp', 'x'), pairs))  7.44 us
  transfers between devices with their start and end apart: 27, of which 16 were waited for; matrix products, arithmetic and copies ran while one was open for 0% of the time, Pallas kernels for 10%

profile of v2, /device:TPU:6, one launch (start us, length us, event | category | flops | bytes accessed | tf_op | source)
XLA Modules:
  0.0 159.0 jit_solution(12051896134517797506)
XLA Ops:
  0.7 1.2 copy-done
  2.1 3.3 %collective-permute-start.1 = (bf16[256,512]{1,0:T(8,128)(2,1)S(1)}, bf16[256,512]{1,0:T(8,128)(2,1)S(1)}, u32[]{:S(2)}, u32[]{:S(2)}) collective-permute-start(bf16[256,512]{1,0:T(8,128)(2,1)S(1)} %shard_map.105), channel_id=1, source_target_pairs={{0,128},{128,0},{1,129},{129,1},{2,130},{130,2},{3,131},{131,3},{4... | collective-permute-start | bytes 786440 | tf_op jit(solution)/shard_map/ppermute | solution.py:52
  5.4 1.9 %collective-permute-start.2 = (bf16[256,512]{1,0:T(8,128)(2,1)S(1)}, bf16[256,512]{1,0:T(8,128)(2,1)S(1)}, u32[]{:S(2)}, u32[]{:S(2)}) collective-permute-start(bf16[256,512]{1,0:T(8,128)(2,1)S(1)} %shard_map.105), channel_id=1, source_target_pairs={{0,16},{16,32},{32,48},{48,64},{64,80},{80,96},{96,112},{112,0},{1... | collective-permute-start | bytes 786440 | tf_op jit(solution)/shard_map/ppermute | solution.py:52
  7.3 3.9 %collective-permute-start.3 = (bf16[256,512]{1,0:T(8,128)(2,1)S(1)}, bf16[256,512]{1,0:T(8,128)(2,1)S(1)}, u32[]{:S(2)}, u32[]{:S(2)}) collective-permute-start(bf16[256,512]{1,0:T(8,128)(2,1)S(1)} %shard_map.105), channel_id=1, source_target_pairs={{0,112},{16,0},{32,16},{48,32},{64,48},{80,64},{96,80},{112,96},{1... | collective-permute-start | bytes 786440 | tf_op jit(solution)/shard_map/ppermute | solution.py:52
  11.2 4.0 %shard_map.103.refs_3_.own = bf16[640,8192]{1,0:T(8,128)(2,1)S(1)} custom-call(bf16[640,8192]{1,0:T(8,128)(2,1)} %source.1), custom_call_target="tpu_custom_call" | custom-call | bytes 20971520 | tf_op jit(solution)/shard_map/pallas_call | solution.py:104
  15.2 2.7 %collective-permute-done.2.refs_1_ = bf16[256,512]{1,0:T(8,128)(2,1)S(1)} collective-permute-done((bf16[256,512]{1,0:T(8,128)(2,1)S(1)}, bf16[256,512]{1,0:T(8,128)(2,1)S(1)}, u32[]{:S(2)}, u32[]{:S(2)}) %collective-permute-start.2) | collective-permute-done | bytes 262176 | tf_op jit(solution)/shard_map/ppermute | solution.py:52
  18.1 3.2 %collective-permute-start.5 = (bf16[512,512]{1,0:T(8,128)(2,1)S(1)}, bf16[512,512]{1,0:T(8,128)(2,1)S(1)}, u32[]{:S(2)}, u32[]{:S(2)}) collective-permute-start(bf16[512,512]{1,0:T(8,128)(2,1)S(1)} %get-tuple-element.32), channel_id=1, source_target_pairs={{0,112},{16,0},{32,16},{48,32},{64,48},{80,64},{96,80},{112,96},{1... | collective-permute-start | bytes 1572872 | tf_op jit(solution)/shard_map/ppermute | solution.py:52
  21.3 0.8 collective-permute-start.6
  22.2 2.4 %collective-permute-start.7 = (bf16[256,512]{1,0:T(8,128)(2,1)S(1)}, bf16[256,512]{1,0:T(8,128)(2,1)S(1)}, u32[]{:S(2)}, u32[]{:S(2)}) collective-permute-start(bf16[256,512]{1,0:T(8,128)(2,1)S(1)} %get-tuple-element.33.refs_2_), channel_id=1, source_target_pairs={{0,2},{2,4},{4,6},{6,0},{1,3},{3,5},{5,7},{7,1},{8,10},{10,12},{12... | collective-permute-start | bytes 786440 | tf_op jit(solution)/shard_map/ppermute | solution.py:52
  24.6 0.7 shard_map.104.refs_4_.sib
  25.3 4.0 %collective-permute-done.7.refs_3_ = bf16[256,512]{1,0:T(8,128)(2,1)S(1)} collective-permute-done((bf16[256,512]{1,0:T(8,128)(2,1)S(1)}, bf16[256,512]{1,0:T(8,128)(2,1)S(1)}, u32[]{:S(2)}, u32[]{:S(2)}) %collective-permute-start.7) | collective-permute-done | bytes 262176 | tf_op jit(solution)/shard_map/ppermute | solution.py:52
  29.3 3.6 %collective-permute-done.4.refs_0_ = bf16[512,512]{1,0:T(8,128)(2,1)S(1)} collective-permute-done((bf16[512,512]{1,0:T(8,128)(2,1)S(1)}, bf16[512,512]{1,0:T(8,128)(2,1)S(1)}, u32[]{:S(2)}, u32[]{:S(2)}) %collective-permute-start.4) | collective-permute-done | bytes 524320 | tf_op jit(solution)/shard_map/ppermute | solution.py:52
  32.9 2.7 %collective-permute-done.6.refs_2_ = bf16[512,512]{1,0:T(8,128)(2,1)S(1)} collective-permute-done((bf16[512,512]{1,0:T(8,128)(2,1)S(1)}, bf16[512,512]{1,0:T(8,128)(2,1)S(1)}, u32[]{:S(2)}, u32[]{:S(2)}) %collective-permute-start.6) | collective-permute-done | bytes 524320 | tf_op jit(solution)/shard_map/ppermute | solution.py:52
  35.6 3.2 %collective-permute-start.9 = (bf16[512,512]{1,0:T(8,128)(2,1)S(1)}, bf16[512,512]{1,0:T(8,128)(2,1)S(1)}, u32[]{:S(2)}, u32[]{:S(2)}) collective-permute-start(bf16[512,512]{1,0:T(8,128)(2,1)S(1)} %get-tuple-element.35.refs_6_), channel_id=1, source_target_pairs={{0,112},{16,0},{32,16},{48,32},{64,48},{80,64},{96,80},{112,96},{1... | collective-permute-start | bytes 1572872 | tf_op jit(solution)/shard_map/ppermute | solution.py:52
  38.9 3.2 %collective-permute-start.11 = (bf16[512,512]{1,0:T(8,128)(2,1)S(1)}, bf16[512,512]{1,0:T(8,128)(2,1)S(1)}, u32[]{:S(2)}, u32[]{:S(2)}) collective-permute-start(bf16[512,512]{1,0:T(8,128)(2,1)S(1)} %get-tuple-element.35.refs_6_), channel_id=1, source_target_pairs={{0,2},{2,4},{4,6},{6,0},{1,3},{3,5},{5,7},{7,1},{8,10},{10,12},{12... | collective-permute-start | bytes 1572872 | tf_op jit(solution)/shard_map/ppermute | solution.py:52
  42.1 4.5 %shard_map.108.refs_4_ = f32[1280,512]{1,0:T(8,128)S(1)} custom-call(bf16[640,8192]{1,0:T(8,128)(2,1)S(1)} %shard_map.103.refs_3_.own, bf16[640,8192]{1,0:T(8,128)(2,1)S(1)} %shard_map.104.refs_4_.sib, bf16[512,1024]{1,0:T(8,128)(2,1)S(1)} %copy-done, bf16[512,512]{1,0:T(8,128)(2,1)S(1)} %get-tuple-element.31.refs_1_, ...), custom_call_target="tpu_custom_call" | custom-call | flops 4026531840 | bytes 3145728 | tf_op jit(solution)/shard_map/pallas_call | solution.py:242
  46.6 2.3 %collective-permute-done.8.refs_0_ = bf16[512,512]{1,0:T(8,128)(2,1)S(1)} collective-permute-done((bf16[512,512]{1,0:T(8,128)(2,1)S(1)}, bf16[512,512]{1,0:T(8,128)(2,1)S(1)}, u32[]{:S(2)}, u32[]{:S(2)}) %collective-permute-start.8) | collective-permute-done | bytes 524320 | tf_op jit(solution)/shard_map/ppermute | solution.py:52
  48.9 2.7 %collective-permute-done.10.refs_2_ = bf16[512,512]{1,0:T(8,128)(2,1)S(1)} collective-permute-done((bf16[512,512]{1,0:T(8,128)(2,1)S(1)}, bf16[512,512]{1,0:T(8,128)(2,1)S(1)}, u32[]{:S(2)}, u32[]{:S(2)}) %collective-permute-start.10) | collective-permute-done | bytes 524320 | tf_op jit(solution)/shard_map/ppermute | solution.py:52
  51.8 3.2 %collective-permute-start.15 = (bf16[512,512]{1,0:T(8,128)(2,1)S(1)}, bf16[512,512]{1,0:T(8,128)(2,1)S(1)}, u32[]{:S(2)}, u32[]{:S(2)}) collective-permute-start(bf16[512,512]{1,0:T(8,128)(2,1)S(1)} %get-tuple-element.40.refs_1_), channel_id=1, source_target_pairs={{0,2},{2,4},{4,6},{6,0},{1,3},{3,5},{5,7},{7,1},{8,10},{10,12},{12... | collective-permute-start | bytes 1572872 | tf_op jit(solution)/shard_map/ppermute | solution.py:52
  55.0 3.1 %collective-permute-start.13 = (bf16[256,512]{1,0:T(8,128)(2,1)S(1)}, bf16[256,512]{1,0:T(8,128)(2,1)S(1)}, u32[]{:S(2)}, u32[]{:S(2)}) collective-permute-start(bf16[256,512]{1,0:T(8,128)(2,1)S(1)} %get-tuple-element.39), channel_id=1, source_target_pairs={{0,112},{16,0},{32,16},{48,32},{64,48},{80,64},{96,80},{112,96},{1... | collective-permute-start | bytes 786440 | tf_op jit(solution)/shard_map/ppermute | solution.py:52
  58.2 3.1 %shard_map.110.refs_4_ = f32[1280,512]{1,0:T(8,128)S(1)} custom-call(bf16[640,8192]{1,0:T(8,128)(2,1)S(1)} %shard_map.103.refs_3_.own, bf16[640,8192]{1,0:T(8,128)(2,1)S(1)} %shard_map.104.refs_4_.sib, bf16[512,512]{1,0:T(8,128)(2,1)S(1)} %get-tuple-element.38.refs_0_, ...), custom_call_target="tpu_custom_call", output_to_operand_aliasing={{}: (6, {})} | custom-call | flops 2684354560 | bytes 2097152 | tf_op jit(solution)/shard_map/pallas_call | solution.py:242
  61.3 0.8 collective-permute-done.13.refs_1_
  62.1 1.4 collective-permute-done.12.refs_0_
  63.5 0.3 collective-permute-done.14.refs_2_
  63.8 0.9 collective-permute-start.16
  64.7 2.4 %collective-permute-start.17 = (bf16[256,512]{1,0:T(8,128)(2,1)S(1)}, bf16[256,512]{1,0:T(8,128)(2,1)S(1)}, u32[]{:S(2)}, u32[]{:S(2)}) collective-permute-start(bf16[256,512]{1,0:T(8,128)(2,1)S(1)} %get-tuple-element.44.refs_1_), channel_id=1, source_target_pairs={{0,2},{2,4},{4,6},{6,0},{1,3},{3,5},{5,7},{7,1},{8,10},{10,12},{12... | collective-permute-start | bytes 786440 | tf_op jit(solution)/shard_map/ppermute | solution.py:52
  67.1 1.0 collective-permute-start.18
  68.2 3.7 %collective-permute-start.19 = (bf16[256,512]{1,0:T(8,128)(2,1)S(1)}, bf16[256,512]{1,0:T(8,128)(2,1)S(1)}, u32[]{:S(2)}, u32[]{:S(2)}) collective-permute-start(bf16[256,512]{1,0:T(8,128)(2,1)S(1)} %get-tuple-element.45), channel_id=1, source_target_pairs={{0,130},{2,132},{4,134},{6,128},{128,2},{130,4},{132,6},{134,0},{1... | collective-permute-start | bytes 786440 | tf_op jit(solution)/shard_map/ppermute | solution.py:52
  71.8 2.7 %shard_map.112.refs_4_ = f32[1280,512]{1,0:T(8,128)S(1)} custom-call(bf16[640,8192]{1,0:T(8,128)(2,1)S(1)} %shard_map.103.refs_3_.own, bf16[640,8192]{1,0:T(8,128)(2,1)S(1)} %shard_map.104.refs_4_.sib, bf16[512,512]{1,0:T(8,128)(2,1)S(1)} %get-tuple-element.43.refs_0_, ...), custom_call_target="tpu_custom_call", output_to_operand_aliasing={{}: (6, {})} | custom-call | flops 2348810240 | bytes 1835008 | tf_op jit(solution)/shard_map/pallas_call | solution.py:242
  74.6 4.0 %collective-permute-done.18.refs_2_ = bf16[256,512]{1,0:T(8,128)(2,1)S(1)} collective-permute-done((bf16[256,512]{1,0:T(8,128)(2,1)S(1)}, bf16[256,512]{1,0:T(8,128)(2,1)S(1)}, u32[]{:S(2)}, u32[]{:S(2)}) %collective-permute-start.18) | collective-permute-done | bytes 262176 | tf_op jit(solution)/shard_map/ppermute | solution.py:52
  78.6 2.7 %shard_map.113 = (f32[1280,512]{1,0:T(8,128)S(1)}, f32[64,1,512]{2,1,0:T(1,128)S(1)}) custom-call(bf16[640,8192]{1,0:T(8,128)(2,1)S(1)} %shard_map.103.refs_3_.own, bf16[640,8192]{1,0:T(8,128)(2,1)S(1)} %shard_map.104.refs_4_.sib, bf16[512,512]{1,0:T(8,128)(2,1)S(1)} %collective-permute-done.16.refs_0_, ...), custom_call_target="tpu_custom_call" | custom-call | flops 1677721600 | bytes 1310720 | tf_op jit(solution)/shard_map/pallas_call | solution.py:242
  81.3 20.6 %all_to_all.15.squares = f32[64,1,512]{2,1,0:T(1,128)S(1)} all-to-all(f32[64,1,512]{2,1,0:T(1,128)S(1)} %get-tuple-element.49), channel_id=1, replica_groups=mesh['yh'=2,'z'=8,'tp'=2,'x'=4,'core'=2] {'yh','z','x'}, dimensions={0} | all-to-all | bytes 262144 | tf_op jit(solution)/shard_map/all_to_all | solution.py:508
  101.9 1.1 shard_map.114
  103.0 2.5 %collective-permute-start.20 = (bf16[1280,128]{1,0:T(8,128)(2,1)S(1)}, bf16[1280,128]{1,0:T(8,128)(2,1)S(1)}, u32[]{:S(2)}, u32[]{:S(2)}) collective-permute-start(bf16[1280,128]{1,0:T(8,128)(2,1)S(1)} %get-tuple-element.50), channel_id=1, source_target_pairs={{0,0},{2,2},{4,12},{6,14},{8,4},{10,6},{12,8},{14,10},{1,1},{3,3},... | collective-permute-start | bytes 983048 | tf_op jit(solution)/shard_map/ppermute | solution.py:517
  105.6 3.2 %collective-permute-start.21 = (bf16[1280,128]{1,0:T(8,128)(2,1)S(1)}, bf16[1280,128]{1,0:T(8,128)(2,1)S(1)}, u32[]{:S(2)}, u32[]{:S(2)}) collective-permute-start(bf16[1280,128]{1,0:T(8,128)(2,1)S(1)} %get-tuple-element.51), channel_id=1, source_target_pairs={{0,2},{2,4},{4,14},{6,8},{8,6},{10,0},{12,10},{14,12},{1,3},{3,5},... | collective-permute-start | bytes 983048 | tf_op jit(solution)/shard_map/ppermute | solution.py:517
  108.8 2.6 %collective-permute-start.22 = (bf16[1280,128]{1,0:T(8,128)(2,1)S(1)}, bf16[1280,128]{1,0:T(8,128)(2,1)S(1)}, u32[]{:S(2)}, u32[]{:S(2)}) collective-permute-start(bf16[1280,128]{1,0:T(8,128)(2,1)S(1)} %get-tuple-element.52), channel_id=1, source_target_pairs={{0,4},{2,6},{4,8},{6,10},{8,0},{10,2},{12,12},{14,14},{1,5},{3,7},... | collective-permute-start | bytes 983048 | tf_op jit(solution)/shard_map/ppermute | solution.py:517
  111.4 0.9 collective-permute-start.24
  112.5 2.9 %collective-permute-done.24.other_scale = f32[1,512]{1,0:T(1,128)S(1)} collective-permute-done((f32[1,512]{1,0:T(1,128)S(1)}, f32[1,512]{1,0:T(1,128)S(1)}, u32[]{:S(2)}, u32[]{:S(2)}) %collective-permute-start.24) | collective-permute-done | bytes 2080 | tf_op jit(solution)/shard_map/ppermute | solution.py:52
  115.3 2.6 %collective-permute-done.21.r1 = bf16[1280,128]{1,0:T(8,128)(2,1)S(1)} collective-permute-done((bf16[1280,128]{1,0:T(8,128)(2,1)S(1)}, bf16[1280,128]{1,0:T(8,128)(2,1)S(1)}, u32[]{:S(2)}, u32[]{:S(2)}) %collective-permute-start.21) | collective-permute-done | bytes 327712 | tf_op jit(solution)/shard_map/ppermute | solution.py:517
  117.9 1.4 collective-permute-done.22.r2
  119.4 3.4 %collective-permute-done.23.r3 = bf16[1280,128]{1,0:T(8,128)(2,1)S(1)} collective-permute-done((bf16[1280,128]{1,0:T(8,128)(2,1)S(1)}, bf16[1280,128]{1,0:T(8,128)(2,1)S(1)}, u32[]{:S(2)}, u32[]{:S(2)}) %collective-permute-start.23) | collective-permute-done | bytes 327712 | tf_op jit(solution)/shard_map/ppermute | solution.py:517
  122.8 4.1 %shard_map.115 = (bf16[2,10,256,128]{3,2,1,0:T(8,128)(2,1)}, f32[16,40,128]{2,1,0:T(8,128)S(1)}) custom-call(s32[10]{0:T(128)S(1)} %copy-done.5, bf16[1280,128]{1,0:T(8,128)(2,1)S(1)} %collective-permute-done.20.r0, bf16[1280,128]{1,0:T(8,128)(2,1)S(1)} %collective-permute-done.21.r1, bf16[1280,128]{1,0:T(8,128)(2,1)S(1)} %collective-permute-done.22.r2, ...), custom_call_target="tpu_custom_call" | custom-call | flops 671088640 | bytes 2621440 | tf_op jit(solution)/shard_map/pallas_call | solution.py:358
  126.9 14.0 %all_to_all.16.parts = f32[16,40,128]{2,1,0:T(8,128)S(1)} all-to-all(f32[16,40,128]{2,1,0:T(8,128)S(1)} %get-tuple-element.56), channel_id=1, replica_groups=mesh['yh'=2,'z'=8,'tp'=2,'x'=4,'core'=2] {'z','tp'}, dimensions={0} | all-to-all | bytes 655360 | tf_op jit(solution)/shard_map/all_to_all | solution.py:526
  140.9 1.1 shard_map.116
  141.9 3.9 %all-to-all-start.2 = ((bf16[32,32,128]{2,1,0:T(8,128)(2,1)}), bf16[32,32,128]{2,1,0:T(8,128)(2,1)S(1)}, u32[]{:S(2)}, u32[]{:S(2)}) async-start(bf16[32,32,128]{2,1,0:T(8,128)(2,1)} %shard_map.116), calls=%async_computation.2 | async-start | bytes 524288 | tf_op jit(solution)/shard_map/all_to_all | solution.py:528
  145.9 1.2 collective-permute-done.25.far
  147.1 11.1 %all-to-all-done.2.whole = bf16[32,32,128]{2,1,0:T(8,128)(2,1)S(1)} async-done(((bf16[32,32,128]{2,1,0:T(8,128)(2,1)}), bf16[32,32,128]{2,1,0:T(8,128)(2,1)S(1)}, u32[]{:S(2)}, u32[]{:S(2)}) %all-to-all-start.2) | async-done | bytes 262176 | tf_op jit(solution)/shard_map/all_to_all | solution.py:528
  158.2 0.8 shard_map.117
  (39 shorter events, 1.1 us)
Async XLA Ops:
  0.6 24.0 %collective-permute-start = (bf16[640,8192]{1,0:T(8,128)(2,1)}, bf16[640,8192]{1,0:T(8,128)(2,1)S(1)}, u32[]{:S(2)}, u32[]{:S(2)}) collective-permute-start(bf16[640,8192]{1,0:T(8,128)(2,1)} %source.1), channel_id=1, source_target_pairs={{0,1},{1,0},{2,3},{3,2},{4,5},{5,4},{6,7},{7,6},{8,9},{9,8},{10,11... | collective-permute-start | bytes 31457288 | tf_op jit(solution)/shard_map/ppermute | solution.py:52
  0.7 1.2 copy-start
  2.1 13.1 %collective-permute-start.1 = (bf16[256,512]{1,0:T(8,128)(2,1)S(1)}, bf16[256,512]{1,0:T(8,128)(2,1)S(1)}, u32[]{:S(2)}, u32[]{:S(2)}) collective-permute-start(bf16[256,512]{1,0:T(8,128)(2,1)S(1)} %shard_map.105), channel_id=1, source_target_pairs={{0,128},{128,0},{1,129},{129,1},{2,130},{130,2},{3,131},{131,3},{4... | collective-permute-start | bytes 786440 | tf_op jit(solution)/shard_map/ppermute | solution.py:52
  5.4 12.5 %collective-permute-start.2 = (bf16[256,512]{1,0:T(8,128)(2,1)S(1)}, bf16[256,512]{1,0:T(8,128)(2,1)S(1)}, u32[]{:S(2)}, u32[]{:S(2)}) collective-permute-start(bf16[256,512]{1,0:T(8,128)(2,1)S(1)} %shard_map.105), channel_id=1, source_target_pairs={{0,16},{16,32},{32,48},{48,64},{64,80},{80,96},{96,112},{112,0},{1... | collective-permute-start | bytes 786440 | tf_op jit(solution)/shard_map/ppermute | solution.py:52
  7.3 10.6 %collective-permute-start.3 = (bf16[256,512]{1,0:T(8,128)(2,1)S(1)}, bf16[256,512]{1,0:T(8,128)(2,1)S(1)}, u32[]{:S(2)}, u32[]{:S(2)}) collective-permute-start(bf16[256,512]{1,0:T(8,128)(2,1)S(1)} %shard_map.105), channel_id=1, source_target_pairs={{0,112},{16,0},{32,16},{48,32},{64,48},{80,64},{96,80},{112,96},{1... | collective-permute-start | bytes 786440 | tf_op jit(solution)/shard_map/ppermute | solution.py:52
  18.0 14.8 %collective-permute-start.4 = (bf16[512,512]{1,0:T(8,128)(2,1)S(1)}, bf16[512,512]{1,0:T(8,128)(2,1)S(1)}, u32[]{:S(2)}, u32[]{:S(2)}) collective-permute-start(bf16[512,512]{1,0:T(8,128)(2,1)S(1)} %get-tuple-element.31.refs_1_), channel_id=1, source_target_pairs={{0,16},{16,32},{32,48},{48,64},{64,80},{80,96},{96,112},{112,0},{1... | collective-permute-start | bytes 1572872 | tf_op jit(solution)/shard_map/ppermute | solution.py:52
  18.1 14.7 %collective-permute-start.5 = (bf16[512,512]{1,0:T(8,128)(2,1)S(1)}, bf16[512,512]{1,0:T(8,128)(2,1)S(1)}, u32[]{:S(2)}, u32[]{:S(2)}) collective-permute-start(bf16[512,512]{1,0:T(8,128)(2,1)S(1)} %get-tuple-element.32), channel_id=1, source_target_pairs={{0,112},{16,0},{32,16},{48,32},{64,48},{80,64},{96,80},{112,96},{1... | collective-permute-start | bytes 1572872 | tf_op jit(solution)/shard_map/ppermute | solution.py:52
  21.3 14.2 %collective-permute-start.6 = (bf16[512,512]{1,0:T(8,128)(2,1)S(1)}, bf16[512,512]{1,0:T(8,128)(2,1)S(1)}, u32[]{:S(2)}, u32[]{:S(2)}) collective-permute-start(bf16[512,512]{1,0:T(8,128)(2,1)S(1)} %get-tuple-element.31.refs_1_), channel_id=1, source_target_pairs={{0,6},{2,0},{4,2},{6,4},{1,7},{3,1},{5,3},{7,5},{8,14},{10,8},{12,... | collective-permute-start | bytes 1572872 | tf_op jit(solution)/shard_map/ppermute | solution.py:52
  22.2 7.1 %collective-permute-start.7 = (bf16[256,512]{1,0:T(8,128)(2,1)S(1)}, bf16[256,512]{1,0:T(8,128)(2,1)S(1)}, u32[]{:S(2)}, u32[]{:S(2)}) collective-permute-start(bf16[256,512]{1,0:T(8,128)(2,1)S(1)} %get-tuple-element.33.refs_2_), channel_id=1, source_target_pairs={{0,2},{2,4},{4,6},{6,0},{1,3},{3,5},{5,7},{7,1},{8,10},{10,12},{12... | collective-permute-start | bytes 786440 | tf_op jit(solution)/shard_map/ppermute | solution.py:52
  35.6 13.4 %collective-permute-start.8 = (bf16[512,512]{1,0:T(8,128)(2,1)S(1)}, bf16[512,512]{1,0:T(8,128)(2,1)S(1)}, u32[]{:S(2)}, u32[]{:S(2)}) collective-permute-start(bf16[512,512]{1,0:T(8,128)(2,1)S(1)} %get-tuple-element.34.refs_5_), channel_id=1, source_target_pairs={{0,16},{16,32},{32,48},{48,64},{64,80},{80,96},{96,112},{112,0},{1... | collective-permute-start | bytes 1572872 | tf_op jit(solution)/shard_map/ppermute | solution.py:52
  35.6 13.3 %collective-permute-start.9 = (bf16[512,512]{1,0:T(8,128)(2,1)S(1)}, bf16[512,512]{1,0:T(8,128)(2,1)S(1)}, u32[]{:S(2)}, u32[]{:S(2)}) collective-permute-start(bf16[512,512]{1,0:T(8,128)(2,1)S(1)} %get-tuple-element.35.refs_6_), channel_id=1, source_target_pairs={{0,112},{16,0},{32,16},{48,32},{64,48},{80,64},{96,80},{112,96},{1... | collective-permute-start | bytes 1572872 | tf_op jit(solution)/shard_map/ppermute | solution.py:52
  38.9 12.7 %collective-permute-start.10 = (bf16[512,512]{1,0:T(8,128)(2,1)S(1)}, bf16[512,512]{1,0:T(8,128)(2,1)S(1)}, u32[]{:S(2)}, u32[]{:S(2)}) collective-permute-start(bf16[512,512]{1,0:T(8,128)(2,1)S(1)} %get-tuple-element.34.refs_5_), channel_id=1, source_target_pairs={{0,6},{2,0},{4,2},{6,4},{1,7},{3,1},{5,3},{7,5},{8,14},{10,8},{12,... | collective-permute-start | bytes 1572872 | tf_op jit(solution)/shard_map/ppermute | solution.py:52
  38.9 12.7 %collective-permute-start.11 = (bf16[512,512]{1,0:T(8,128)(2,1)S(1)}, bf16[512,512]{1,0:T(8,128)(2,1)S(1)}, u32[]{:S(2)}, u32[]{:S(2)}) collective-permute-start(bf16[512,512]{1,0:T(8,128)(2,1)S(1)} %get-tuple-element.35.refs_6_), channel_id=1, source_target_pairs={{0,2},{2,4},{4,6},{6,0},{1,3},{3,5},{5,7},{7,1},{8,10},{10,12},{12... | collective-permute-start | bytes 1572872 | tf_op jit(solution)/shard_map/ppermute | solution.py:52
  51.6 11.9 %collective-permute-start.12 = (bf16[512,512]{1,0:T(8,128)(2,1)S(1)}, bf16[512,512]{1,0:T(8,128)(2,1)S(1)}, u32[]{:S(2)}, u32[]{:S(2)}) collective-permute-start(bf16[512,512]{1,0:T(8,128)(2,1)S(1)} %get-tuple-element.38.refs_0_), channel_id=1, source_target_pairs={{0,16},{16,32},{32,48},{48,64},{64,80},{80,96},{96,112},{112,0},{1... | collective-permute-start | bytes 1572872 | tf_op jit(solution)/shard_map/ppermute | solution.py:52
  51.7 12.0 %collective-permute-start.14 = (bf16[512,512]{1,0:T(8,128)(2,1)S(1)}, bf16[512,512]{1,0:T(8,128)(2,1)S(1)}, u32[]{:S(2)}, u32[]{:S(2)}) collective-permute-start(bf16[512,512]{1,0:T(8,128)(2,1)S(1)} %get-tuple-element.38.refs_0_), channel_id=1, source_target_pairs={{0,6},{2,0},{4,2},{6,4},{1,7},{3,1},{5,3},{7,5},{8,14},{10,8},{12,... | collective-permute-start | bytes 1572872 | tf_op jit(solution)/shard_map/ppermute | solution.py:52
  51.8 12.0 %collective-permute-start.15 = (bf16[512,512]{1,0:T(8,128)(2,1)S(1)}, bf16[512,512]{1,0:T(8,128)(2,1)S(1)}, u32[]{:S(2)}, u32[]{:S(2)}) collective-permute-start(bf16[512,512]{1,0:T(8,128)(2,1)S(1)} %get-tuple-element.40.refs_1_), channel_id=1, source_target_pairs={{0,2},{2,4},{4,6},{6,0},{1,3},{3,5},{5,7},{7,1},{8,10},{10,12},{12... | collective-permute-start | bytes 1572872 | tf_op jit(solution)/shard_map/ppermute | solution.py:52
  55.0 7.0 %collective-permute-start.13 = (bf16[256,512]{1,0:T(8,128)(2,1)S(1)}, bf16[256,512]{1,0:T(8,128)(2,1)S(1)}, u32[]{:S(2)}, u32[]{:S(2)}) collective-permute-start(bf16[256,512]{1,0:T(8,128)(2,1)S(1)} %get-tuple-element.39), channel_id=1, source_target_pairs={{0,112},{16,0},{32,16},{48,32},{64,48},{80,64},{96,80},{112,96},{1... | collective-permute-start | bytes 786440 | tf_op jit(solution)/shard_map/ppermute | solution.py:52
  63.8 14.8 %collective-permute-start.16 = (bf16[512,512]{1,0:T(8,128)(2,1)S(1)}, bf16[512,512]{1,0:T(8,128)(2,1)S(1)}, u32[]{:S(2)}, u32[]{:S(2)}) collective-permute-start(bf16[512,512]{1,0:T(8,128)(2,1)S(1)} %get-tuple-element.43.refs_0_), channel_id=1, source_target_pairs={{0,6},{2,0},{4,2},{6,4},{1,7},{3,1},{5,3},{7,5},{8,14},{10,8},{12,... | collective-permute-start | bytes 1572872 | tf_op jit(solution)/shard_map/ppermute | solution.py:52
  64.7 9.8 %collective-permute-start.17 = (bf16[256,512]{1,0:T(8,128)(2,1)S(1)}, bf16[256,512]{1,0:T(8,128)(2,1)S(1)}, u32[]{:S(2)}, u32[]{:S(2)}) collective-permute-start(bf16[256,512]{1,0:T(8,128)(2,1)S(1)} %get-tuple-element.44.refs_1_), channel_id=1, source_target_pairs={{0,2},{2,4},{4,6},{6,0},{1,3},{3,5},{5,7},{7,1},{8,10},{10,12},{12... | collective-permute-start | bytes 786440 | tf_op jit(solution)/shard_map/ppermute | solution.py:52
  67.1 11.5 %collective-permute-start.18 = (bf16[256,512]{1,0:T(8,128)(2,1)S(1)}, bf16[256,512]{1,0:T(8,128)(2,1)S(1)}, u32[]{:S(2)}, u32[]{:S(2)}) collective-permute-start(bf16[256,512]{1,0:T(8,128)(2,1)S(1)} %get-tuple-element.45), channel_id=1, source_target_pairs={{0,128},{128,0},{1,129},{129,1},{2,130},{130,2},{3,131},{131,3},{4... | collective-permute-start | bytes 786440 | tf_op jit(solution)/shard_map/ppermute | solution.py:52
  68.2 10.4 %collective-permute-start.19 = (bf16[256,512]{1,0:T(8,128)(2,1)S(1)}, bf16[256,512]{1,0:T(8,128)(2,1)S(1)}, u32[]{:S(2)}, u32[]{:S(2)}) collective-permute-start(bf16[256,512]{1,0:T(8,128)(2,1)S(1)} %get-tuple-element.45), channel_id=1, source_target_pairs={{0,130},{2,132},{4,134},{6,128},{128,2},{130,4},{132,6},{134,0},{1... | collective-permute-start | bytes 786440 | tf_op jit(solution)/shard_map/ppermute | solution.py:52
  71.8 6.8 %copy-start.4 = (s32[2]{0:T(128)S(1)}, s32[2]{0:T(128)}, u32[]{:S(2)}) copy-start(s32[2]{0:T(128)} %lengths.1) | copy-start | bytes 28
  81.3 31.0 %copy-start.6 = (s32[2,64]{1,0:T(2,128)S(1)}, s32[2,64]{1,0:T(2,128)}, u32[]{:S(2)}) copy-start(s32[2,64]{1,0:T(2,128)} %param.15) | copy-start | bytes 1540
  81.3 41.5 %copy-start.1 = (bf16[2,64,1024]{2,1,0:T(8,128)(2,1)S(1)}, bf16[2,64,1024]{2,1,0:T(8,128)(2,1)}, u32[]{:S(2)}) copy-start(bf16[2,64,1024]{2,1,0:T(8,128)(2,1)} %query.3) | copy-start | bytes 786436
  81.3 41.5 %copy-start.5 = (s32[10]{0:T(128)S(1)}, s32[10]{0:T(128)}, u32[]{:S(2)}) copy-start(s32[10]{0:T(128)} %pages.1) | copy-start | bytes 124
  101.9 38.9 %copy-start.2 = (bf16[2,64,128]{2,1,0:T(8,128)(2,1)S(1)}, bf16[2,64,128]{2,1,0:T(8,128)(2,1)}, u32[]{:S(2)}) copy-start(bf16[2,64,128]{2,1,0:T(8,128)(2,1)} %new_key.1) | copy-start | bytes 98308
  101.9 38.9 %copy-start.3 = (bf16[2,64,128]{2,1,0:T(8,128)(2,1)S(1)}, bf16[2,64,128]{2,1,0:T(8,128)(2,1)}, u32[]{:S(2)}) copy-start(bf16[2,64,128]{2,1,0:T(8,128)(2,1)} %new_value.1) | copy-start | bytes 98308
  103.0 12.3 %collective-permute-start.20 = (bf16[1280,128]{1,0:T(8,128)(2,1)S(1)}, bf16[1280,128]{1,0:T(8,128)(2,1)S(1)}, u32[]{:S(2)}, u32[]{:S(2)}) collective-permute-start(bf16[1280,128]{1,0:T(8,128)(2,1)S(1)} %get-tuple-element.50), channel_id=1, source_target_pairs={{0,0},{2,2},{4,12},{6,14},{8,4},{10,6},{12,8},{14,10},{1,1},{3,3},... | collective-permute-start | bytes 983048 | tf_op jit(solution)/shard_map/ppermute | solution.py:517
  105.6 12.4 %collective-permute-start.21 = (bf16[1280,128]{1,0:T(8,128)(2,1)S(1)}, bf16[1280,128]{1,0:T(8,128)(2,1)S(1)}, u32[]{:S(2)}, u32[]{:S(2)}) collective-permute-start(bf16[1280,128]{1,0:T(8,128)(2,1)S(1)} %get-tuple-element.51), channel_id=1, source_target_pairs={{0,2},{2,4},{4,14},{6,8},{8,6},{10,0},{12,10},{14,12},{1,3},{3,5},... | collective-permute-start | bytes 983048 | tf_op jit(solution)/shard_map/ppermute | solution.py:517
  108.8 10.6 %collective-permute-start.22 = (bf16[1280,128]{1,0:T(8,128)(2,1)S(1)}, bf16[1280,128]{1,0:T(8,128)(2,1)S(1)}, u32[]{:S(2)}, u32[]{:S(2)}) collective-permute-start(bf16[1280,128]{1,0:T(8,128)(2,1)S(1)} %get-tuple-element.52), channel_id=1, source_target_pairs={{0,4},{2,6},{4,8},{6,10},{8,0},{10,2},{12,12},{14,14},{1,5},{3,7},... | collective-permute-start | bytes 983048 | tf_op jit(solution)/shard_map/ppermute | solution.py:517
  111.4 11.4 %collective-permute-start.23 = (bf16[1280,128]{1,0:T(8,128)(2,1)S(1)}, bf16[1280,128]{1,0:T(8,128)(2,1)S(1)}, u32[]{:S(2)}, u32[]{:S(2)}) collective-permute-start(bf16[1280,128]{1,0:T(8,128)(2,1)S(1)} %get-tuple-element.53), channel_id=1, source_target_pairs={{0,6},{2,0},{4,10},{6,12},{8,2},{10,4},{12,14},{14,8},{1,7},{3,1},... | collective-permute-start | bytes 983048 | tf_op jit(solution)/shard_map/ppermute | solution.py:517
  111.4 3.9 %collective-permute-start.24 = (f32[1,512]{1,0:T(1,128)S(1)}, f32[1,512]{1,0:T(1,128)S(1)}, u32[]{:S(2)}, u32[]{:S(2)}) collective-permute-start(f32[1,512]{1,0:T(1,128)S(1)} %get-tuple-element.54.own_scale), channel_id=1, source_target_pairs={{0,8},{8,0},{1,9},{9,1},{2,10},{10,2},{3,11},{11,3},{4,12},{12,4},... | collective-permute-start | bytes 6152 | tf_op jit(solution)/shard_map/ppermute | solution.py:52
  141.9 16.3 %all-to-all-start.2 = ((bf16[32,32,128]{2,1,0:T(8,128)(2,1)}), bf16[32,32,128]{2,1,0:T(8,128)(2,1)S(1)}, u32[]{:S(2)}, u32[]{:S(2)}) async-start(bf16[32,32,128]{2,1,0:T(8,128)(2,1)} %shard_map.116), calls=%async_computation.2 | async-start | bytes 524288 | tf_op jit(solution)/shard_map/all_to_all | solution.py:528
  145.8 1.3 collective-permute-start.25

commit v3 on v2

--- a/solution.py
+++ b/solution.py
@@ -21,6 +21,7 @@
 clip_level = 2.5
 masked_fill = -1e30
 inverse = 1.0 / (float(HD) ** 0.5)
+log2e = 1.4426950408889634
 
 SIZES = {"yh": 2, "z": 8, "tp": 2, "x": 4, "core": 2}
 ANYWHERE = pl.BlockSpec(memory_space=pl.ANY)
@@ -92,6 +93,25 @@
         compiler_params=params(SHARED),
         cost_estimate=cost(),
     )(*args, after)
+
+
+def picked_kernel(count, picks, *refs):
+    relay_kernel(count, picks, *refs[:count], None, *[None] * count, *refs[count:])
+
+
+def picked(values, picks):
+    return pl.pallas_call(
+        functools.partial(picked_kernel, len(values), picks),
+        in_specs=[ANYWHERE] * len(values),
+        out_specs=[ANYWHERE] * len(picks),
+        out_shape=[
+            pltpu.VMEM((sum(rows for _, _, rows in parts), values[0].shape[1]), values[0].dtype)
+            for parts in picks
+        ],
+        scratch_shapes=[pltpu.SemaphoreType.DMA((sum(len(p) for p in picks),))],
+        compiler_params=params(SHARED),
+        cost_estimate=cost(),
+    )(*in_vmem(values))
 
 
 def keep_kernel(source, target, sem):
@@ -207,7 +227,9 @@
         kept = jnp.where(place < limit, value * value, 0.0)
         part = part + jnp.sum(kept, axis=0, keepdims=True)
         outs[0][pl.ds(goes, TILE)] = value
-    squares[...] = jnp.broadcast_to(part[None], squares.shape)
+    for i in range(4):
+        lanes = part[None, :, i * HD : (i + 1) * HD]
+        squares[:, i : i + 1, :] = jnp.broadcast_to(lanes, (squares.shape[0], 1, HD))
 
 
 def project(own, sib, pieces, acc=None, lengths=None):
@@ -237,7 +259,7 @@
         in_specs.append(SCALAR)
         args.append(lengths)
         out_shape = [pltpu.VMEM((2 * rows, width), jnp.float32)]
-        out_shape.append(jax.ShapeDtypeStruct((64, 1, width), jnp.float32))
+        out_shape.append(jax.ShapeDtypeStruct((64, 4, HD), jnp.float32))
         scratch.insert(0, pltpu.VMEM((2 * rows, width), jnp.float32))
     return pl.pallas_call(
         functools.partial(project_kernel, names, acc is not None, last),
@@ -254,8 +276,9 @@
 def quantize_kernel(proj, squares, lengths, *outs):
     x, tp = lax.axis_index("x"), lax.axis_index("tp")
     count = (lengths[0] + lengths[1]).astype(jnp.float32)
-    scale = jnp.sqrt(jnp.sum(squares[:, 0, :], axis=0, keepdims=True) / count + eps)
-    outs[4][...] = scale
+    mean = jnp.sum(squares[...], axis=0) / count
+    for i in range(4):
+        outs[4][:, i * HD : (i + 1) * HD] = jnp.sqrt(mean[i : i + 1] + eps)
     for k in range(4):
         head = pl.ds(pl.multiple_of(((x + k + 2 * tp) % 4) * HD, HD), HD)
         value = proj[:, head] * (1.0 / outs[4][:, head])
@@ -310,7 +333,7 @@
     seen = pl.multiple_of(yh * 32, 32)
     limit = jnp.concatenate([limits[pl.ds(s * 64 + seen, 32)] for s in range(2)], axis=0)
     limit = jnp.concatenate([limit, limit], axis=0)
-    base = (z * 2 + tp) * 2 * rows
+    place = (z * 2 + tp) * 2 * rows + lax.broadcasted_iota(jnp.int32, (1, 2 * rows), 1)
     for pair in range(GROUP // 2):
         asked = [
             query[s, pl.ds(seen, 32), g * HD : (g + 1) * HD]
@@ -319,15 +342,13 @@
         ]
         asked = jnp.concatenate(asked, axis=0)
         scaled = (asked.astype(jnp.float32) * scales[0]).astype(jnp.bfloat16)
-        score = (
-            lax.dot_general(
-                scaled, keys, (((1,), (1,)), ((), ())), preferred_element_type=jnp.float32
-            )
-            * inverse
+        score = lax.dot_general(
+            scaled, keys, (((1,), (1,)), ((), ())), preferred_element_type=jnp.float32
         )
-        mask = base + lax.broadcasted_iota(jnp.int32, score.shape, 1) < limit
-        top = jnp.max(jnp.where(mask, score, masked_fill), axis=1, keepdims=True)
-        weight = jnp.where(mask, jnp.exp(score - top), 0.0)
+        score = jnp.where(place < limit, score, masked_fill)
+        top = jnp.max(score, axis=1, keepdims=True)
+        weight = jnp.exp2((score - top) * (inverse * log2e))
+        top = top * inverse
         total = jnp.sum(weight, axis=1, keepdims=True)
         summed = jnp.dot(weight.astype(jnp.bfloat16), values, preferred_element_type=jnp.float32)
         for side in range(2):
@@ -480,32 +501,37 @@
     wave = [(kv_weight, None), (both_up, at(-1)), (down, near(1))]
 
     over, under = send(both_up, x=-1), send(down, x=1)
-    up, down = send(both_up, z=1), send(both_down, z=-1)
+    next_up, next_down = send(both_up, z=1), send(both_down, z=-1)
     sib = keep(sibling)
-    up, down, over, under = relay([up, down, over, under], sib)
+    up, down, last = relay([next_up, next_down], sib, [[part(0)]])
     wave += [(over, swapped(at(-1))), (under, swapped(near(1))), (up, at(-2)), (down, at(2))]
-
-    over, under = send(up, x=-1), send(down, x=1)
+    (over,) = picked([over], [[part(0)]])
+
+    side, over, under = send(over, yh=1), send(last, x=-1), send(down, x=1)
     next_up, next_down = send(up, z=1), send(down, z=-1)
     acc = project(own, sib, wave)[0]
-    up, down, over, under, last = relay(
-        [next_up, next_down, over, under], acc, [[(1, PIECE, PIECE)]]
-    )
-    wave = [(up, at(-3)), (down, at(3)), (over, swapped(at(-2))), (under, swapped(at(2)))]
-
-    over, under = send(up, x=-1), send(down, x=1)
-    next_up, next_down = send(up, z=1), send(last, z=-1)
+    up, down, last, next_last = relay(
+        [next_up, next_down], acc, [[part(0)], [(1, PIECE, PIECE)]]
+    )
+    wave = [(up, at(-3)), (down, at(3)), (over, swapped(near(-2))), (under, swapped(at(2)))]
+    wave += [(side, swapped(far(-1)))]
+
+    side, over, under = send(over, yh=1), send(last, x=-1), send(down, x=1)
+    next_up, next_down = send(up, z=1), send(next_last, z=-1)
     acc = project(own, sib, wave, acc)[0]
-    up, down, over, under, last = relay([next_up, next_down, over, under], acc, [[part(0)]])
-    wave = [(up, at(-4)), (down, far(3)), (over, swapped(at(-3))), (under, swapped(at(3)))]
-
-    over, under = send(up, x=-1), send(down, x=1)
-    cross, corner = send(last, yh=1), send(last, yh=1, x=1)
+    up, down, last, next_last = relay(
+        [next_up, next_down], acc, [[part(0)], [(0, PIECE, PIECE)]]
+    )
+    wave = [(up, at(-4)), (down, far(3)), (over, swapped(near(-3))), (under, swapped(at(3)))]
+    wave += [(side, swapped(far(-2)))]
+
+    side, under, cross = send(over, yh=1), send(down, x=1), send(next_last, z=1)
+    corner, over = send(last, yh=1, x=-1), send(last, x=-1)
     acc = project(own, sib, wave, acc)[0]
-    wave = [(over, swapped(at(-4))), (under, swapped(far(3)))]
+    wave = [(over, swapped(near(-4))), (under, swapped(far(3))), (side, swapped(far(-3)))]
     wave += [(cross, far(-4)), (corner, swapped(far(-4)))]
     proj, squares = project(own, sib, wave, acc, lengths)
-    squares = lax.all_to_all(squares, ("yh", "z", "x"), 0, 0, tiled=True)
+    squares = lax.all_to_all(squares, ("x", "z", "yh"), 0, 0, tiled=True)
     *sent, scale = quantize(proj, squares, lengths)
 
     received = []

time: 159 us -> 155 us (0.975)
  waiting for transfers between devices: 47 us -> 44.9 us
    ppermute x22 -> x25, waiting for transfers between devices: 28.4 us -> 24.9 us  [send(): return lax.ppermute(value, names if len(names) > 1 else names[0], pairs)]
    ppermute x22 -> x25, starting transfers between devices: 37.8 us -> 36.3 us  [send(): return lax.ppermute(value, names if len(names) > 1 else names[0], pairs)]
  transfers between devices with their start and end apart: 27 -> 30, of which waited for: 16 -> 14; matrix products, arithmetic and copies ran while one was open for 0% -> 0% of each run, Pallas kernels for 10% -> 10%
where the time goes in v3:
time: 155 us
  starting transfers between devices  48.8 us (31%)
  waiting for transfers between devices  44.9 us (29%)
  blocking collectives  34.2 us (22%)
  Pallas kernels  24.8 us (16%)
    ppermute x25, starting transfers between devices, send(): return lax.ppermute(value, names if len(names) > 1 else names[0], pairs)  36.3 us
    ppermute x25, waiting for transfers between devices, send(): return lax.ppermute(value, names if len(names) > 1 else names[0], pairs)  24.9 us
    all_to_all x1, blocking collectives, body(): squares = lax.all_to_all(squares, ('x', 'z', 'yh'), 0, 0, tiled=True)  19.9 us
    all_to_all x1, blocking collectives, body(): parts = lax.all_to_all(part, ('z', 'tp'), 0, 0, tiled=True)  14.3 us
    pallas_call x4, Pallas kernels, project(): pl.pallas_call(functools.partial(project_kernel, names, acc is not None,...  13 us
    all_to_all x1, waiting for transfers between devices, body(): whole = lax.all_to_all(result, ('yh', 'z', 'tp'), 0, 0, tiled=True)  11.1 us
    ppermute x4, waiting for transfers between devices, body(): received.append(lax.ppermute(sent[k], ('tp', 'x'), pairs))  8.84 us
    ppermute x4, starting transfers between devices, body(): received.append(lax.ppermute(sent[k], ('tp', 'x'), pairs))  8.62 us
  transfers between devices with their start and end apart: 30, of which 14 were waited for; matrix products, arithmetic and copies ran while one was open for 0% of the time, Pallas kernels for 10%

profile of v3, /device:TPU:6, one launch (start us, length us, event | category | flops | bytes accessed | tf_op | source)
XLA Modules:
  0.0 155.0 jit_solution(17168735513167147161)
XLA Ops:
  0.7 1.2 copy-done
  2.1 3.3 %collective-permute-start.1 = (bf16[256,512]{1,0:T(8,128)(2,1)S(1)}, bf16[256,512]{1,0:T(8,128)(2,1)S(1)}, u32[]{:S(2)}, u32[]{:S(2)}) collective-permute-start(bf16[256,512]{1,0:T(8,128)(2,1)S(1)} %shard_map.105), channel_id=1, source_target_pairs={{0,128},{128,0},{1,129},{129,1},{2,130},{130,2},{3,131},{131,3},{4... | collective-permute-start | bytes 786440 | tf_op jit(solution)/shard_map/ppermute | solution.py:53
  5.4 1.9 %collective-permute-start.2 = (bf16[256,512]{1,0:T(8,128)(2,1)S(1)}, bf16[256,512]{1,0:T(8,128)(2,1)S(1)}, u32[]{:S(2)}, u32[]{:S(2)}) collective-permute-start(bf16[256,512]{1,0:T(8,128)(2,1)S(1)} %shard_map.105), channel_id=1, source_target_pairs={{0,16},{16,32},{32,48},{48,64},{64,80},{80,96},{96,112},{112,0},{1... | collective-permute-start | bytes 786440 | tf_op jit(solution)/shard_map/ppermute | solution.py:53
  7.3 3.9 %collective-permute-start.3 = (bf16[256,512]{1,0:T(8,128)(2,1)S(1)}, bf16[256,512]{1,0:T(8,128)(2,1)S(1)}, u32[]{:S(2)}, u32[]{:S(2)}) collective-permute-start(bf16[256,512]{1,0:T(8,128)(2,1)S(1)} %shard_map.105), channel_id=1, source_target_pairs={{0,112},{16,0},{32,16},{48,32},{64,48},{80,64},{96,80},{112,96},{1... | collective-permute-start | bytes 786440 | tf_op jit(solution)/shard_map/ppermute | solution.py:53
  11.2 4.0 %shard_map.103.refs_3_.own = bf16[640,8192]{1,0:T(8,128)(2,1)S(1)} custom-call(bf16[640,8192]{1,0:T(8,128)(2,1)} %source.1), custom_call_target="tpu_custom_call" | custom-call | bytes 20971520 | tf_op jit(solution)/shard_map/pallas_call | solution.py:124
  15.2 2.7 %collective-permute-done.2.refs_1_ = bf16[256,512]{1,0:T(8,128)(2,1)S(1)} collective-permute-done((bf16[256,512]{1,0:T(8,128)(2,1)S(1)}, bf16[256,512]{1,0:T(8,128)(2,1)S(1)}, u32[]{:S(2)}, u32[]{:S(2)}) %collective-permute-start.2) | collective-permute-done | bytes 262176 | tf_op jit(solution)/shard_map/ppermute | solution.py:53
  18.1 3.2 %collective-permute-start.5 = (bf16[512,512]{1,0:T(8,128)(2,1)S(1)}, bf16[512,512]{1,0:T(8,128)(2,1)S(1)}, u32[]{:S(2)}, u32[]{:S(2)}) collective-permute-start(bf16[512,512]{1,0:T(8,128)(2,1)S(1)} %get-tuple-element.29), channel_id=1, source_target_pairs={{0,112},{16,0},{32,16},{48,32},{64,48},{80,64},{96,80},{112,96},{1... | collective-permute-start | bytes 1572872 | tf_op jit(solution)/shard_map/ppermute | solution.py:53
  21.3 0.8 collective-permute-start.8
  22.2 2.4 %collective-permute-start.9 = (bf16[256,512]{1,0:T(8,128)(2,1)S(1)}, bf16[256,512]{1,0:T(8,128)(2,1)S(1)}, u32[]{:S(2)}, u32[]{:S(2)}) collective-permute-start(bf16[256,512]{1,0:T(8,128)(2,1)S(1)} %get-tuple-element.32.refs_2_), channel_id=1, source_target_pairs={{0,2},{2,4},{4,6},{6,0},{1,3},{3,5},{5,7},{7,1},{8,10},{10,12},{12... | collective-permute-start | bytes 786440 | tf_op jit(solution)/shard_map/ppermute | solution.py:53
  24.6 0.7 shard_map.104.refs_2_.sib
  25.3 7.5 %collective-permute-done.4.refs_0_ = bf16[512,512]{1,0:T(8,128)(2,1)S(1)} collective-permute-done((bf16[512,512]{1,0:T(8,128)(2,1)S(1)}, bf16[512,512]{1,0:T(8,128)(2,1)S(1)}, u32[]{:S(2)}, u32[]{:S(2)}) %collective-permute-start.4) | collective-permute-done | bytes 524320 | tf_op jit(solution)/shard_map/ppermute | solution.py:53
  32.9 1.9 %collective-permute-start.6 = (bf16[512,512]{1,0:T(8,128)(2,1)S(1)}, bf16[512,512]{1,0:T(8,128)(2,1)S(1)}, u32[]{:S(2)}, u32[]{:S(2)}) collective-permute-start(bf16[512,512]{1,0:T(8,128)(2,1)S(1)} %get-tuple-element.30.refs_5_), channel_id=1, source_target_pairs={{0,16},{16,32},{32,48},{48,64},{64,80},{80,96},{96,112},{112,0},{1... | collective-permute-start | bytes 1572872 | tf_op jit(solution)/shard_map/ppermute | solution.py:53
  34.8 1.4 collective-permute-start.7
  36.2 0.7 collective-permute-start.14
  37.4 1.5 collective-permute-start.12
  38.9 4.5 %shard_map.108.refs_2_.refs_5_ = f32[1280,512]{1,0:T(8,128)S(1)} custom-call(bf16[640,8192]{1,0:T(8,128)(2,1)S(1)} %shard_map.103.refs_3_.own, bf16[640,8192]{1,0:T(8,128)(2,1)S(1)} %shard_map.104.refs_2_.sib, bf16[512,1024]{1,0:T(8,128)(2,1)S(1)} %copy-done.1, bf16[512,512]{1,0:T(8,128)(2,1)S(1)} %get-tuple-element.28.refs_1_, ...), custom_call_target="tpu_custom_call" | custom-call | flops 4026531840 | bytes 3145728 | tf_op jit(solution)/shard_map/pallas_call | solution.py:264
  43.5 3.4 %collective-permute-done.6.refs_0_ = bf16[512,512]{1,0:T(8,128)(2,1)S(1)} collective-permute-done((bf16[512,512]{1,0:T(8,128)(2,1)S(1)}, bf16[512,512]{1,0:T(8,128)(2,1)S(1)}, u32[]{:S(2)}, u32[]{:S(2)}) %collective-permute-start.6) | collective-permute-done | bytes 524320 | tf_op jit(solution)/shard_map/ppermute | solution.py:53
  46.9 1.6 %collective-permute-start.10 = (bf16[512,512]{1,0:T(8,128)(2,1)S(1)}, bf16[512,512]{1,0:T(8,128)(2,1)S(1)}, u32[]{:S(2)}, u32[]{:S(2)}) collective-permute-start(bf16[512,512]{1,0:T(8,128)(2,1)S(1)} %get-tuple-element.33.refs_0_), channel_id=1, source_target_pairs={{0,16},{16,32},{32,48},{48,64},{64,80},{80,96},{96,112},{112,0},{1... | collective-permute-start | bytes 1572872 | tf_op jit(solution)/shard_map/ppermute | solution.py:53
  49.0 1.5 collective-permute-start.17
  50.5 1.7 %collective-permute-start.11 = (bf16[256,512]{1,0:T(8,128)(2,1)S(1)}, bf16[256,512]{1,0:T(8,128)(2,1)S(1)}, u32[]{:S(2)}, u32[]{:S(2)}) collective-permute-start(bf16[256,512]{1,0:T(8,128)(2,1)S(1)} %get-tuple-element.34), channel_id=1, source_target_pairs={{0,112},{16,0},{32,16},{48,32},{64,48},{80,64},{96,80},{112,96},{1... | collective-permute-start | bytes 786440 | tf_op jit(solution)/shard_map/ppermute | solution.py:53
  52.3 1.4 collective-permute-start.22
  53.7 3.1 %shard_map.111.refs_2_.refs_5_ = f32[1280,512]{1,0:T(8,128)S(1)} custom-call(bf16[640,8192]{1,0:T(8,128)(2,1)S(1)} %shard_map.103.refs_3_.own, bf16[640,8192]{1,0:T(8,128)(2,1)S(1)} %shard_map.104.refs_2_.sib, bf16[512,512]{1,0:T(8,128)(2,1)S(1)} %get-tuple-element.33.refs_0_, ...), custom_call_target="tpu_custom_call", output_to_operand_aliasing={{}: (7, {})} | custom-call | flops 2684354560 | bytes 2097152 | tf_op jit(solution)/shard_map/pallas_call | solution.py:264
  56.8 2.2 %collective-permute-start.18 = (bf16[256,512]{1,0:T(8,128)(2,1)S(1)}, bf16[256,512]{1,0:T(8,128)(2,1)S(1)}, u32[]{:S(2)}, u32[]{:S(2)}) collective-permute-start(bf16[256,512]{1,0:T(8,128)(2,1)S(1)} %collective-permute-done.17.refs_2_), channel_id=1, source_target_pairs={{0,128},{128,0},{1,129},{129,1},{2,130},{130,2},{3,131},{131,3},{4... | collective-permute-start | bytes 786440 | tf_op jit(solution)/shard_map/ppermute | solution.py:53
  59.0 0.9 collective-permute-done.10.refs_0_
  60.0 0.9 collective-permute-start.15
  60.9 2.4 %collective-permute-start.16 = (bf16[256,512]{1,0:T(8,128)(2,1)S(1)}, bf16[256,512]{1,0:T(8,128)(2,1)S(1)}, u32[]{:S(2)}, u32[]{:S(2)}) collective-permute-start(bf16[256,512]{1,0:T(8,128)(2,1)S(1)} %get-tuple-element.38.refs_1_), channel_id=1, source_target_pairs={{0,2},{2,4},{4,6},{6,0},{1,3},{3,5},{5,7},{7,1},{8,10},{10,12},{12... | collective-permute-start | bytes 786440 | tf_op jit(solution)/shard_map/ppermute | solution.py:53
  63.3 1.6 %collective-permute-start.20 = (bf16[256,512]{1,0:T(8,128)(2,1)S(1)}, bf16[256,512]{1,0:T(8,128)(2,1)S(1)}, u32[]{:S(2)}, u32[]{:S(2)}) collective-permute-start(bf16[256,512]{1,0:T(8,128)(2,1)S(1)} %get-tuple-element.37), channel_id=1, source_target_pairs={{0,134},{2,128},{4,130},{6,132},{128,6},{130,0},{132,2},{134,4},{1... | collective-permute-start | bytes 786440 | tf_op jit(solution)/shard_map/ppermute | solution.py:53
  64.9 2.7 %shard_map.113.refs_5_ = f32[1280,512]{1,0:T(8,128)S(1)} custom-call(bf16[640,8192]{1,0:T(8,128)(2,1)S(1)} %shard_map.103.refs_3_.own, bf16[640,8192]{1,0:T(8,128)(2,1)S(1)} %shard_map.104.refs_2_.sib, bf16[512,512]{1,0:T(8,128)(2,1)S(1)} %get-tuple-element.41.refs_0_, ...), custom_call_target="tpu_custom_call", output_to_operand_aliasing={{}: (7, {})} | custom-call | flops 2348810240 | bytes 1835008 | tf_op jit(solution)/shard_map/pallas_call | solution.py:264
  67.6 2.3 %collective-permute-done.15.refs_0_ = bf16[256,512]{1,0:T(8,128)(2,1)S(1)} collective-permute-done((bf16[256,512]{1,0:T(8,128)(2,1)S(1)}, bf16[256,512]{1,0:T(8,128)(2,1)S(1)}, u32[]{:S(2)}, u32[]{:S(2)}) %collective-permute-start.15) | collective-permute-done | bytes 262176 | tf_op jit(solution)/shard_map/ppermute | solution.py:53
  69.9 0.9 collective-permute-done.19.refs_3_
  70.9 2.9 %collective-permute-done.20.refs_4_ = bf16[256,512]{1,0:T(8,128)(2,1)S(1)} collective-permute-done((bf16[256,512]{1,0:T(8,128)(2,1)S(1)}, bf16[256,512]{1,0:T(8,128)(2,1)S(1)}, u32[]{:S(2)}, u32[]{:S(2)}) %collective-permute-start.20) | collective-permute-done | bytes 262176 | tf_op jit(solution)/shard_map/ppermute | solution.py:53
  73.7 2.7 %shard_map.114 = (f32[1280,512]{1,0:T(8,128)S(1)}, f32[64,4,128]{2,1,0:T(4,128)S(1)}) custom-call(bf16[640,8192]{1,0:T(8,128)(2,1)S(1)} %shard_map.103.refs_3_.own, bf16[640,8192]{1,0:T(8,128)(2,1)S(1)} %shard_map.104.refs_2_.sib, bf16[256,512]{1,0:T(8,128)(2,1)S(1)} %collective-permute-done.15.refs_0_, ...), custom_call_target="tpu_custom_call" | custom-call | flops 1677721600 | bytes 1310720 | tf_op jit(solution)/shard_map/pallas_call | solution.py:264
  76.5 19.9 %all_to_all.15.squares = f32[64,4,128]{2,1,0:T(4,128)S(1)} all-to-all(f32[64,4,128]{2,1,0:T(4,128)S(1)} %get-tuple-element.43), channel_id=1, replica_groups=mesh['yh'=2,'z'=8,'tp'=2,'x'=4,'core'=2] {'x','z','yh'}, dimensions={0} | all-to-all | bytes 262144 | tf_op jit(solution)/shard_map/all_to_all | solution.py:534
  96.4 1.1 shard_map.115
  97.5 2.4 %collective-permute-start.23 = (bf16[1280,128]{1,0:T(8,128)(2,1)S(1)}, bf16[1280,128]{1,0:T(8,128)(2,1)S(1)}, u32[]{:S(2)}, u32[]{:S(2)}) collective-permute-start(bf16[1280,128]{1,0:T(8,128)(2,1)S(1)} %get-tuple-element.44), channel_id=1, source_target_pairs={{0,0},{2,2},{4,12},{6,14},{8,4},{10,6},{12,8},{14,10},{1,1},{3,3},... | collective-permute-start | bytes 983048 | tf_op jit(solution)/shard_map/ppermute | solution.py:543
  99.9 4.2 %collective-permute-start.24 = (bf16[1280,128]{1,0:T(8,128)(2,1)S(1)}, bf16[1280,128]{1,0:T(8,128)(2,1)S(1)}, u32[]{:S(2)}, u32[]{:S(2)}) collective-permute-start(bf16[1280,128]{1,0:T(8,128)(2,1)S(1)} %get-tuple-element.45), channel_id=1, source_target_pairs={{0,2},{2,4},{4,14},{6,8},{8,6},{10,0},{12,10},{14,12},{1,3},{3,5},... | collective-permute-start | bytes 983048 | tf_op jit(solution)/shard_map/ppermute | solution.py:543
  104.2 1.9 %collective-permute-start.25 = (bf16[1280,128]{1,0:T(8,128)(2,1)S(1)}, bf16[1280,128]{1,0:T(8,128)(2,1)S(1)}, u32[]{:S(2)}, u32[]{:S(2)}) collective-permute-start(bf16[1280,128]{1,0:T(8,128)(2,1)S(1)} %get-tuple-element.46), channel_id=1, source_target_pairs={{0,4},{2,6},{4,8},{6,10},{8,0},{10,2},{12,12},{14,14},{1,5},{3,7},... | collective-permute-start | bytes 983048 | tf_op jit(solution)/shard_map/ppermute | solution.py:543
  106.9 3.1 %collective-permute-done.27.other_scale = f32[1,512]{1,0:T(1,128)S(1)} collective-permute-done((f32[1,512]{1,0:T(1,128)S(1)}, f32[1,512]{1,0:T(1,128)S(1)}, u32[]{:S(2)}, u32[]{:S(2)}) %collective-permute-start.27) | collective-permute-done | bytes 2080 | tf_op jit(solution)/shard_map/ppermute | solution.py:53
  110.6 3.3 %collective-permute-done.24.r1 = bf16[1280,128]{1,0:T(8,128)(2,1)S(1)} collective-permute-done((bf16[1280,128]{1,0:T(8,128)(2,1)S(1)}, bf16[1280,128]{1,0:T(8,128)(2,1)S(1)}, u32[]{:S(2)}, u32[]{:S(2)}) %collective-permute-start.24) | collective-permute-done | bytes 327712 | tf_op jit(solution)/shard_map/ppermute | solution.py:543
  113.9 1.8 %collective-permute-done.25.r2 = bf16[1280,128]{1,0:T(8,128)(2,1)S(1)} collective-permute-done((bf16[1280,128]{1,0:T(8,128)(2,1)S(1)}, bf16[1280,128]{1,0:T(8,128)(2,1)S(1)}, u32[]{:S(2)}, u32[]{:S(2)}) %collective-permute-start.25) | collective-permute-done | bytes 327712 | tf_op jit(solution)/shard_map/ppermute | solution.py:543
  115.6 3.2 %collective-permute-done.26.r3 = bf16[1280,128]{1,0:T(8,128)(2,1)S(1)} collective-permute-done((bf16[1280,128]{1,0:T(8,128)(2,1)S(1)}, bf16[1280,128]{1,0:T(8,128)(2,1)S(1)}, u32[]{:S(2)}, u32[]{:S(2)}) %collective-permute-start.26) | collective-permute-done | bytes 327712 | tf_op jit(solution)/shard_map/ppermute | solution.py:543
  118.8 3.7 %shard_map.116 = (bf16[2,10,256,128]{3,2,1,0:T(8,128)(2,1)}, f32[16,40,128]{2,1,0:T(8,128)S(1)}) custom-call(s32[10]{0:T(128)S(1)} %copy-done.6, bf16[1280,128]{1,0:T(8,128)(2,1)S(1)} %collective-permute-done.23.r0, bf16[1280,128]{1,0:T(8,128)(2,1)S(1)} %collective-permute-done.24.r1, bf16[1280,128]{1,0:T(8,128)(2,1)S(1)} %collective-permute-done.25.r2, ...), custom_call_target="tpu_custom_call" | custom-call | flops 671088640 | bytes 2621440 | tf_op jit(solution)/shard_map/pallas_call | solution.py:379
  122.6 14.3 %all_to_all.16.parts = f32[16,40,128]{2,1,0:T(8,128)S(1)} all-to-all(f32[16,40,128]{2,1,0:T(8,128)S(1)} %get-tuple-element.50), channel_id=1, replica_groups=mesh['yh'=2,'z'=8,'tp'=2,'x'=4,'core'=2] {'z','tp'}, dimensions={0} | all-to-all | bytes 655360 | tf_op jit(solution)/shard_map/all_to_all | solution.py:552
  136.9 1.1 shard_map.117
  138.0 3.9 %all-to-all-start.2 = ((bf16[32,32,128]{2,1,0:T(8,128)(2,1)}), bf16[32,32,128]{2,1,0:T(8,128)(2,1)S(1)}, u32[]{:S(2)}, u32[]{:S(2)}) async-start(bf16[32,32,128]{2,1,0:T(8,128)(2,1)} %shard_map.117), calls=%async_computation.2 | async-start | bytes 524288 | tf_op jit(solution)/shard_map/all_to_all | solution.py:554
  142.0 1.2 collective-permute-done.28.far
  143.1 11.1 %all-to-all-done.2.whole = bf16[32,32,128]{2,1,0:T(8,128)(2,1)S(1)} async-done(((bf16[32,32,128]{2,1,0:T(8,128)(2,1)}), bf16[32,32,128]{2,1,0:T(8,128)(2,1)S(1)}, u32[]{:S(2)}, u32[]{:S(2)}) %all-to-all-start.2) | async-done | bytes 262176 | tf_op jit(solution)/shard_map/all_to_all | solution.py:554
  154.2 0.8 shard_map.118
  (48 shorter events, 3.1 us)
Async XLA Ops:
  0.6 24.0 %collective-permute-start = (bf16[640,8192]{1,0:T(8,128)(2,1)}, bf16[640,8192]{1,0:T(8,128)(2,1)S(1)}, u32[]{:S(2)}, u32[]{:S(2)}) collective-permute-start(bf16[640,8192]{1,0:T(8,128)(2,1)} %source.1), channel_id=1, source_target_pairs={{0,1},{1,0},{2,3},{3,2},{4,5},{5,4},{6,7},{7,6},{8,9},{9,8},{10,11... | collective-permute-start | bytes 31457288 | tf_op jit(solution)/shard_map/ppermute | solution.py:53
  0.7 1.2 copy-start
  2.1 13.1 %collective-permute-start.1 = (bf16[256,512]{1,0:T(8,128)(2,1)S(1)}, bf16[256,512]{1,0:T(8,128)(2,1)S(1)}, u32[]{:S(2)}, u32[]{:S(2)}) collective-permute-start(bf16[256,512]{1,0:T(8,128)(2,1)S(1)} %shard_map.105), channel_id=1, source_target_pairs={{0,128},{128,0},{1,129},{129,1},{2,130},{130,2},{3,131},{131,3},{4... | collective-permute-start | bytes 786440 | tf_op jit(solution)/shard_map/ppermute | solution.py:53
  5.4 12.5 %collective-permute-start.2 = (bf16[256,512]{1,0:T(8,128)(2,1)S(1)}, bf16[256,512]{1,0:T(8,128)(2,1)S(1)}, u32[]{:S(2)}, u32[]{:S(2)}) collective-permute-start(bf16[256,512]{1,0:T(8,128)(2,1)S(1)} %shard_map.105), channel_id=1, source_target_pairs={{0,16},{16,32},{32,48},{48,64},{64,80},{80,96},{96,112},{112,0},{1... | collective-permute-start | bytes 786440 | tf_op jit(solution)/shard_map/ppermute | solution.py:53
  7.3 10.6 %collective-permute-start.3 = (bf16[256,512]{1,0:T(8,128)(2,1)S(1)}, bf16[256,512]{1,0:T(8,128)(2,1)S(1)}, u32[]{:S(2)}, u32[]{:S(2)}) collective-permute-start(bf16[256,512]{1,0:T(8,128)(2,1)S(1)} %shard_map.105), channel_id=1, source_target_pairs={{0,112},{16,0},{32,16},{48,32},{64,48},{80,64},{96,80},{112,96},{1... | collective-permute-start | bytes 786440 | tf_op jit(solution)/shard_map/ppermute | solution.py:53
  18.0 14.8 %collective-permute-start.4 = (bf16[512,512]{1,0:T(8,128)(2,1)S(1)}, bf16[512,512]{1,0:T(8,128)(2,1)S(1)}, u32[]{:S(2)}, u32[]{:S(2)}) collective-permute-start(bf16[512,512]{1,0:T(8,128)(2,1)S(1)} %get-tuple-element.28.refs_1_), channel_id=1, source_target_pairs={{0,16},{16,32},{32,48},{48,64},{64,80},{80,96},{96,112},{112,0},{1... | collective-permute-start | bytes 1572872 | tf_op jit(solution)/shard_map/ppermute | solution.py:53
  18.1 14.7 %collective-permute-start.5 = (bf16[512,512]{1,0:T(8,128)(2,1)S(1)}, bf16[512,512]{1,0:T(8,128)(2,1)S(1)}, u32[]{:S(2)}, u32[]{:S(2)}) collective-permute-start(bf16[512,512]{1,0:T(8,128)(2,1)S(1)} %get-tuple-element.29), channel_id=1, source_target_pairs={{0,112},{16,0},{32,16},{48,32},{64,48},{80,64},{96,80},{112,96},{1... | collective-permute-start | bytes 1572872 | tf_op jit(solution)/shard_map/ppermute | solution.py:53
  21.3 14.9 %collective-permute-start.8 = (bf16[512,512]{1,0:T(8,128)(2,1)S(1)}, bf16[512,512]{1,0:T(8,128)(2,1)S(1)}, u32[]{:S(2)}, u32[]{:S(2)}) collective-permute-start(bf16[512,512]{1,0:T(8,128)(2,1)S(1)} %get-tuple-element.28.refs_1_), channel_id=1, source_target_pairs={{0,6},{2,0},{4,2},{6,4},{1,7},{3,1},{5,3},{7,5},{8,14},{10,8},{12,... | collective-permute-start | bytes 1572872 | tf_op jit(solution)/shard_map/ppermute | solution.py:53
  22.2 15.2 %collective-permute-start.9 = (bf16[256,512]{1,0:T(8,128)(2,1)S(1)}, bf16[256,512]{1,0:T(8,128)(2,1)S(1)}, u32[]{:S(2)}, u32[]{:S(2)}) collective-permute-start(bf16[256,512]{1,0:T(8,128)(2,1)S(1)} %get-tuple-element.32.refs_2_), channel_id=1, source_target_pairs={{0,2},{2,4},{4,6},{6,0},{1,3},{3,5},{5,7},{7,1},{8,10},{10,12},{12... | collective-permute-start | bytes 786440 | tf_op jit(solution)/shard_map/ppermute | solution.py:53
  25.3 13.7 %copy-start.1 = (bf16[512,1024]{1,0:T(8,128)(2,1)S(1)}, bf16[512,1024]{1,0:T(8,128)(2,1)}, u32[]{:S(2)}) copy-start(bf16[512,1024]{1,0:T(8,128)(2,1)} %refs_0_.1) | copy-start | bytes 3145732
  32.9 13.9 %collective-permute-start.6 = (bf16[512,512]{1,0:T(8,128)(2,1)S(1)}, bf16[512,512]{1,0:T(8,128)(2,1)S(1)}, u32[]{:S(2)}, u32[]{:S(2)}) collective-permute-start(bf16[512,512]{1,0:T(8,128)(2,1)S(1)} %get-tuple-element.30.refs_5_), channel_id=1, source_target_pairs={{0,16},{16,32},{32,48},{48,64},{64,80},{80,96},{96,112},{112,0},{1... | collective-permute-start | bytes 1572872 | tf_op jit(solution)/shard_map/ppermute | solution.py:53
  34.8 12.0 %collective-permute-start.7 = (bf16[512,512]{1,0:T(8,128)(2,1)S(1)}, bf16[512,512]{1,0:T(8,128)(2,1)S(1)}, u32[]{:S(2)}, u32[]{:S(2)}) collective-permute-start(bf16[512,512]{1,0:T(8,128)(2,1)S(1)} %get-tuple-element.31.refs_6_), channel_id=1, source_target_pairs={{0,112},{16,0},{32,16},{48,32},{64,48},{80,64},{96,80},{112,96},{1... | collective-permute-start | bytes 1572872 | tf_op jit(solution)/shard_map/ppermute | solution.py:53
  36.2 12.7 %collective-permute-start.14 = (bf16[256,512]{1,0:T(8,128)(2,1)S(1)}, bf16[256,512]{1,0:T(8,128)(2,1)S(1)}, u32[]{:S(2)}, u32[]{:S(2)}) collective-permute-start(bf16[256,512]{1,0:T(8,128)(2,1)S(1)} %shard_map.110), channel_id=1, source_target_pairs={{0,128},{128,0},{1,129},{129,1},{2,130},{130,2},{3,131},{131,3},{4... | collective-permute-start | bytes 786440 | tf_op jit(solution)/shard_map/ppermute | solution.py:53
  36.9 15.3 %collective-permute-start.13 = (bf16[512,512]{1,0:T(8,128)(2,1)S(1)}, bf16[512,512]{1,0:T(8,128)(2,1)S(1)}, u32[]{:S(2)}, u32[]{:S(2)}) collective-permute-start(bf16[512,512]{1,0:T(8,128)(2,1)S(1)} %get-tuple-element.31.refs_6_), channel_id=1, source_target_pairs={{0,2},{2,4},{4,6},{6,0},{1,3},{3,5},{5,7},{7,1},{8,10},{10,12},{12... | collective-permute-start | bytes 1572872 | tf_op jit(solution)/shard_map/ppermute | solution.py:53
  37.4 13.1 %collective-permute-start.12 = (bf16[256,512]{1,0:T(8,128)(2,1)S(1)}, bf16[256,512]{1,0:T(8,128)(2,1)S(1)}, u32[]{:S(2)}, u32[]{:S(2)}) collective-permute-start(bf16[256,512]{1,0:T(8,128)(2,1)S(1)} %get-tuple-element.36), channel_id=1, source_target_pairs={{0,6},{2,0},{4,2},{6,4},{1,7},{3,1},{5,3},{7,5},{8,14},{10,8},{12,... | collective-permute-start | bytes 786440 | tf_op jit(solution)/shard_map/ppermute | solution.py:53
  46.9 13.0 %collective-permute-start.10 = (bf16[512,512]{1,0:T(8,128)(2,1)S(1)}, bf16[512,512]{1,0:T(8,128)(2,1)S(1)}, u32[]{:S(2)}, u32[]{:S(2)}) collective-permute-start(bf16[512,512]{1,0:T(8,128)(2,1)S(1)} %get-tuple-element.33.refs_0_), channel_id=1, source_target_pairs={{0,16},{16,32},{32,48},{48,64},{64,80},{80,96},{96,112},{112,0},{1... | collective-permute-start | bytes 1572872 | tf_op jit(solution)/shard_map/ppermute | solution.py:53
  48.5 14.8 %collective-permute-start.21 = (bf16[512,512]{1,0:T(8,128)(2,1)S(1)}, bf16[512,512]{1,0:T(8,128)(2,1)S(1)}, u32[]{:S(2)}, u32[]{:S(2)}) collective-permute-start(bf16[512,512]{1,0:T(8,128)(2,1)S(1)} %get-tuple-element.35.refs_1_), channel_id=1, source_target_pairs={{0,2},{2,4},{4,6},{6,0},{1,3},{3,5},{5,7},{7,1},{8,10},{10,12},{12... | collective-permute-start | bytes 1572872 | tf_op jit(solution)/shard_map/ppermute | solution.py:53
  49.0 7.8 %collective-permute-start.17 = (bf16[256,512]{1,0:T(8,128)(2,1)S(1)}, bf16[256,512]{1,0:T(8,128)(2,1)S(1)}, u32[]{:S(2)}, u32[]{:S(2)}) collective-permute-start(bf16[256,512]{1,0:T(8,128)(2,1)S(1)} %get-tuple-element.39), channel_id=1, source_target_pairs={{0,6},{2,0},{4,2},{6,4},{1,7},{3,1},{5,3},{7,5},{8,14},{10,8},{12,... | collective-permute-start | bytes 786440 | tf_op jit(solution)/shard_map/ppermute | solution.py:53
  50.5 8.5 %collective-permute-start.11 = (bf16[256,512]{1,0:T(8,128)(2,1)S(1)}, bf16[256,512]{1,0:T(8,128)(2,1)S(1)}, u32[]{:S(2)}, u32[]{:S(2)}) collective-permute-start(bf16[256,512]{1,0:T(8,128)(2,1)S(1)} %get-tuple-element.34), channel_id=1, source_target_pairs={{0,112},{16,0},{32,16},{48,32},{64,48},{80,64},{96,80},{112,96},{1... | collective-permute-start | bytes 786440 | tf_op jit(solution)/shard_map/ppermute | solution.py:53
  52.3 11.0 %collective-permute-start.22 = (bf16[256,512]{1,0:T(8,128)(2,1)S(1)}, bf16[256,512]{1,0:T(8,128)(2,1)S(1)}, u32[]{:S(2)}, u32[]{:S(2)}) collective-permute-start(bf16[256,512]{1,0:T(8,128)(2,1)S(1)} %collective-permute-done.12.refs_2_), channel_id=1, source_target_pairs={{0,128},{128,0},{1,129},{129,1},{2,130},{130,2},{3,131},{131,3},{4... | collective-permute-start | bytes 786440 | tf_op jit(solution)/shard_map/ppermute | solution.py:53
  56.8 10.8 %collective-permute-start.18 = (bf16[256,512]{1,0:T(8,128)(2,1)S(1)}, bf16[256,512]{1,0:T(8,128)(2,1)S(1)}, u32[]{:S(2)}, u32[]{:S(2)}) collective-permute-start(bf16[256,512]{1,0:T(8,128)(2,1)S(1)} %collective-permute-done.17.refs_2_), channel_id=1, source_target_pairs={{0,128},{128,0},{1,129},{129,1},{2,130},{130,2},{3,131},{131,3},{4... | collective-permute-start | bytes 786440 | tf_op jit(solution)/shard_map/ppermute | solution.py:53
  60.0 9.9 %collective-permute-start.15 = (bf16[256,512]{1,0:T(8,128)(2,1)S(1)}, bf16[256,512]{1,0:T(8,128)(2,1)S(1)}, u32[]{:S(2)}, u32[]{:S(2)}) collective-permute-start(bf16[256,512]{1,0:T(8,128)(2,1)S(1)} %get-tuple-element.37), channel_id=1, source_target_pairs={{0,6},{2,0},{4,2},{6,4},{1,7},{3,1},{5,3},{7,5},{8,14},{10,8},{12,... | collective-permute-start | bytes 786440 | tf_op jit(solution)/shard_map/ppermute | solution.py:53
  60.9 9.0 %collective-permute-start.16 = (bf16[256,512]{1,0:T(8,128)(2,1)S(1)}, bf16[256,512]{1,0:T(8,128)(2,1)S(1)}, u32[]{:S(2)}, u32[]{:S(2)}) collective-permute-start(bf16[256,512]{1,0:T(8,128)(2,1)S(1)} %get-tuple-element.38.refs_1_), channel_id=1, source_target_pairs={{0,2},{2,4},{4,6},{6,0},{1,3},{3,5},{5,7},{7,1},{8,10},{10,12},{12... | collective-permute-start | bytes 786440 | tf_op jit(solution)/shard_map/ppermute | solution.py:53
  63.3 7.6 %collective-permute-start.19 = (bf16[256,512]{1,0:T(8,128)(2,1)S(1)}, bf16[256,512]{1,0:T(8,128)(2,1)S(1)}, u32[]{:S(2)}, u32[]{:S(2)}) collective-permute-start(bf16[256,512]{1,0:T(8,128)(2,1)S(1)} %get-tuple-element.40), channel_id=1, source_target_pairs={{0,16},{16,32},{32,48},{48,64},{64,80},{80,96},{96,112},{112,0},{1... | collective-permute-start | bytes 786440 | tf_op jit(solution)/shard_map/ppermute | solution.py:53
  63.3 10.4 %collective-permute-start.20 = (bf16[256,512]{1,0:T(8,128)(2,1)S(1)}, bf16[256,512]{1,0:T(8,128)(2,1)S(1)}, u32[]{:S(2)}, u32[]{:S(2)}) collective-permute-start(bf16[256,512]{1,0:T(8,128)(2,1)S(1)} %get-tuple-element.37), channel_id=1, source_target_pairs={{0,134},{2,128},{4,130},{6,132},{128,6},{130,0},{132,2},{134,4},{1... | collective-permute-start | bytes 786440 | tf_op jit(solution)/shard_map/ppermute | solution.py:53
  64.9 8.9 %copy-start.5 = (s32[2]{0:T(128)S(1)}, s32[2]{0:T(128)}, u32[]{:S(2)}) copy-start(s32[2]{0:T(128)} %lengths.1) | copy-start | bytes 28
  76.4 30.3 %copy-start.7 = (s32[2,64]{1,0:T(2,128)S(1)}, s32[2,64]{1,0:T(2,128)}, u32[]{:S(2)}) copy-start(s32[2,64]{1,0:T(2,128)} %param.15) | copy-start | bytes 1540
  76.5 42.4 %copy-start.2 = (bf16[2,64,1024]{2,1,0:T(8,128)(2,1)S(1)}, bf16[2,64,1024]{2,1,0:T(8,128)(2,1)}, u32[]{:S(2)}) copy-start(bf16[2,64,1024]{2,1,0:T(8,128)(2,1)} %query.3) | copy-start | bytes 786436
  76.5 42.4 %copy-start.6 = (s32[10]{0:T(128)S(1)}, s32[10]{0:T(128)}, u32[]{:S(2)}) copy-start(s32[10]{0:T(128)} %pages.1) | copy-start | bytes 124
  96.4 40.5 %copy-start.3 = (bf16[2,64,128]{2,1,0:T(8,128)(2,1)S(1)}, bf16[2,64,128]{2,1,0:T(8,128)(2,1)}, u32[]{:S(2)}) copy-start(bf16[2,64,128]{2,1,0:T(8,128)(2,1)} %new_key.1) | copy-start | bytes 98308
  96.4 40.5 %copy-start.4 = (bf16[2,64,128]{2,1,0:T(8,128)(2,1)S(1)}, bf16[2,64,128]{2,1,0:T(8,128)(2,1)}, u32[]{:S(2)}) copy-start(bf16[2,64,128]{2,1,0:T(8,128)(2,1)} %new_value.1) | copy-start | bytes 98308
  97.5 13.1 %collective-permute-start.23 = (bf16[1280,128]{1,0:T(8,128)(2,1)S(1)}, bf16[1280,128]{1,0:T(8,128)(2,1)S(1)}, u32[]{:S(2)}, u32[]{:S(2)}) collective-permute-start(bf16[1280,128]{1,0:T(8,128)(2,1)S(1)} %get-tuple-element.44), channel_id=1, source_target_pairs={{0,0},{2,2},{4,12},{6,14},{8,4},{10,6},{12,8},{14,10},{1,1},{3,3},... | collective-permute-start | bytes 983048 | tf_op jit(solution)/shard_map/ppermute | solution.py:543
  99.9 13.9 %collective-permute-start.24 = (bf16[1280,128]{1,0:T(8,128)(2,1)S(1)}, bf16[1280,128]{1,0:T(8,128)(2,1)S(1)}, u32[]{:S(2)}, u32[]{:S(2)}) collective-permute-start(bf16[1280,128]{1,0:T(8,128)(2,1)S(1)} %get-tuple-element.45), channel_id=1, source_target_pairs={{0,2},{2,4},{4,14},{6,8},{8,6},{10,0},{12,10},{14,12},{1,3},{3,5},... | collective-permute-start | bytes 983048 | tf_op jit(solution)/shard_map/ppermute | solution.py:543
  104.2 11.5 %collective-permute-start.25 = (bf16[1280,128]{1,0:T(8,128)(2,1)S(1)}, bf16[1280,128]{1,0:T(8,128)(2,1)S(1)}, u32[]{:S(2)}, u32[]{:S(2)}) collective-permute-start(bf16[1280,128]{1,0:T(8,128)(2,1)S(1)} %get-tuple-element.46), channel_id=1, source_target_pairs={{0,4},{2,6},{4,8},{6,10},{8,0},{10,2},{12,12},{14,14},{1,5},{3,7},... | collective-permute-start | bytes 983048 | tf_op jit(solution)/shard_map/ppermute | solution.py:543
  106.1 12.8 %collective-permute-start.26 = (bf16[1280,128]{1,0:T(8,128)(2,1)S(1)}, bf16[1280,128]{1,0:T(8,128)(2,1)S(1)}, u32[]{:S(2)}, u32[]{:S(2)}) collective-permute-start(bf16[1280,128]{1,0:T(8,128)(2,1)S(1)} %get-tuple-element.47), channel_id=1, source_target_pairs={{0,6},{2,0},{4,10},{6,12},{8,2},{10,4},{12,14},{14,8},{1,7},{3,1},... | collective-permute-start | bytes 983048 | tf_op jit(solution)/shard_map/ppermute | solution.py:543
  106.2 3.8 %collective-permute-start.27 = (f32[1,512]{1,0:T(1,128)S(1)}, f32[1,512]{1,0:T(1,128)S(1)}, u32[]{:S(2)}, u32[]{:S(2)}) collective-permute-start(f32[1,512]{1,0:T(1,128)S(1)} %get-tuple-element.48.own_scale), channel_id=1, source_target_pairs={{0,8},{8,0},{1,9},{9,1},{2,10},{10,2},{3,11},{11,3},{4,12},{12,4},... | collective-permute-start | bytes 6152 | tf_op jit(solution)/shard_map/ppermute | solution.py:53
  138.0 16.3 %all-to-all-start.2 = ((bf16[32,32,128]{2,1,0:T(8,128)(2,1)}), bf16[32,32,128]{2,1,0:T(8,128)(2,1)S(1)}, u32[]{:S(2)}, u32[]{:S(2)}) async-start(bf16[32,32,128]{2,1,0:T(8,128)(2,1)} %shard_map.117), calls=%async_computation.2 | async-start | bytes 524288 | tf_op jit(solution)/shard_map/all_to_all | solution.py:554
  141.9 1.3 collective-permute-start.28

commit v4 on v3

--- a/solution.py
+++ b/solution.py
@@ -525,8 +525,8 @@
     wave = [(up, at(-4)), (down, far(3)), (over, swapped(near(-3))), (under, swapped(at(3)))]
     wave += [(side, swapped(far(-2)))]
 
-    side, under, cross = send(over, yh=1), send(down, x=1), send(next_last, z=1)
-    corner, over = send(last, yh=1, x=-1), send(last, x=-1)
+    side, under, cross = send(over, yh=1), send(down, x=1), send(down, z=-1)
+    corner, over = send(next_last, z=1, x=1), send(last, x=-1)
     acc = project(own, sib, wave, acc)[0]
     wave = [(over, swapped(near(-4))), (under, swapped(far(3))), (side, swapped(far(-3)))]
     wave += [(cross, far(-4)), (corner, swapped(far(-4)))]

time: 155 us -> 154 us (level)
  waiting for transfers between devices: 44.9 us -> 39.3 us
  starting transfers between devices: 48.8 us -> 51.9 us
    ppermute x25, waiting for transfers between devices: 24.9 us -> 20.9 us  [send(): return lax.ppermute(value, names if len(names) > 1 else names[0], pairs)]
    ppermute x25, starting transfers between devices: 36.3 us -> 39.5 us  [send(): return lax.ppermute(value, names if len(names) > 1 else names[0], pairs)]
    ppermute x4, waiting for transfers between devices: 8.84 us -> 7.24 us  [body(): received.append(lax.ppermute(sent[k], ('tp', 'x'), pairs))]
  transfers between devices with their start and end apart: 30 -> 30, of which waited for: 14 -> 13; matrix products, arithmetic and copies ran while one was open for 0% -> 0% of each run, Pallas kernels for 10% -> 10%
where the time goes in v4:
time: 154 us; the launch traced here: 153 us
  starting transfers between devices  51.9 us (34%)
  waiting for transfers between devices  39.3 us (26%)
  blocking collectives  35 us (23%)
  Pallas kernels  24.8 us (16%)
    ppermute x25, starting transfers between devices, send(): return lax.ppermute(value, names if len(names) > 1 else names[0], pairs)  39.5 us
    all_to_all x1, blocking collectives, body(): squares = lax.all_to_all(squares, ('x', 'z', 'yh'), 0, 0, tiled=True)  21.1 us
    ppermute x25, waiting for transfers between devices, send(): return lax.ppermute(value, names if len(names) > 1 else names[0], pairs)  20.9 us
    all_to_all x1, blocking collectives, body(): parts = lax.all_to_all(part, ('z', 'tp'), 0, 0, tiled=True)  13.9 us
    pallas_call x4, Pallas kernels, project(): pl.pallas_call(functools.partial(project_kernel, names, acc is not None,...  13 us
    all_to_all x1, waiting for transfers between devices, body(): whole = lax.all_to_all(result, ('yh', 'z', 'tp'), 0, 0, tiled=True)  11.1 us
    ppermute x4, starting transfers between devices, body(): received.append(lax.ppermute(sent[k], ('tp', 'x'), pairs))  8.55 us
    ppermute x4, waiting for transfers between devices, body(): received.append(lax.ppermute(sent[k], ('tp', 'x'), pairs))  7.24 us
  transfers between devices with their start and end apart: 30, of which 13 were waited for; matrix products, arithmetic and copies ran while one was open for 0% of the time, Pallas kernels for 10%

profile of v4, /device:TPU:6, one launch (start us, length us, event | category | flops | bytes accessed | tf_op | source)
XLA Modules:
  0.0 153.3 jit_solution(1003276098639838733)
XLA Ops:
  0.7 1.2 copy-done
  2.1 3.3 %collective-permute-start.1 = (bf16[256,512]{1,0:T(8,128)(2,1)S(1)}, bf16[256,512]{1,0:T(8,128)(2,1)S(1)}, u32[]{:S(2)}, u32[]{:S(2)}) collective-permute-start(bf16[256,512]{1,0:T(8,128)(2,1)S(1)} %shard_map.105), channel_id=1, source_target_pairs={{0,128},{128,0},{1,129},{129,1},{2,130},{130,2},{3,131},{131,3},{4... | collective-permute-start | bytes 786440 | tf_op jit(solution)/shard_map/ppermute | solution.py:53
  5.4 1.9 %collective-permute-start.2 = (bf16[256,512]{1,0:T(8,128)(2,1)S(1)}, bf16[256,512]{1,0:T(8,128)(2,1)S(1)}, u32[]{:S(2)}, u32[]{:S(2)}) collective-permute-start(bf16[256,512]{1,0:T(8,128)(2,1)S(1)} %shard_map.105), channel_id=1, source_target_pairs={{0,16},{16,32},{32,48},{48,64},{64,80},{80,96},{96,112},{112,0},{1... | collective-permute-start | bytes 786440 | tf_op jit(solution)/shard_map/ppermute | solution.py:53
  7.3 3.9 %collective-permute-start.3 = (bf16[256,512]{1,0:T(8,128)(2,1)S(1)}, bf16[256,512]{1,0:T(8,128)(2,1)S(1)}, u32[]{:S(2)}, u32[]{:S(2)}) collective-permute-start(bf16[256,512]{1,0:T(8,128)(2,1)S(1)} %shard_map.105), channel_id=1, source_target_pairs={{0,112},{16,0},{32,16},{48,32},{64,48},{80,64},{96,80},{112,96},{1... | collective-permute-start | bytes 786440 | tf_op jit(solution)/shard_map/ppermute | solution.py:53
  11.2 4.0 %shard_map.103.refs_3_.own = bf16[640,8192]{1,0:T(8,128)(2,1)S(1)} custom-call(bf16[640,8192]{1,0:T(8,128)(2,1)} %source.1), custom_call_target="tpu_custom_call" | custom-call | bytes 20971520 | tf_op jit(solution)/shard_map/pallas_call | solution.py:124
  15.2 2.7 %collective-permute-done.2.refs_1_ = bf16[256,512]{1,0:T(8,128)(2,1)S(1)} collective-permute-done((bf16[256,512]{1,0:T(8,128)(2,1)S(1)}, bf16[256,512]{1,0:T(8,128)(2,1)S(1)}, u32[]{:S(2)}, u32[]{:S(2)}) %collective-permute-start.2) | collective-permute-done | bytes 262176 | tf_op jit(solution)/shard_map/ppermute | solution.py:53
  18.1 3.2 %collective-permute-start.5 = (bf16[512,512]{1,0:T(8,128)(2,1)S(1)}, bf16[512,512]{1,0:T(8,128)(2,1)S(1)}, u32[]{:S(2)}, u32[]{:S(2)}) collective-permute-start(bf16[512,512]{1,0:T(8,128)(2,1)S(1)} %get-tuple-element.29), channel_id=1, source_target_pairs={{0,112},{16,0},{32,16},{48,32},{64,48},{80,64},{96,80},{112,96},{1... | collective-permute-start | bytes 1572872 | tf_op jit(solution)/shard_map/ppermute | solution.py:53
  21.3 0.8 collective-permute-start.8
  22.2 2.4 %collective-permute-start.9 = (bf16[256,512]{1,0:T(8,128)(2,1)S(1)}, bf16[256,512]{1,0:T(8,128)(2,1)S(1)}, u32[]{:S(2)}, u32[]{:S(2)}) collective-permute-start(bf16[256,512]{1,0:T(8,128)(2,1)S(1)} %get-tuple-element.32.refs_2_), channel_id=1, source_target_pairs={{0,2},{2,4},{4,6},{6,0},{1,3},{3,5},{5,7},{7,1},{8,10},{10,12},{12... | collective-permute-start | bytes 786440 | tf_op jit(solution)/shard_map/ppermute | solution.py:53
  24.6 0.7 shard_map.104.refs_2_.sib
  25.3 7.5 %collective-permute-done.4.refs_0_ = bf16[512,512]{1,0:T(8,128)(2,1)S(1)} collective-permute-done((bf16[512,512]{1,0:T(8,128)(2,1)S(1)}, bf16[512,512]{1,0:T(8,128)(2,1)S(1)}, u32[]{:S(2)}, u32[]{:S(2)}) %collective-permute-start.4) | collective-permute-done | bytes 524320 | tf_op jit(solution)/shard_map/ppermute | solution.py:53
  32.9 1.9 %collective-permute-start.6 = (bf16[512,512]{1,0:T(8,128)(2,1)S(1)}, bf16[512,512]{1,0:T(8,128)(2,1)S(1)}, u32[]{:S(2)}, u32[]{:S(2)}) collective-permute-start(bf16[512,512]{1,0:T(8,128)(2,1)S(1)} %get-tuple-element.30.refs_5_), channel_id=1, source_target_pairs={{0,16},{16,32},{32,48},{48,64},{64,80},{80,96},{96,112},{112,0},{1... | collective-permute-start | bytes 1572872 | tf_op jit(solution)/shard_map/ppermute | solution.py:53
  34.8 1.4 collective-permute-start.7
  37.4 1.5 %collective-permute-start.12 = (bf16[256,512]{1,0:T(8,128)(2,1)S(1)}, bf16[256,512]{1,0:T(8,128)(2,1)S(1)}, u32[]{:S(2)}, u32[]{:S(2)}) collective-permute-start(bf16[256,512]{1,0:T(8,128)(2,1)S(1)} %get-tuple-element.36), channel_id=1, source_target_pairs={{0,6},{2,0},{4,2},{6,4},{1,7},{3,1},{5,3},{7,5},{8,14},{10,8},{12,... | collective-permute-start | bytes 786440 | tf_op jit(solution)/shard_map/ppermute | solution.py:53
  38.9 4.5 %shard_map.108.refs_2_.refs_5_ = f32[1280,512]{1,0:T(8,128)S(1)} custom-call(bf16[640,8192]{1,0:T(8,128)(2,1)S(1)} %shard_map.103.refs_3_.own, bf16[640,8192]{1,0:T(8,128)(2,1)S(1)} %shard_map.104.refs_2_.sib, bf16[512,1024]{1,0:T(8,128)(2,1)S(1)} %copy-done.1, bf16[512,512]{1,0:T(8,128)(2,1)S(1)} %get-tuple-element.28.refs_1_, ...), custom_call_target="tpu_custom_call" | custom-call | flops 4026531840 | bytes 3145728 | tf_op jit(solution)/shard_map/pallas_call | solution.py:264
  43.5 3.4 %collective-permute-done.6.refs_0_ = bf16[512,512]{1,0:T(8,128)(2,1)S(1)} collective-permute-done((bf16[512,512]{1,0:T(8,128)(2,1)S(1)}, bf16[512,512]{1,0:T(8,128)(2,1)S(1)}, u32[]{:S(2)}, u32[]{:S(2)}) %collective-permute-start.6) | collective-permute-done | bytes 524320 | tf_op jit(solution)/shard_map/ppermute | solution.py:53
  46.9 1.6 %collective-permute-start.10 = (bf16[512,512]{1,0:T(8,128)(2,1)S(1)}, bf16[512,512]{1,0:T(8,128)(2,1)S(1)}, u32[]{:S(2)}, u32[]{:S(2)}) collective-permute-start(bf16[512,512]{1,0:T(8,128)(2,1)S(1)} %get-tuple-element.33.refs_0_), channel_id=1, source_target_pairs={{0,16},{16,32},{32,48},{48,64},{64,80},{80,96},{96,112},{112,0},{1... | collective-permute-start | bytes 1572872 | tf_op jit(solution)/shard_map/ppermute | solution.py:53
  49.0 1.5 %collective-permute-start.17 = (bf16[256,512]{1,0:T(8,128)(2,1)S(1)}, bf16[256,512]{1,0:T(8,128)(2,1)S(1)}, u32[]{:S(2)}, u32[]{:S(2)}) collective-permute-start(bf16[256,512]{1,0:T(8,128)(2,1)S(1)} %get-tuple-element.39), channel_id=1, source_target_pairs={{0,6},{2,0},{4,2},{6,4},{1,7},{3,1},{5,3},{7,5},{8,14},{10,8},{12,... | collective-permute-start | bytes 786440 | tf_op jit(solution)/shard_map/ppermute | solution.py:53
  50.5 1.7 %collective-permute-start.11 = (bf16[256,512]{1,0:T(8,128)(2,1)S(1)}, bf16[256,512]{1,0:T(8,128)(2,1)S(1)}, u32[]{:S(2)}, u32[]{:S(2)}) collective-permute-start(bf16[256,512]{1,0:T(8,128)(2,1)S(1)} %get-tuple-element.34), channel_id=1, source_target_pairs={{0,112},{16,0},{32,16},{48,32},{64,48},{80,64},{96,80},{112,96},{1... | collective-permute-start | bytes 786440 | tf_op jit(solution)/shard_map/ppermute | solution.py:53
  52.3 1.4 collective-permute-start.22
  53.7 3.1 %shard_map.111.refs_2_.refs_5_ = f32[1280,512]{1,0:T(8,128)S(1)} custom-call(bf16[640,8192]{1,0:T(8,128)(2,1)S(1)} %shard_map.103.refs_3_.own, bf16[640,8192]{1,0:T(8,128)(2,1)S(1)} %shard_map.104.refs_2_.sib, bf16[512,512]{1,0:T(8,128)(2,1)S(1)} %get-tuple-element.33.refs_0_, ...), custom_call_target="tpu_custom_call", output_to_operand_aliasing={{}: (7, {})} | custom-call | flops 2684354560 | bytes 2097152 | tf_op jit(solution)/shard_map/pallas_call | solution.py:264
  56.8 2.2 %collective-permute-start.18 = (bf16[256,512]{1,0:T(8,128)(2,1)S(1)}, bf16[256,512]{1,0:T(8,128)(2,1)S(1)}, u32[]{:S(2)}, u32[]{:S(2)}) collective-permute-start(bf16[256,512]{1,0:T(8,128)(2,1)S(1)} %collective-permute-done.17.refs_2_), channel_id=1, source_target_pairs={{0,128},{128,0},{1,129},{129,1},{2,130},{130,2},{3,131},{131,3},{4... | collective-permute-start | bytes 786440 | tf_op jit(solution)/shard_map/ppermute | solution.py:53
  59.0 0.9 collective-permute-done.10.refs_0_
  60.0 0.8 collective-permute-start.16
  60.8 1.7 %collective-permute-start.19 = (bf16[256,512]{1,0:T(8,128)(2,1)S(1)}, bf16[256,512]{1,0:T(8,128)(2,1)S(1)}, u32[]{:S(2)}, u32[]{:S(2)}) collective-permute-start(bf16[256,512]{1,0:T(8,128)(2,1)S(1)} %get-tuple-element.38.refs_1_), channel_id=1, source_target_pairs={{0,112},{16,0},{32,16},{48,32},{64,48},{80,64},{96,80},{112,96},{1... | collective-permute-start | bytes 786440 | tf_op jit(solution)/shard_map/ppermute | solution.py:53
  62.7 0.9 collective-permute-start.15
  63.6 2.3 %collective-permute-start.20 = (bf16[256,512]{1,0:T(8,128)(2,1)S(1)}, bf16[256,512]{1,0:T(8,128)(2,1)S(1)}, u32[]{:S(2)}, u32[]{:S(2)}) collective-permute-start(bf16[256,512]{1,0:T(8,128)(2,1)S(1)} %get-tuple-element.40), channel_id=1, source_target_pairs={{0,18},{2,20},{4,22},{6,16},{16,34},{18,36},{20,38},{22,32},{32,50... | collective-permute-start | bytes 786440 | tf_op jit(solution)/shard_map/ppermute | solution.py:53
  65.9 2.7 %shard_map.113.refs_5_ = f32[1280,512]{1,0:T(8,128)S(1)} custom-call(bf16[640,8192]{1,0:T(8,128)(2,1)S(1)} %shard_map.103.refs_3_.own, bf16[640,8192]{1,0:T(8,128)(2,1)S(1)} %shard_map.104.refs_2_.sib, bf16[512,512]{1,0:T(8,128)(2,1)S(1)} %get-tuple-element.41.refs_0_, ...), custom_call_target="tpu_custom_call", output_to_operand_aliasing={{}: (7, {})} | custom-call | flops 2348810240 | bytes 1835008 | tf_op jit(solution)/shard_map/pallas_call | solution.py:264
  68.6 1.7 %collective-permute-done.15.refs_0_ = bf16[256,512]{1,0:T(8,128)(2,1)S(1)} collective-permute-done((bf16[256,512]{1,0:T(8,128)(2,1)S(1)}, bf16[256,512]{1,0:T(8,128)(2,1)S(1)}, u32[]{:S(2)}, u32[]{:S(2)}) %collective-permute-start.15) | collective-permute-done | bytes 262176 | tf_op jit(solution)/shard_map/ppermute | solution.py:53
  70.3 1.8 %collective-permute-done.20.refs_4_ = bf16[256,512]{1,0:T(8,128)(2,1)S(1)} collective-permute-done((bf16[256,512]{1,0:T(8,128)(2,1)S(1)}, bf16[256,512]{1,0:T(8,128)(2,1)S(1)}, u32[]{:S(2)}, u32[]{:S(2)}) %collective-permute-start.20) | collective-permute-done | bytes 262176 | tf_op jit(solution)/shard_map/ppermute | solution.py:53
  72.1 2.7 %shard_map.114 = (f32[1280,512]{1,0:T(8,128)S(1)}, f32[64,4,128]{2,1,0:T(4,128)S(1)}) custom-call(bf16[640,8192]{1,0:T(8,128)(2,1)S(1)} %shard_map.103.refs_3_.own, bf16[640,8192]{1,0:T(8,128)(2,1)S(1)} %shard_map.104.refs_2_.sib, bf16[256,512]{1,0:T(8,128)(2,1)S(1)} %collective-permute-done.15.refs_0_, ...), custom_call_target="tpu_custom_call" | custom-call | flops 1677721600 | bytes 1310720 | tf_op jit(solution)/shard_map/pallas_call | solution.py:264
  74.8 21.1 %all_to_all.15.squares = f32[64,4,128]{2,1,0:T(4,128)S(1)} all-to-all(f32[64,4,128]{2,1,0:T(4,128)S(1)} %get-tuple-element.43), channel_id=1, replica_groups=mesh['yh'=2,'z'=8,'tp'=2,'x'=4,'core'=2] {'x','z','yh'}, dimensions={0} | all-to-all | bytes 262144 | tf_op jit(solution)/shard_map/all_to_all | solution.py:534
  95.9 1.1 shard_map.115
  97.0 4.7 %collective-permute-start.23 = (bf16[1280,128]{1,0:T(8,128)(2,1)S(1)}, bf16[1280,128]{1,0:T(8,128)(2,1)S(1)}, u32[]{:S(2)}, u32[]{:S(2)}) collective-permute-start(bf16[1280,128]{1,0:T(8,128)(2,1)S(1)} %get-tuple-element.44), channel_id=1, source_target_pairs={{0,0},{2,2},{4,12},{6,14},{8,4},{10,6},{12,8},{14,10},{1,1},{3,3},... | collective-permute-start | bytes 983048 | tf_op jit(solution)/shard_map/ppermute | solution.py:543
  101.8 1.8 %collective-permute-start.24 = (bf16[1280,128]{1,0:T(8,128)(2,1)S(1)}, bf16[1280,128]{1,0:T(8,128)(2,1)S(1)}, u32[]{:S(2)}, u32[]{:S(2)}) collective-permute-start(bf16[1280,128]{1,0:T(8,128)(2,1)S(1)} %get-tuple-element.45), channel_id=1, source_target_pairs={{0,2},{2,4},{4,14},{6,8},{8,6},{10,0},{12,10},{14,12},{1,3},{3,5},... | collective-permute-start | bytes 983048 | tf_op jit(solution)/shard_map/ppermute | solution.py:543
  103.6 1.9 %collective-permute-start.25 = (bf16[1280,128]{1,0:T(8,128)(2,1)S(1)}, bf16[1280,128]{1,0:T(8,128)(2,1)S(1)}, u32[]{:S(2)}, u32[]{:S(2)}) collective-permute-start(bf16[1280,128]{1,0:T(8,128)(2,1)S(1)} %get-tuple-element.46), channel_id=1, source_target_pairs={{0,4},{2,6},{4,8},{6,10},{8,0},{10,2},{12,12},{14,14},{1,5},{3,7},... | collective-permute-start | bytes 983048 | tf_op jit(solution)/shard_map/ppermute | solution.py:543
  105.6 2.9 %collective-permute-start.27 = (f32[1,512]{1,0:T(1,128)S(1)}, f32[1,512]{1,0:T(1,128)S(1)}, u32[]{:S(2)}, u32[]{:S(2)}) collective-permute-start(f32[1,512]{1,0:T(1,128)S(1)} %get-tuple-element.48.own_scale), channel_id=1, source_target_pairs={{0,8},{8,0},{1,9},{9,1},{2,10},{10,2},{3,11},{11,3},{4,12},{12,4},... | collective-permute-start | bytes 6152 | tf_op jit(solution)/shard_map/ppermute | solution.py:53
  108.7 1.6 %collective-permute-done.27.other_scale = f32[1,512]{1,0:T(1,128)S(1)} collective-permute-done((f32[1,512]{1,0:T(1,128)S(1)}, f32[1,512]{1,0:T(1,128)S(1)}, u32[]{:S(2)}, u32[]{:S(2)}) %collective-permute-start.27) | collective-permute-done | bytes 2080 | tf_op jit(solution)/shard_map/ppermute | solution.py:53
  110.3 1.7 %collective-permute-done.24.r1 = bf16[1280,128]{1,0:T(8,128)(2,1)S(1)} collective-permute-done((bf16[1280,128]{1,0:T(8,128)(2,1)S(1)}, bf16[1280,128]{1,0:T(8,128)(2,1)S(1)}, u32[]{:S(2)}, u32[]{:S(2)}) %collective-permute-start.24) | collective-permute-done | bytes 327712 | tf_op jit(solution)/shard_map/ppermute | solution.py:543
  112.0 2.1 %collective-permute-done.25.r2 = bf16[1280,128]{1,0:T(8,128)(2,1)S(1)} collective-permute-done((bf16[1280,128]{1,0:T(8,128)(2,1)S(1)}, bf16[1280,128]{1,0:T(8,128)(2,1)S(1)}, u32[]{:S(2)}, u32[]{:S(2)}) %collective-permute-start.25) | collective-permute-done | bytes 327712 | tf_op jit(solution)/shard_map/ppermute | solution.py:543
  114.1 3.4 %collective-permute-done.26.r3 = bf16[1280,128]{1,0:T(8,128)(2,1)S(1)} collective-permute-done((bf16[1280,128]{1,0:T(8,128)(2,1)S(1)}, bf16[1280,128]{1,0:T(8,128)(2,1)S(1)}, u32[]{:S(2)}, u32[]{:S(2)}) %collective-permute-start.26) | collective-permute-done | bytes 327712 | tf_op jit(solution)/shard_map/ppermute | solution.py:543
  117.5 3.7 %shard_map.116 = (bf16[2,10,256,128]{3,2,1,0:T(8,128)(2,1)}, f32[16,40,128]{2,1,0:T(8,128)S(1)}) custom-call(s32[10]{0:T(128)S(1)} %copy-done.6, bf16[1280,128]{1,0:T(8,128)(2,1)S(1)} %collective-permute-done.23.r0, bf16[1280,128]{1,0:T(8,128)(2,1)S(1)} %collective-permute-done.24.r1, bf16[1280,128]{1,0:T(8,128)(2,1)S(1)} %collective-permute-done.25.r2, ...), custom_call_target="tpu_custom_call" | custom-call | flops 671088640 | bytes 2621440 | tf_op jit(solution)/shard_map/pallas_call | solution.py:379
  121.3 13.9 %all_to_all.16.parts = f32[16,40,128]{2,1,0:T(8,128)S(1)} all-to-all(f32[16,40,128]{2,1,0:T(8,128)S(1)} %get-tuple-element.50), channel_id=1, replica_groups=mesh['yh'=2,'z'=8,'tp'=2,'x'=4,'core'=2] {'z','tp'}, dimensions={0} | all-to-all | bytes 655360 | tf_op jit(solution)/shard_map/all_to_all | solution.py:552
  135.2 1.1 shard_map.117
  136.3 3.9 %all-to-all-start.2 = ((bf16[32,32,128]{2,1,0:T(8,128)(2,1)}), bf16[32,32,128]{2,1,0:T(8,128)(2,1)S(1)}, u32[]{:S(2)}, u32[]{:S(2)}) async-start(bf16[32,32,128]{2,1,0:T(8,128)(2,1)} %shard_map.117), calls=%async_computation.2 | async-start | bytes 524288 | tf_op jit(solution)/shard_map/all_to_all | solution.py:554
  140.3 1.2 collective-permute-done.28.far
  141.4 11.1 %all-to-all-done.2.whole = bf16[32,32,128]{2,1,0:T(8,128)(2,1)S(1)} async-done(((bf16[32,32,128]{2,1,0:T(8,128)(2,1)}), bf16[32,32,128]{2,1,0:T(8,128)(2,1)S(1)}, u32[]{:S(2)}, u32[]{:S(2)}) %all-to-all-start.2) | async-done | bytes 262176 | tf_op jit(solution)/shard_map/all_to_all | solution.py:554
  152.6 0.8 shard_map.118
  (48 shorter events, 2.7 us)
Async XLA Ops:
  0.6 24.0 %collective-permute-start = (bf16[640,8192]{1,0:T(8,128)(2,1)}, bf16[640,8192]{1,0:T(8,128)(2,1)S(1)}, u32[]{:S(2)}, u32[]{:S(2)}) collective-permute-start(bf16[640,8192]{1,0:T(8,128)(2,1)} %source.1), channel_id=1, source_target_pairs={{0,1},{1,0},{2,3},{3,2},{4,5},{5,4},{6,7},{7,6},{8,9},{9,8},{10,11... | collective-permute-start | bytes 31457288 | tf_op jit(solution)/shard_map/ppermute | solution.py:53
  0.7 1.2 copy-start
  2.1 13.1 %collective-permute-start.1 = (bf16[256,512]{1,0:T(8,128)(2,1)S(1)}, bf16[256,512]{1,0:T(8,128)(2,1)S(1)}, u32[]{:S(2)}, u32[]{:S(2)}) collective-permute-start(bf16[256,512]{1,0:T(8,128)(2,1)S(1)} %shard_map.105), channel_id=1, source_target_pairs={{0,128},{128,0},{1,129},{129,1},{2,130},{130,2},{3,131},{131,3},{4... | collective-permute-start | bytes 786440 | tf_op jit(solution)/shard_map/ppermute | solution.py:53
  5.4 12.5 %collective-permute-start.2 = (bf16[256,512]{1,0:T(8,128)(2,1)S(1)}, bf16[256,512]{1,0:T(8,128)(2,1)S(1)}, u32[]{:S(2)}, u32[]{:S(2)}) collective-permute-start(bf16[256,512]{1,0:T(8,128)(2,1)S(1)} %shard_map.105), channel_id=1, source_target_pairs={{0,16},{16,32},{32,48},{48,64},{64,80},{80,96},{96,112},{112,0},{1... | collective-permute-start | bytes 786440 | tf_op jit(solution)/shard_map/ppermute | solution.py:53
  7.3 10.6 %collective-permute-start.3 = (bf16[256,512]{1,0:T(8,128)(2,1)S(1)}, bf16[256,512]{1,0:T(8,128)(2,1)S(1)}, u32[]{:S(2)}, u32[]{:S(2)}) collective-permute-start(bf16[256,512]{1,0:T(8,128)(2,1)S(1)} %shard_map.105), channel_id=1, source_target_pairs={{0,112},{16,0},{32,16},{48,32},{64,48},{80,64},{96,80},{112,96},{1... | collective-permute-start | bytes 786440 | tf_op jit(solution)/shard_map/ppermute | solution.py:53
  18.0 14.8 %collective-permute-start.4 = (bf16[512,512]{1,0:T(8,128)(2,1)S(1)}, bf16[512,512]{1,0:T(8,128)(2,1)S(1)}, u32[]{:S(2)}, u32[]{:S(2)}) collective-permute-start(bf16[512,512]{1,0:T(8,128)(2,1)S(1)} %get-tuple-element.28.refs_1_), channel_id=1, source_target_pairs={{0,16},{16,32},{32,48},{48,64},{64,80},{80,96},{96,112},{112,0},{1... | collective-permute-start | bytes 1572872 | tf_op jit(solution)/shard_map/ppermute | solution.py:53
  18.1 14.7 %collective-permute-start.5 = (bf16[512,512]{1,0:T(8,128)(2,1)S(1)}, bf16[512,512]{1,0:T(8,128)(2,1)S(1)}, u32[]{:S(2)}, u32[]{:S(2)}) collective-permute-start(bf16[512,512]{1,0:T(8,128)(2,1)S(1)} %get-tuple-element.29), channel_id=1, source_target_pairs={{0,112},{16,0},{32,16},{48,32},{64,48},{80,64},{96,80},{112,96},{1... | collective-permute-start | bytes 1572872 | tf_op jit(solution)/shard_map/ppermute | solution.py:53
  21.3 14.9 %collective-permute-start.8 = (bf16[512,512]{1,0:T(8,128)(2,1)S(1)}, bf16[512,512]{1,0:T(8,128)(2,1)S(1)}, u32[]{:S(2)}, u32[]{:S(2)}) collective-permute-start(bf16[512,512]{1,0:T(8,128)(2,1)S(1)} %get-tuple-element.28.refs_1_), channel_id=1, source_target_pairs={{0,6},{2,0},{4,2},{6,4},{1,7},{3,1},{5,3},{7,5},{8,14},{10,8},{12,... | collective-permute-start | bytes 1572872 | tf_op jit(solution)/shard_map/ppermute | solution.py:53
  22.2 15.2 %collective-permute-start.9 = (bf16[256,512]{1,0:T(8,128)(2,1)S(1)}, bf16[256,512]{1,0:T(8,128)(2,1)S(1)}, u32[]{:S(2)}, u32[]{:S(2)}) collective-permute-start(bf16[256,512]{1,0:T(8,128)(2,1)S(1)} %get-tuple-element.32.refs_2_), channel_id=1, source_target_pairs={{0,2},{2,4},{4,6},{6,0},{1,3},{3,5},{5,7},{7,1},{8,10},{10,12},{12... | collective-permute-start | bytes 786440 | tf_op jit(solution)/shard_map/ppermute | solution.py:53
  25.3 13.7 %copy-start.1 = (bf16[512,1024]{1,0:T(8,128)(2,1)S(1)}, bf16[512,1024]{1,0:T(8,128)(2,1)}, u32[]{:S(2)}) copy-start(bf16[512,1024]{1,0:T(8,128)(2,1)} %refs_0_.1) | copy-start | bytes 3145732
  32.9 13.9 %collective-permute-start.6 = (bf16[512,512]{1,0:T(8,128)(2,1)S(1)}, bf16[512,512]{1,0:T(8,128)(2,1)S(1)}, u32[]{:S(2)}, u32[]{:S(2)}) collective-permute-start(bf16[512,512]{1,0:T(8,128)(2,1)S(1)} %get-tuple-element.30.refs_5_), channel_id=1, source_target_pairs={{0,16},{16,32},{32,48},{48,64},{64,80},{80,96},{96,112},{112,0},{1... | collective-permute-start | bytes 1572872 | tf_op jit(solution)/shard_map/ppermute | solution.py:53
  34.8 12.0 %collective-permute-start.7 = (bf16[512,512]{1,0:T(8,128)(2,1)S(1)}, bf16[512,512]{1,0:T(8,128)(2,1)S(1)}, u32[]{:S(2)}, u32[]{:S(2)}) collective-permute-start(bf16[512,512]{1,0:T(8,128)(2,1)S(1)} %get-tuple-element.31.refs_6_), channel_id=1, source_target_pairs={{0,112},{16,0},{32,16},{48,32},{64,48},{80,64},{96,80},{112,96},{1... | collective-permute-start | bytes 1572872 | tf_op jit(solution)/shard_map/ppermute | solution.py:53
  36.2 12.7 %collective-permute-start.14 = (bf16[256,512]{1,0:T(8,128)(2,1)S(1)}, bf16[256,512]{1,0:T(8,128)(2,1)S(1)}, u32[]{:S(2)}, u32[]{:S(2)}) collective-permute-start(bf16[256,512]{1,0:T(8,128)(2,1)S(1)} %shard_map.110), channel_id=1, source_target_pairs={{0,128},{128,0},{1,129},{129,1},{2,130},{130,2},{3,131},{131,3},{4... | collective-permute-start | bytes 786440 | tf_op jit(solution)/shard_map/ppermute | solution.py:53
  36.9 15.3 %collective-permute-start.13 = (bf16[512,512]{1,0:T(8,128)(2,1)S(1)}, bf16[512,512]{1,0:T(8,128)(2,1)S(1)}, u32[]{:S(2)}, u32[]{:S(2)}) collective-permute-start(bf16[512,512]{1,0:T(8,128)(2,1)S(1)} %get-tuple-element.31.refs_6_), channel_id=1, source_target_pairs={{0,2},{2,4},{4,6},{6,0},{1,3},{3,5},{5,7},{7,1},{8,10},{10,12},{12... | collective-permute-start | bytes 1572872 | tf_op jit(solution)/shard_map/ppermute | solution.py:53
  37.4 13.1 %collective-permute-start.12 = (bf16[256,512]{1,0:T(8,128)(2,1)S(1)}, bf16[256,512]{1,0:T(8,128)(2,1)S(1)}, u32[]{:S(2)}, u32[]{:S(2)}) collective-permute-start(bf16[256,512]{1,0:T(8,128)(2,1)S(1)} %get-tuple-element.36), channel_id=1, source_target_pairs={{0,6},{2,0},{4,2},{6,4},{1,7},{3,1},{5,3},{7,5},{8,14},{10,8},{12,... | collective-permute-start | bytes 786440 | tf_op jit(solution)/shard_map/ppermute | solution.py:53
  46.9 13.0 %collective-permute-start.10 = (bf16[512,512]{1,0:T(8,128)(2,1)S(1)}, bf16[512,512]{1,0:T(8,128)(2,1)S(1)}, u32[]{:S(2)}, u32[]{:S(2)}) collective-permute-start(bf16[512,512]{1,0:T(8,128)(2,1)S(1)} %get-tuple-element.33.refs_0_), channel_id=1, source_target_pairs={{0,16},{16,32},{32,48},{48,64},{64,80},{80,96},{96,112},{112,0},{1... | collective-permute-start | bytes 1572872 | tf_op jit(solution)/shard_map/ppermute | solution.py:53
  48.5 15.1 %collective-permute-start.21 = (bf16[512,512]{1,0:T(8,128)(2,1)S(1)}, bf16[512,512]{1,0:T(8,128)(2,1)S(1)}, u32[]{:S(2)}, u32[]{:S(2)}) collective-permute-start(bf16[512,512]{1,0:T(8,128)(2,1)S(1)} %get-tuple-element.35.refs_1_), channel_id=1, source_target_pairs={{0,2},{2,4},{4,6},{6,0},{1,3},{3,5},{5,7},{7,1},{8,10},{10,12},{12... | collective-permute-start | bytes 1572872 | tf_op jit(solution)/shard_map/ppermute | solution.py:53
  49.0 7.8 %collective-permute-start.17 = (bf16[256,512]{1,0:T(8,128)(2,1)S(1)}, bf16[256,512]{1,0:T(8,128)(2,1)S(1)}, u32[]{:S(2)}, u32[]{:S(2)}) collective-permute-start(bf16[256,512]{1,0:T(8,128)(2,1)S(1)} %get-tuple-element.39), channel_id=1, source_target_pairs={{0,6},{2,0},{4,2},{6,4},{1,7},{3,1},{5,3},{7,5},{8,14},{10,8},{12,... | collective-permute-start | bytes 786440 | tf_op jit(solution)/shard_map/ppermute | solution.py:53
  50.5 8.5 %collective-permute-start.11 = (bf16[256,512]{1,0:T(8,128)(2,1)S(1)}, bf16[256,512]{1,0:T(8,128)(2,1)S(1)}, u32[]{:S(2)}, u32[]{:S(2)}) collective-permute-start(bf16[256,512]{1,0:T(8,128)(2,1)S(1)} %get-tuple-element.34), channel_id=1, source_target_pairs={{0,112},{16,0},{32,16},{48,32},{64,48},{80,64},{96,80},{112,96},{1... | collective-permute-start | bytes 786440 | tf_op jit(solution)/shard_map/ppermute | solution.py:53
  52.3 10.4 %collective-permute-start.22 = (bf16[256,512]{1,0:T(8,128)(2,1)S(1)}, bf16[256,512]{1,0:T(8,128)(2,1)S(1)}, u32[]{:S(2)}, u32[]{:S(2)}) collective-permute-start(bf16[256,512]{1,0:T(8,128)(2,1)S(1)} %collective-permute-done.12.refs_2_), channel_id=1, source_target_pairs={{0,128},{128,0},{1,129},{129,1},{2,130},{130,2},{3,131},{131,3},{4... | collective-permute-start | bytes 786440 | tf_op jit(solution)/shard_map/ppermute | solution.py:53
  56.8 11.8 %collective-permute-start.18 = (bf16[256,512]{1,0:T(8,128)(2,1)S(1)}, bf16[256,512]{1,0:T(8,128)(2,1)S(1)}, u32[]{:S(2)}, u32[]{:S(2)}) collective-permute-start(bf16[256,512]{1,0:T(8,128)(2,1)S(1)} %collective-permute-done.17.refs_2_), channel_id=1, source_target_pairs={{0,128},{128,0},{1,129},{129,1},{2,130},{130,2},{3,131},{131,3},{4... | collective-permute-start | bytes 786440 | tf_op jit(solution)/shard_map/ppermute | solution.py:53
  60.0 10.3 %collective-permute-start.16 = (bf16[256,512]{1,0:T(8,128)(2,1)S(1)}, bf16[256,512]{1,0:T(8,128)(2,1)S(1)}, u32[]{:S(2)}, u32[]{:S(2)}) collective-permute-start(bf16[256,512]{1,0:T(8,128)(2,1)S(1)} %get-tuple-element.38.refs_1_), channel_id=1, source_target_pairs={{0,2},{2,4},{4,6},{6,0},{1,3},{3,5},{5,7},{7,1},{8,10},{10,12},{12... | collective-permute-start | bytes 786440 | tf_op jit(solution)/shard_map/ppermute | solution.py:53
  60.8 9.5 %collective-permute-start.19 = (bf16[256,512]{1,0:T(8,128)(2,1)S(1)}, bf16[256,512]{1,0:T(8,128)(2,1)S(1)}, u32[]{:S(2)}, u32[]{:S(2)}) collective-permute-start(bf16[256,512]{1,0:T(8,128)(2,1)S(1)} %get-tuple-element.38.refs_1_), channel_id=1, source_target_pairs={{0,112},{16,0},{32,16},{48,32},{64,48},{80,64},{96,80},{112,96},{1... | collective-permute-start | bytes 786440 | tf_op jit(solution)/shard_map/ppermute | solution.py:53
  62.7 7.6 %collective-permute-start.15 = (bf16[256,512]{1,0:T(8,128)(2,1)S(1)}, bf16[256,512]{1,0:T(8,128)(2,1)S(1)}, u32[]{:S(2)}, u32[]{:S(2)}) collective-permute-start(bf16[256,512]{1,0:T(8,128)(2,1)S(1)} %get-tuple-element.37), channel_id=1, source_target_pairs={{0,6},{2,0},{4,2},{6,4},{1,7},{3,1},{5,3},{7,5},{8,14},{10,8},{12,... | collective-permute-start | bytes 786440 | tf_op jit(solution)/shard_map/ppermute | solution.py:53
  63.6 8.5 %collective-permute-start.20 = (bf16[256,512]{1,0:T(8,128)(2,1)S(1)}, bf16[256,512]{1,0:T(8,128)(2,1)S(1)}, u32[]{:S(2)}, u32[]{:S(2)}) collective-permute-start(bf16[256,512]{1,0:T(8,128)(2,1)S(1)} %get-tuple-element.40), channel_id=1, source_target_pairs={{0,18},{2,20},{4,22},{6,16},{16,34},{18,36},{20,38},{22,32},{32,50... | collective-permute-start | bytes 786440 | tf_op jit(solution)/shard_map/ppermute | solution.py:53
  65.9 6.2 %copy-start.5 = (s32[2]{0:T(128)S(1)}, s32[2]{0:T(128)}, u32[]{:S(2)}) copy-start(s32[2]{0:T(128)} %lengths.1) | copy-start | bytes 28
  74.8 33.8 %copy-start.7 = (s32[2,64]{1,0:T(2,128)S(1)}, s32[2,64]{1,0:T(2,128)}, u32[]{:S(2)}) copy-start(s32[2,64]{1,0:T(2,128)} %param.15) | copy-start | bytes 1540
  74.8 42.8 %copy-start.2 = (bf16[2,64,1024]{2,1,0:T(8,128)(2,1)S(1)}, bf16[2,64,1024]{2,1,0:T(8,128)(2,1)}, u32[]{:S(2)}) copy-start(bf16[2,64,1024]{2,1,0:T(8,128)(2,1)} %query.3) | copy-start | bytes 786436
  74.8 42.8 %copy-start.6 = (s32[10]{0:T(128)S(1)}, s32[10]{0:T(128)}, u32[]{:S(2)}) copy-start(s32[10]{0:T(128)} %pages.1) | copy-start | bytes 124
  95.9 39.3 %copy-start.3 = (bf16[2,64,128]{2,1,0:T(8,128)(2,1)S(1)}, bf16[2,64,128]{2,1,0:T(8,128)(2,1)}, u32[]{:S(2)}) copy-start(bf16[2,64,128]{2,1,0:T(8,128)(2,1)} %new_key.1) | copy-start | bytes 98308
  95.9 39.3 %copy-start.4 = (bf16[2,64,128]{2,1,0:T(8,128)(2,1)S(1)}, bf16[2,64,128]{2,1,0:T(8,128)(2,1)}, u32[]{:S(2)}) copy-start(bf16[2,64,128]{2,1,0:T(8,128)(2,1)} %new_value.1) | copy-start | bytes 98308
  97.0 13.3 %collective-permute-start.23 = (bf16[1280,128]{1,0:T(8,128)(2,1)S(1)}, bf16[1280,128]{1,0:T(8,128)(2,1)S(1)}, u32[]{:S(2)}, u32[]{:S(2)}) collective-permute-start(bf16[1280,128]{1,0:T(8,128)(2,1)S(1)} %get-tuple-element.44), channel_id=1, source_target_pairs={{0,0},{2,2},{4,12},{6,14},{8,4},{10,6},{12,8},{14,10},{1,1},{3,3},... | collective-permute-start | bytes 983048 | tf_op jit(solution)/shard_map/ppermute | solution.py:543
  101.8 10.3 %collective-permute-start.24 = (bf16[1280,128]{1,0:T(8,128)(2,1)S(1)}, bf16[1280,128]{1,0:T(8,128)(2,1)S(1)}, u32[]{:S(2)}, u32[]{:S(2)}) collective-permute-start(bf16[1280,128]{1,0:T(8,128)(2,1)S(1)} %get-tuple-element.45), channel_id=1, source_target_pairs={{0,2},{2,4},{4,14},{6,8},{8,6},{10,0},{12,10},{14,12},{1,3},{3,5},... | collective-permute-start | bytes 983048 | tf_op jit(solution)/shard_map/ppermute | solution.py:543
  103.6 10.6 %collective-permute-start.25 = (bf16[1280,128]{1,0:T(8,128)(2,1)S(1)}, bf16[1280,128]{1,0:T(8,128)(2,1)S(1)}, u32[]{:S(2)}, u32[]{:S(2)}) collective-permute-start(bf16[1280,128]{1,0:T(8,128)(2,1)S(1)} %get-tuple-element.46), channel_id=1, source_target_pairs={{0,4},{2,6},{4,8},{6,10},{8,0},{10,2},{12,12},{14,14},{1,5},{3,7},... | collective-permute-start | bytes 983048 | tf_op jit(solution)/shard_map/ppermute | solution.py:543
  105.5 12.0 %collective-permute-start.26 = (bf16[1280,128]{1,0:T(8,128)(2,1)S(1)}, bf16[1280,128]{1,0:T(8,128)(2,1)S(1)}, u32[]{:S(2)}, u32[]{:S(2)}) collective-permute-start(bf16[1280,128]{1,0:T(8,128)(2,1)S(1)} %get-tuple-element.47), channel_id=1, source_target_pairs={{0,6},{2,0},{4,10},{6,12},{8,2},{10,4},{12,14},{14,8},{1,7},{3,1},... | collective-permute-start | bytes 983048 | tf_op jit(solution)/shard_map/ppermute | solution.py:543
  105.6 4.7 %collective-permute-start.27 = (f32[1,512]{1,0:T(1,128)S(1)}, f32[1,512]{1,0:T(1,128)S(1)}, u32[]{:S(2)}, u32[]{:S(2)}) collective-permute-start(f32[1,512]{1,0:T(1,128)S(1)} %get-tuple-element.48.own_scale), channel_id=1, source_target_pairs={{0,8},{8,0},{1,9},{9,1},{2,10},{10,2},{3,11},{11,3},{4,12},{12,4},... | collective-permute-start | bytes 6152 | tf_op jit(solution)/shard_map/ppermute | solution.py:53
  136.3 16.3 %all-to-all-start.2 = ((bf16[32,32,128]{2,1,0:T(8,128)(2,1)}), bf16[32,32,128]{2,1,0:T(8,128)(2,1)S(1)}, u32[]{:S(2)}, u32[]{:S(2)}) async-start(bf16[32,32,128]{2,1,0:T(8,128)(2,1)} %shard_map.117), calls=%async_computation.2 | async-start | bytes 524288 | tf_op jit(solution)/shard_map/all_to_all | solution.py:554
  140.2 1.3 collective-permute-start.28

commit v5 on v4

--- a/solution.py
+++ b/solution.py
@@ -304,7 +304,7 @@
 
 
 def attend_kernel(
-    pages, r0, r1, r2, r3, query, limits, own_scale, other_scale, cache, part, held, tops, totals, sems
+    pages, r0, r1, r2, r3, query, limits, own_scale, other_scale, cache, part, held, sums, tops, totals, sems
 ):
     yh, z, x, tp = [lax.axis_index(name) for name in ("yh", "z", "x", "tp")]
     got = (r0, r1, r2, r3)
@@ -356,7 +356,7 @@
             for block in range(8):
                 source = slice(side * 64 + block * 8, side * 64 + block * 8 + 8)
                 target = 2 * block + g // 4, slice((g % 4) * 8, (g % 4) * 8 + 8)
-                part[target] = summed[source]
+                sums[target] = summed[source]
                 tops[target], totals[target] = [
                     jnp.broadcast_to(value[source], (8, HD)) for value in (top, total)
                 ]
@@ -364,10 +364,16 @@
         jnp.int32, (32, HD), 1
     )
     for share in range(16):
-        for at, column in enumerate((tops, totals)):
-            part[share, 32 + at : 33 + at] = jnp.sum(
-                jnp.where(here, column[share], 0.0), axis=0, keepdims=True
-            )
+        part[share, 0:32] = sums[share].astype(part.dtype)
+        lines = []
+        for column in (tops, totals):
+            line = jnp.sum(jnp.where(here, column[share], 0.0), axis=0, keepdims=True)
+            for _ in range(3):
+                piece = line.astype(jnp.bfloat16).astype(jnp.float32)
+                lines.append(piece)
+                line = line - piece
+        lines.append(jnp.zeros((10, HD), jnp.float32))
+        part[share, 32:48] = jnp.concatenate(lines, axis=0).astype(part.dtype)
     for copy in copies:
         copy.wait()
 
@@ -384,11 +390,12 @@
             pltpu.VMEM((2, 2 * rows, HD), jnp.bfloat16),
             pltpu.VMEM((16, 32, HD), jnp.float32),
             pltpu.VMEM((16, 32, HD), jnp.float32),
+            pltpu.VMEM((16, 32, HD), jnp.float32),
             pltpu.SemaphoreType.DMA((2, pages)),
         ],
         out_shape=[
             jax.ShapeDtypeStruct((2, pages, PAGE, HD), jnp.bfloat16),
-            jax.ShapeDtypeStruct((16, 40, HD), jnp.float32),
+            jax.ShapeDtypeStruct((16, 48, HD), jnp.bfloat16),
         ],
         compiler_params=params(VMEM),
         cost_estimate=cost(8 * heads * rows * HD, 16 * rows * HD, 2 * heads * rows),
@@ -417,15 +424,20 @@
     here = lax.broadcasted_iota(jnp.int32, (1, 32, HD), 1) == lax.broadcasted_iota(
         jnp.int32, (1, 32, HD), 2
     )
+    lines = parts[:, 32:48, :].astype(jnp.float32)
     top, total = [
-        jnp.sum(jnp.where(here, parts[:, at : at + 1, :], 0.0), axis=2, keepdims=True)
-        for at in (32, 33)
+        jnp.sum(
+            jnp.where(here, lines[:, at : at + 1] + lines[:, at + 1 : at + 2] + lines[:, at + 2 : at + 3], 0.0),
+            axis=2,
+            keepdims=True,
+        )
+        for at in (0, 3)
     ]
     overall = jnp.maximum(jnp.max(top, axis=0), own)
     factor = jnp.exp(top - overall[None])
     own_weight = jnp.exp(own - overall)
     denominator = jnp.sum(total * factor, axis=0) + own_weight
-    summed = jnp.sum(parts[:, :32, :] * factor, axis=0)
+    summed = jnp.sum(parts[:, :32, :].astype(jnp.float32) * factor, axis=0)
     result = (summed * scale + own_weight * value) / denominator
     out[...] = jnp.broadcast_to(result.astype(out.dtype)[None], out.shape)
 

time: 154 us -> 153 us (level)
  no operation moved by 1% of the time
where the time goes in v5:
time: 153 us; the launch traced here: 152 us
  starting transfers between devices  51.9 us (34%)
  waiting for transfers between devices  39.3 us (26%)
  blocking collectives  33.9 us (22%)
  Pallas kernels  24.8 us (16%)
    ppermute x25, starting transfers between devices, send(): return lax.ppermute(value, names if len(names) > 1 else names[0], pairs)  39.5 us
    all_to_all x1, blocking collectives, body(): squares = lax.all_to_all(squares, ('x', 'z', 'yh'), 0, 0, tiled=True)  21.1 us
    ppermute x25, waiting for transfers between devices, send(): return lax.ppermute(value, names if len(names) > 1 else names[0], pairs)  20.9 us
    pallas_call x4, Pallas kernels, project(): pl.pallas_call(functools.partial(project_kernel, names, acc is not None,...  13 us
    all_to_all x1, blocking collectives, body(): parts = lax.all_to_all(part, ('z', 'tp'), 0, 0, tiled=True)  12.8 us
    all_to_all x1, waiting for transfers between devices, body(): whole = lax.all_to_all(result, ('yh', 'z', 'tp'), 0, 0, tiled=True)  11.1 us
    ppermute x4, starting transfers between devices, body(): received.append(lax.ppermute(sent[k], ('tp', 'x'), pairs))  8.55 us
    ppermute x4, waiting for transfers between devices, body(): received.append(lax.ppermute(sent[k], ('tp', 'x'), pairs))  7.24 us
  transfers between devices with their start and end apart: 30, of which 13 were waited for; matrix products, arithmetic and copies ran while one was open for 0% of the time, Pallas kernels for 10%

profile of v5, /device:TPU:6, one launch (start us, length us, event | category | flops | bytes accessed | tf_op | source)
XLA Modules:
  0.0 152.3 jit_solution(13702087075090167793)
XLA Ops:
  0.7 1.2 copy-done
  2.1 3.3 %collective-permute-start.1 = (bf16[256,512]{1,0:T(8,128)(2,1)S(1)}, bf16[256,512]{1,0:T(8,128)(2,1)S(1)}, u32[]{:S(2)}, u32[]{:S(2)}) collective-permute-start(bf16[256,512]{1,0:T(8,128)(2,1)S(1)} %shard_map.105), channel_id=1, source_target_pairs={{0,128},{128,0},{1,129},{129,1},{2,130},{130,2},{3,131},{131,3},{4... | collective-permute-start | bytes 786440 | tf_op jit(solution)/shard_map/ppermute | solution.py:53
  5.4 1.9 %collective-permute-start.2 = (bf16[256,512]{1,0:T(8,128)(2,1)S(1)}, bf16[256,512]{1,0:T(8,128)(2,1)S(1)}, u32[]{:S(2)}, u32[]{:S(2)}) collective-permute-start(bf16[256,512]{1,0:T(8,128)(2,1)S(1)} %shard_map.105), channel_id=1, source_target_pairs={{0,16},{16,32},{32,48},{48,64},{64,80},{80,96},{96,112},{112,0},{1... | collective-permute-start | bytes 786440 | tf_op jit(solution)/shard_map/ppermute | solution.py:53
  7.3 3.9 %collective-permute-start.3 = (bf16[256,512]{1,0:T(8,128)(2,1)S(1)}, bf16[256,512]{1,0:T(8,128)(2,1)S(1)}, u32[]{:S(2)}, u32[]{:S(2)}) collective-permute-start(bf16[256,512]{1,0:T(8,128)(2,1)S(1)} %shard_map.105), channel_id=1, source_target_pairs={{0,112},{16,0},{32,16},{48,32},{64,48},{80,64},{96,80},{112,96},{1... | collective-permute-start | bytes 786440 | tf_op jit(solution)/shard_map/ppermute | solution.py:53
  11.2 4.0 %shard_map.103.refs_3_.own = bf16[640,8192]{1,0:T(8,128)(2,1)S(1)} custom-call(bf16[640,8192]{1,0:T(8,128)(2,1)} %source.1), custom_call_target="tpu_custom_call" | custom-call | bytes 20971520 | tf_op jit(solution)/shard_map/pallas_call | solution.py:124
  15.2 2.7 %collective-permute-done.2.refs_1_ = bf16[256,512]{1,0:T(8,128)(2,1)S(1)} collective-permute-done((bf16[256,512]{1,0:T(8,128)(2,1)S(1)}, bf16[256,512]{1,0:T(8,128)(2,1)S(1)}, u32[]{:S(2)}, u32[]{:S(2)}) %collective-permute-start.2) | collective-permute-done | bytes 262176 | tf_op jit(solution)/shard_map/ppermute | solution.py:53
  18.1 3.2 %collective-permute-start.5 = (bf16[512,512]{1,0:T(8,128)(2,1)S(1)}, bf16[512,512]{1,0:T(8,128)(2,1)S(1)}, u32[]{:S(2)}, u32[]{:S(2)}) collective-permute-start(bf16[512,512]{1,0:T(8,128)(2,1)S(1)} %get-tuple-element.29), channel_id=1, source_target_pairs={{0,112},{16,0},{32,16},{48,32},{64,48},{80,64},{96,80},{112,96},{1... | collective-permute-start | bytes 1572872 | tf_op jit(solution)/shard_map/ppermute | solution.py:53
  21.3 0.8 collective-permute-start.8
  22.2 2.4 %collective-permute-start.9 = (bf16[256,512]{1,0:T(8,128)(2,1)S(1)}, bf16[256,512]{1,0:T(8,128)(2,1)S(1)}, u32[]{:S(2)}, u32[]{:S(2)}) collective-permute-start(bf16[256,512]{1,0:T(8,128)(2,1)S(1)} %get-tuple-element.32.refs_2_), channel_id=1, source_target_pairs={{0,2},{2,4},{4,6},{6,0},{1,3},{3,5},{5,7},{7,1},{8,10},{10,12},{12... | collective-permute-start | bytes 786440 | tf_op jit(solution)/shard_map/ppermute | solution.py:53
  24.6 0.7 shard_map.104.refs_2_.sib
  25.3 7.5 %collective-permute-done.4.refs_0_ = bf16[512,512]{1,0:T(8,128)(2,1)S(1)} collective-permute-done((bf16[512,512]{1,0:T(8,128)(2,1)S(1)}, bf16[512,512]{1,0:T(8,128)(2,1)S(1)}, u32[]{:S(2)}, u32[]{:S(2)}) %collective-permute-start.4) | collective-permute-done | bytes 524320 | tf_op jit(solution)/shard_map/ppermute | solution.py:53
  32.9 1.9 %collective-permute-start.6 = (bf16[512,512]{1,0:T(8,128)(2,1)S(1)}, bf16[512,512]{1,0:T(8,128)(2,1)S(1)}, u32[]{:S(2)}, u32[]{:S(2)}) collective-permute-start(bf16[512,512]{1,0:T(8,128)(2,1)S(1)} %get-tuple-element.30.refs_5_), channel_id=1, source_target_pairs={{0,16},{16,32},{32,48},{48,64},{64,80},{80,96},{96,112},{112,0},{1... | collective-permute-start | bytes 1572872 | tf_op jit(solution)/shard_map/ppermute | solution.py:53
  34.8 1.4 collective-permute-start.7
  37.4 1.5 %collective-permute-start.12 = (bf16[256,512]{1,0:T(8,128)(2,1)S(1)}, bf16[256,512]{1,0:T(8,128)(2,1)S(1)}, u32[]{:S(2)}, u32[]{:S(2)}) collective-permute-start(bf16[256,512]{1,0:T(8,128)(2,1)S(1)} %get-tuple-element.36), channel_id=1, source_target_pairs={{0,6},{2,0},{4,2},{6,4},{1,7},{3,1},{5,3},{7,5},{8,14},{10,8},{12,... | collective-permute-start | bytes 786440 | tf_op jit(solution)/shard_map/ppermute | solution.py:53
  38.9 4.5 %shard_map.108.refs_2_.refs_5_ = f32[1280,512]{1,0:T(8,128)S(1)} custom-call(bf16[640,8192]{1,0:T(8,128)(2,1)S(1)} %shard_map.103.refs_3_.own, bf16[640,8192]{1,0:T(8,128)(2,1)S(1)} %shard_map.104.refs_2_.sib, bf16[512,1024]{1,0:T(8,128)(2,1)S(1)} %copy-done.1, bf16[512,512]{1,0:T(8,128)(2,1)S(1)} %get-tuple-element.28.refs_1_, ...), custom_call_target="tpu_custom_call" | custom-call | flops 4026531840 | bytes 3145728 | tf_op jit(solution)/shard_map/pallas_call | solution.py:264
  43.5 3.4 %collective-permute-done.6.refs_0_ = bf16[512,512]{1,0:T(8,128)(2,1)S(1)} collective-permute-done((bf16[512,512]{1,0:T(8,128)(2,1)S(1)}, bf16[512,512]{1,0:T(8,128)(2,1)S(1)}, u32[]{:S(2)}, u32[]{:S(2)}) %collective-permute-start.6) | collective-permute-done | bytes 524320 | tf_op jit(solution)/shard_map/ppermute | solution.py:53
  46.9 1.6 %collective-permute-start.10 = (bf16[512,512]{1,0:T(8,128)(2,1)S(1)}, bf16[512,512]{1,0:T(8,128)(2,1)S(1)}, u32[]{:S(2)}, u32[]{:S(2)}) collective-permute-start(bf16[512,512]{1,0:T(8,128)(2,1)S(1)} %get-tuple-element.33.refs_0_), channel_id=1, source_target_pairs={{0,16},{16,32},{32,48},{48,64},{64,80},{80,96},{96,112},{112,0},{1... | collective-permute-start | bytes 1572872 | tf_op jit(solution)/shard_map/ppermute | solution.py:53
  49.0 1.5 %collective-permute-start.17 = (bf16[256,512]{1,0:T(8,128)(2,1)S(1)}, bf16[256,512]{1,0:T(8,128)(2,1)S(1)}, u32[]{:S(2)}, u32[]{:S(2)}) collective-permute-start(bf16[256,512]{1,0:T(8,128)(2,1)S(1)} %get-tuple-element.39), channel_id=1, source_target_pairs={{0,6},{2,0},{4,2},{6,4},{1,7},{3,1},{5,3},{7,5},{8,14},{10,8},{12,... | collective-permute-start | bytes 786440 | tf_op jit(solution)/shard_map/ppermute | solution.py:53
  50.5 1.7 %collective-permute-start.11 = (bf16[256,512]{1,0:T(8,128)(2,1)S(1)}, bf16[256,512]{1,0:T(8,128)(2,1)S(1)}, u32[]{:S(2)}, u32[]{:S(2)}) collective-permute-start(bf16[256,512]{1,0:T(8,128)(2,1)S(1)} %get-tuple-element.34), channel_id=1, source_target_pairs={{0,112},{16,0},{32,16},{48,32},{64,48},{80,64},{96,80},{112,96},{1... | collective-permute-start | bytes 786440 | tf_op jit(solution)/shard_map/ppermute | solution.py:53
  52.3 1.4 collective-permute-start.22
  53.7 3.1 %shard_map.111.refs_2_.refs_5_ = f32[1280,512]{1,0:T(8,128)S(1)} custom-call(bf16[640,8192]{1,0:T(8,128)(2,1)S(1)} %shard_map.103.refs_3_.own, bf16[640,8192]{1,0:T(8,128)(2,1)S(1)} %shard_map.104.refs_2_.sib, bf16[512,512]{1,0:T(8,128)(2,1)S(1)} %get-tuple-element.33.refs_0_, ...), custom_call_target="tpu_custom_call", output_to_operand_aliasing={{}: (7, {})} | custom-call | flops 2684354560 | bytes 2097152 | tf_op jit(solution)/shard_map/pallas_call | solution.py:264
  56.8 2.2 %collective-permute-start.18 = (bf16[256,512]{1,0:T(8,128)(2,1)S(1)}, bf16[256,512]{1,0:T(8,128)(2,1)S(1)}, u32[]{:S(2)}, u32[]{:S(2)}) collective-permute-start(bf16[256,512]{1,0:T(8,128)(2,1)S(1)} %collective-permute-done.17.refs_2_), channel_id=1, source_target_pairs={{0,128},{128,0},{1,129},{129,1},{2,130},{130,2},{3,131},{131,3},{4... | collective-permute-start | bytes 786440 | tf_op jit(solution)/shard_map/ppermute | solution.py:53
  59.0 0.9 collective-permute-done.10.refs_0_
  60.0 0.8 collective-permute-start.16
  60.8 1.7 %collective-permute-start.19 = (bf16[256,512]{1,0:T(8,128)(2,1)S(1)}, bf16[256,512]{1,0:T(8,128)(2,1)S(1)}, u32[]{:S(2)}, u32[]{:S(2)}) collective-permute-start(bf16[256,512]{1,0:T(8,128)(2,1)S(1)} %get-tuple-element.38.refs_1_), channel_id=1, source_target_pairs={{0,112},{16,0},{32,16},{48,32},{64,48},{80,64},{96,80},{112,96},{1... | collective-permute-start | bytes 786440 | tf_op jit(solution)/shard_map/ppermute | solution.py:53
  62.7 0.9 collective-permute-start.15
  63.6 2.3 %collective-permute-start.20 = (bf16[256,512]{1,0:T(8,128)(2,1)S(1)}, bf16[256,512]{1,0:T(8,128)(2,1)S(1)}, u32[]{:S(2)}, u32[]{:S(2)}) collective-permute-start(bf16[256,512]{1,0:T(8,128)(2,1)S(1)} %get-tuple-element.40), channel_id=1, source_target_pairs={{0,18},{2,20},{4,22},{6,16},{16,34},{18,36},{20,38},{22,32},{32,50... | collective-permute-start | bytes 786440 | tf_op jit(solution)/shard_map/ppermute | solution.py:53
  65.9 2.7 %shard_map.113.refs_5_ = f32[1280,512]{1,0:T(8,128)S(1)} custom-call(bf16[640,8192]{1,0:T(8,128)(2,1)S(1)} %shard_map.103.refs_3_.own, bf16[640,8192]{1,0:T(8,128)(2,1)S(1)} %shard_map.104.refs_2_.sib, bf16[512,512]{1,0:T(8,128)(2,1)S(1)} %get-tuple-element.41.refs_0_, ...), custom_call_target="tpu_custom_call", output_to_operand_aliasing={{}: (7, {})} | custom-call | flops 2348810240 | bytes 1835008 | tf_op jit(solution)/shard_map/pallas_call | solution.py:264
  68.6 1.7 %collective-permute-done.15.refs_0_ = bf16[256,512]{1,0:T(8,128)(2,1)S(1)} collective-permute-done((bf16[256,512]{1,0:T(8,128)(2,1)S(1)}, bf16[256,512]{1,0:T(8,128)(2,1)S(1)}, u32[]{:S(2)}, u32[]{:S(2)}) %collective-permute-start.15) | collective-permute-done | bytes 262176 | tf_op jit(solution)/shard_map/ppermute | solution.py:53
  70.3 1.8 %collective-permute-done.20.refs_4_ = bf16[256,512]{1,0:T(8,128)(2,1)S(1)} collective-permute-done((bf16[256,512]{1,0:T(8,128)(2,1)S(1)}, bf16[256,512]{1,0:T(8,128)(2,1)S(1)}, u32[]{:S(2)}, u32[]{:S(2)}) %collective-permute-start.20) | collective-permute-done | bytes 262176 | tf_op jit(solution)/shard_map/ppermute | solution.py:53
  72.1 2.7 %shard_map.114 = (f32[1280,512]{1,0:T(8,128)S(1)}, f32[64,4,128]{2,1,0:T(4,128)S(1)}) custom-call(bf16[640,8192]{1,0:T(8,128)(2,1)S(1)} %shard_map.103.refs_3_.own, bf16[640,8192]{1,0:T(8,128)(2,1)S(1)} %shard_map.104.refs_2_.sib, bf16[256,512]{1,0:T(8,128)(2,1)S(1)} %collective-permute-done.15.refs_0_, ...), custom_call_target="tpu_custom_call" | custom-call | flops 1677721600 | bytes 1310720 | tf_op jit(solution)/shard_map/pallas_call | solution.py:264
  74.8 21.1 %all_to_all.15.squares = f32[64,4,128]{2,1,0:T(4,128)S(1)} all-to-all(f32[64,4,128]{2,1,0:T(4,128)S(1)} %get-tuple-element.43), channel_id=1, replica_groups=mesh['yh'=2,'z'=8,'tp'=2,'x'=4,'core'=2] {'x','z','yh'}, dimensions={0} | all-to-all | bytes 262144 | tf_op jit(solution)/shard_map/all_to_all | solution.py:546
  95.9 1.1 shard_map.115
  97.0 4.7 %collective-permute-start.23 = (bf16[1280,128]{1,0:T(8,128)(2,1)S(1)}, bf16[1280,128]{1,0:T(8,128)(2,1)S(1)}, u32[]{:S(2)}, u32[]{:S(2)}) collective-permute-start(bf16[1280,128]{1,0:T(8,128)(2,1)S(1)} %get-tuple-element.44), channel_id=1, source_target_pairs={{0,0},{2,2},{4,12},{6,14},{8,4},{10,6},{12,8},{14,10},{1,1},{3,3},... | collective-permute-start | bytes 983048 | tf_op jit(solution)/shard_map/ppermute | solution.py:555
  101.8 1.8 %collective-permute-start.24 = (bf16[1280,128]{1,0:T(8,128)(2,1)S(1)}, bf16[1280,128]{1,0:T(8,128)(2,1)S(1)}, u32[]{:S(2)}, u32[]{:S(2)}) collective-permute-start(bf16[1280,128]{1,0:T(8,128)(2,1)S(1)} %get-tuple-element.45), channel_id=1, source_target_pairs={{0,2},{2,4},{4,14},{6,8},{8,6},{10,0},{12,10},{14,12},{1,3},{3,5},... | collective-permute-start | bytes 983048 | tf_op jit(solution)/shard_map/ppermute | solution.py:555
  103.6 1.9 %collective-permute-start.25 = (bf16[1280,128]{1,0:T(8,128)(2,1)S(1)}, bf16[1280,128]{1,0:T(8,128)(2,1)S(1)}, u32[]{:S(2)}, u32[]{:S(2)}) collective-permute-start(bf16[1280,128]{1,0:T(8,128)(2,1)S(1)} %get-tuple-element.46), channel_id=1, source_target_pairs={{0,4},{2,6},{4,8},{6,10},{8,0},{10,2},{12,12},{14,14},{1,5},{3,7},... | collective-permute-start | bytes 983048 | tf_op jit(solution)/shard_map/ppermute | solution.py:555
  105.6 2.9 %collective-permute-start.27 = (f32[1,512]{1,0:T(1,128)S(1)}, f32[1,512]{1,0:T(1,128)S(1)}, u32[]{:S(2)}, u32[]{:S(2)}) collective-permute-start(f32[1,512]{1,0:T(1,128)S(1)} %get-tuple-element.48.own_scale), channel_id=1, source_target_pairs={{0,8},{8,0},{1,9},{9,1},{2,10},{10,2},{3,11},{11,3},{4,12},{12,4},... | collective-permute-start | bytes 6152 | tf_op jit(solution)/shard_map/ppermute | solution.py:53
  108.7 1.6 %collective-permute-done.27.other_scale = f32[1,512]{1,0:T(1,128)S(1)} collective-permute-done((f32[1,512]{1,0:T(1,128)S(1)}, f32[1,512]{1,0:T(1,128)S(1)}, u32[]{:S(2)}, u32[]{:S(2)}) %collective-permute-start.27) | collective-permute-done | bytes 2080 | tf_op jit(solution)/shard_map/ppermute | solution.py:53
  110.3 1.7 %collective-permute-done.24.r1 = bf16[1280,128]{1,0:T(8,128)(2,1)S(1)} collective-permute-done((bf16[1280,128]{1,0:T(8,128)(2,1)S(1)}, bf16[1280,128]{1,0:T(8,128)(2,1)S(1)}, u32[]{:S(2)}, u32[]{:S(2)}) %collective-permute-start.24) | collective-permute-done | bytes 327712 | tf_op jit(solution)/shard_map/ppermute | solution.py:555
  112.0 2.1 %collective-permute-done.25.r2 = bf16[1280,128]{1,0:T(8,128)(2,1)S(1)} collective-permute-done((bf16[1280,128]{1,0:T(8,128)(2,1)S(1)}, bf16[1280,128]{1,0:T(8,128)(2,1)S(1)}, u32[]{:S(2)}, u32[]{:S(2)}) %collective-permute-start.25) | collective-permute-done | bytes 327712 | tf_op jit(solution)/shard_map/ppermute | solution.py:555
  114.1 3.4 %collective-permute-done.26.r3 = bf16[1280,128]{1,0:T(8,128)(2,1)S(1)} collective-permute-done((bf16[1280,128]{1,0:T(8,128)(2,1)S(1)}, bf16[1280,128]{1,0:T(8,128)(2,1)S(1)}, u32[]{:S(2)}, u32[]{:S(2)}) %collective-permute-start.26) | collective-permute-done | bytes 327712 | tf_op jit(solution)/shard_map/ppermute | solution.py:555
  117.5 3.8 %shard_map.116 = (bf16[2,10,256,128]{3,2,1,0:T(8,128)(2,1)}, bf16[16,48,128]{2,1,0:T(8,128)(2,1)S(1)}) custom-call(s32[10]{0:T(128)S(1)} %copy-done.6, bf16[1280,128]{1,0:T(8,128)(2,1)S(1)} %collective-permute-done.23.r0, bf16[1280,128]{1,0:T(8,128)(2,1)S(1)} %collective-permute-done.24.r1, bf16[1280,128]{1,0:T(8,128)(2,1)S(1)} %collective-permute-done.25.r2, ...), custom_call_target="tpu_custom_call" | custom-call | flops 671088640 | bytes 2621440 | tf_op jit(solution)/shard_map/pallas_call | solution.py:385
  121.3 12.8 %all_to_all.16.parts = bf16[16,48,128]{2,1,0:T(8,128)(2,1)S(1)} all-to-all(bf16[16,48,128]{2,1,0:T(8,128)(2,1)S(1)} %get-tuple-element.50), channel_id=1, replica_groups=mesh['yh'=2,'z'=8,'tp'=2,'x'=4,'core'=2] {'z','tp'}, dimensions={0} | all-to-all | bytes 393216 | tf_op jit(solution)/shard_map/all_to_all | solution.py:564
  134.1 1.1 shard_map.117
  135.2 3.9 %all-to-all-start.2 = ((bf16[32,32,128]{2,1,0:T(8,128)(2,1)}), bf16[32,32,128]{2,1,0:T(8,128)(2,1)S(1)}, u32[]{:S(2)}, u32[]{:S(2)}) async-start(bf16[32,32,128]{2,1,0:T(8,128)(2,1)} %shard_map.117), calls=%async_computation.2 | async-start | bytes 524288 | tf_op jit(solution)/shard_map/all_to_all | solution.py:566
  139.2 1.2 collective-permute-done.28.far
  140.4 11.1 %all-to-all-done.2.whole = bf16[32,32,128]{2,1,0:T(8,128)(2,1)S(1)} async-done(((bf16[32,32,128]{2,1,0:T(8,128)(2,1)}), bf16[32,32,128]{2,1,0:T(8,128)(2,1)S(1)}, u32[]{:S(2)}, u32[]{:S(2)}) %all-to-all-start.2) | async-done | bytes 262176 | tf_op jit(solution)/shard_map/all_to_all | solution.py:566
  151.5 0.8 shard_map.118
  (48 shorter events, 2.7 us)
Async XLA Ops:
  0.6 24.0 %collective-permute-start = (bf16[640,8192]{1,0:T(8,128)(2,1)}, bf16[640,8192]{1,0:T(8,128)(2,1)S(1)}, u32[]{:S(2)}, u32[]{:S(2)}) collective-permute-start(bf16[640,8192]{1,0:T(8,128)(2,1)} %source.1), channel_id=1, source_target_pairs={{0,1},{1,0},{2,3},{3,2},{4,5},{5,4},{6,7},{7,6},{8,9},{9,8},{10,11... | collective-permute-start | bytes 31457288 | tf_op jit(solution)/shard_map/ppermute | solution.py:53
  0.7 1.2 copy-start
  2.1 13.1 %collective-permute-start.1 = (bf16[256,512]{1,0:T(8,128)(2,1)S(1)}, bf16[256,512]{1,0:T(8,128)(2,1)S(1)}, u32[]{:S(2)}, u32[]{:S(2)}) collective-permute-start(bf16[256,512]{1,0:T(8,128)(2,1)S(1)} %shard_map.105), channel_id=1, source_target_pairs={{0,128},{128,0},{1,129},{129,1},{2,130},{130,2},{3,131},{131,3},{4... | collective-permute-start | bytes 786440 | tf_op jit(solution)/shard_map/ppermute | solution.py:53
  5.4 12.5 %collective-permute-start.2 = (bf16[256,512]{1,0:T(8,128)(2,1)S(1)}, bf16[256,512]{1,0:T(8,128)(2,1)S(1)}, u32[]{:S(2)}, u32[]{:S(2)}) collective-permute-start(bf16[256,512]{1,0:T(8,128)(2,1)S(1)} %shard_map.105), channel_id=1, source_target_pairs={{0,16},{16,32},{32,48},{48,64},{64,80},{80,96},{96,112},{112,0},{1... | collective-permute-start | bytes 786440 | tf_op jit(solution)/shard_map/ppermute | solution.py:53
  7.3 10.6 %collective-permute-start.3 = (bf16[256,512]{1,0:T(8,128)(2,1)S(1)}, bf16[256,512]{1,0:T(8,128)(2,1)S(1)}, u32[]{:S(2)}, u32[]{:S(2)}) collective-permute-start(bf16[256,512]{1,0:T(8,128)(2,1)S(1)} %shard_map.105), channel_id=1, source_target_pairs={{0,112},{16,0},{32,16},{48,32},{64,48},{80,64},{96,80},{112,96},{1... | collective-permute-start | bytes 786440 | tf_op jit(solution)/shard_map/ppermute | solution.py:53
  18.0 14.8 %collective-permute-start.4 = (bf16[512,512]{1,0:T(8,128)(2,1)S(1)}, bf16[512,512]{1,0:T(8,128)(2,1)S(1)}, u32[]{:S(2)}, u32[]{:S(2)}) collective-permute-start(bf16[512,512]{1,0:T(8,128)(2,1)S(1)} %get-tuple-element.28.refs_1_), channel_id=1, source_target_pairs={{0,16},{16,32},{32,48},{48,64},{64,80},{80,96},{96,112},{112,0},{1... | collective-permute-start | bytes 1572872 | tf_op jit(solution)/shard_map/ppermute | solution.py:53
  18.1 14.7 %collective-permute-start.5 = (bf16[512,512]{1,0:T(8,128)(2,1)S(1)}, bf16[512,512]{1,0:T(8,128)(2,1)S(1)}, u32[]{:S(2)}, u32[]{:S(2)}) collective-permute-start(bf16[512,512]{1,0:T(8,128)(2,1)S(1)} %get-tuple-element.29), channel_id=1, source_target_pairs={{0,112},{16,0},{32,16},{48,32},{64,48},{80,64},{96,80},{112,96},{1... | collective-permute-start | bytes 1572872 | tf_op jit(solution)/shard_map/ppermute | solution.py:53
  21.3 14.9 %collective-permute-start.8 = (bf16[512,512]{1,0:T(8,128)(2,1)S(1)}, bf16[512,512]{1,0:T(8,128)(2,1)S(1)}, u32[]{:S(2)}, u32[]{:S(2)}) collective-permute-start(bf16[512,512]{1,0:T(8,128)(2,1)S(1)} %get-tuple-element.28.refs_1_), channel_id=1, source_target_pairs={{0,6},{2,0},{4,2},{6,4},{1,7},{3,1},{5,3},{7,5},{8,14},{10,8},{12,... | collective-permute-start | bytes 1572872 | tf_op jit(solution)/shard_map/ppermute | solution.py:53
  22.2 15.2 %collective-permute-start.9 = (bf16[256,512]{1,0:T(8,128)(2,1)S(1)}, bf16[256,512]{1,0:T(8,128)(2,1)S(1)}, u32[]{:S(2)}, u32[]{:S(2)}) collective-permute-start(bf16[256,512]{1,0:T(8,128)(2,1)S(1)} %get-tuple-element.32.refs_2_), channel_id=1, source_target_pairs={{0,2},{2,4},{4,6},{6,0},{1,3},{3,5},{5,7},{7,1},{8,10},{10,12},{12... | collective-permute-start | bytes 786440 | tf_op jit(solution)/shard_map/ppermute | solution.py:53
  25.3 13.7 %copy-start.1 = (bf16[512,1024]{1,0:T(8,128)(2,1)S(1)}, bf16[512,1024]{1,0:T(8,128)(2,1)}, u32[]{:S(2)}) copy-start(bf16[512,1024]{1,0:T(8,128)(2,1)} %refs_0_.1) | copy-start | bytes 3145732
  32.9 13.9 %collective-permute-start.6 = (bf16[512,512]{1,0:T(8,128)(2,1)S(1)}, bf16[512,512]{1,0:T(8,128)(2,1)S(1)}, u32[]{:S(2)}, u32[]{:S(2)}) collective-permute-start(bf16[512,512]{1,0:T(8,128)(2,1)S(1)} %get-tuple-element.30.refs_5_), channel_id=1, source_target_pairs={{0,16},{16,32},{32,48},{48,64},{64,80},{80,96},{96,112},{112,0},{1... | collective-permute-start | bytes 1572872 | tf_op jit(solution)/shard_map/ppermute | solution.py:53
  34.8 12.0 %collective-permute-start.7 = (bf16[512,512]{1,0:T(8,128)(2,1)S(1)}, bf16[512,512]{1,0:T(8,128)(2,1)S(1)}, u32[]{:S(2)}, u32[]{:S(2)}) collective-permute-start(bf16[512,512]{1,0:T(8,128)(2,1)S(1)} %get-tuple-element.31.refs_6_), channel_id=1, source_target_pairs={{0,112},{16,0},{32,16},{48,32},{64,48},{80,64},{96,80},{112,96},{1... | collective-permute-start | bytes 1572872 | tf_op jit(solution)/shard_map/ppermute | solution.py:53
  36.2 12.7 %collective-permute-start.14 = (bf16[256,512]{1,0:T(8,128)(2,1)S(1)}, bf16[256,512]{1,0:T(8,128)(2,1)S(1)}, u32[]{:S(2)}, u32[]{:S(2)}) collective-permute-start(bf16[256,512]{1,0:T(8,128)(2,1)S(1)} %shard_map.110), channel_id=1, source_target_pairs={{0,128},{128,0},{1,129},{129,1},{2,130},{130,2},{3,131},{131,3},{4... | collective-permute-start | bytes 786440 | tf_op jit(solution)/shard_map/ppermute | solution.py:53
  36.9 15.3 %collective-permute-start.13 = (bf16[512,512]{1,0:T(8,128)(2,1)S(1)}, bf16[512,512]{1,0:T(8,128)(2,1)S(1)}, u32[]{:S(2)}, u32[]{:S(2)}) collective-permute-start(bf16[512,512]{1,0:T(8,128)(2,1)S(1)} %get-tuple-element.31.refs_6_), channel_id=1, source_target_pairs={{0,2},{2,4},{4,6},{6,0},{1,3},{3,5},{5,7},{7,1},{8,10},{10,12},{12... | collective-permute-start | bytes 1572872 | tf_op jit(solution)/shard_map/ppermute | solution.py:53
  37.4 13.1 %collective-permute-start.12 = (bf16[256,512]{1,0:T(8,128)(2,1)S(1)}, bf16[256,512]{1,0:T(8,128)(2,1)S(1)}, u32[]{:S(2)}, u32[]{:S(2)}) collective-permute-start(bf16[256,512]{1,0:T(8,128)(2,1)S(1)} %get-tuple-element.36), channel_id=1, source_target_pairs={{0,6},{2,0},{4,2},{6,4},{1,7},{3,1},{5,3},{7,5},{8,14},{10,8},{12,... | collective-permute-start | bytes 786440 | tf_op jit(solution)/shard_map/ppermute | solution.py:53
  46.9 13.0 %collective-permute-start.10 = (bf16[512,512]{1,0:T(8,128)(2,1)S(1)}, bf16[512,512]{1,0:T(8,128)(2,1)S(1)}, u32[]{:S(2)}, u32[]{:S(2)}) collective-permute-start(bf16[512,512]{1,0:T(8,128)(2,1)S(1)} %get-tuple-element.33.refs_0_), channel_id=1, source_target_pairs={{0,16},{16,32},{32,48},{48,64},{64,80},{80,96},{96,112},{112,0},{1... | collective-permute-start | bytes 1572872 | tf_op jit(solution)/shard_map/ppermute | solution.py:53
  48.5 15.1 %collective-permute-start.21 = (bf16[512,512]{1,0:T(8,128)(2,1)S(1)}, bf16[512,512]{1,0:T(8,128)(2,1)S(1)}, u32[]{:S(2)}, u32[]{:S(2)}) collective-permute-start(bf16[512,512]{1,0:T(8,128)(2,1)S(1)} %get-tuple-element.35.refs_1_), channel_id=1, source_target_pairs={{0,2},{2,4},{4,6},{6,0},{1,3},{3,5},{5,7},{7,1},{8,10},{10,12},{12... | collective-permute-start | bytes 1572872 | tf_op jit(solution)/shard_map/ppermute | solution.py:53
  49.0 7.8 %collective-permute-start.17 = (bf16[256,512]{1,0:T(8,128)(2,1)S(1)}, bf16[256,512]{1,0:T(8,128)(2,1)S(1)}, u32[]{:S(2)}, u32[]{:S(2)}) collective-permute-start(bf16[256,512]{1,0:T(8,128)(2,1)S(1)} %get-tuple-element.39), channel_id=1, source_target_pairs={{0,6},{2,0},{4,2},{6,4},{1,7},{3,1},{5,3},{7,5},{8,14},{10,8},{12,... | collective-permute-start | bytes 786440 | tf_op jit(solution)/shard_map/ppermute | solution.py:53
  50.5 8.5 %collective-permute-start.11 = (bf16[256,512]{1,0:T(8,128)(2,1)S(1)}, bf16[256,512]{1,0:T(8,128)(2,1)S(1)}, u32[]{:S(2)}, u32[]{:S(2)}) collective-permute-start(bf16[256,512]{1,0:T(8,128)(2,1)S(1)} %get-tuple-element.34), channel_id=1, source_target_pairs={{0,112},{16,0},{32,16},{48,32},{64,48},{80,64},{96,80},{112,96},{1... | collective-permute-start | bytes 786440 | tf_op jit(solution)/shard_map/ppermute | solution.py:53
  52.3 10.4 %collective-permute-start.22 = (bf16[256,512]{1,0:T(8,128)(2,1)S(1)}, bf16[256,512]{1,0:T(8,128)(2,1)S(1)}, u32[]{:S(2)}, u32[]{:S(2)}) collective-permute-start(bf16[256,512]{1,0:T(8,128)(2,1)S(1)} %collective-permute-done.12.refs_2_), channel_id=1, source_target_pairs={{0,128},{128,0},{1,129},{129,1},{2,130},{130,2},{3,131},{131,3},{4... | collective-permute-start | bytes 786440 | tf_op jit(solution)/shard_map/ppermute | solution.py:53
  56.8 11.8 %collective-permute-start.18 = (bf16[256,512]{1,0:T(8,128)(2,1)S(1)}, bf16[256,512]{1,0:T(8,128)(2,1)S(1)}, u32[]{:S(2)}, u32[]{:S(2)}) collective-permute-start(bf16[256,512]{1,0:T(8,128)(2,1)S(1)} %collective-permute-done.17.refs_2_), channel_id=1, source_target_pairs={{0,128},{128,0},{1,129},{129,1},{2,130},{130,2},{3,131},{131,3},{4... | collective-permute-start | bytes 786440 | tf_op jit(solution)/shard_map/ppermute | solution.py:53
  60.0 10.3 %collective-permute-start.16 = (bf16[256,512]{1,0:T(8,128)(2,1)S(1)}, bf16[256,512]{1,0:T(8,128)(2,1)S(1)}, u32[]{:S(2)}, u32[]{:S(2)}) collective-permute-start(bf16[256,512]{1,0:T(8,128)(2,1)S(1)} %get-tuple-element.38.refs_1_), channel_id=1, source_target_pairs={{0,2},{2,4},{4,6},{6,0},{1,3},{3,5},{5,7},{7,1},{8,10},{10,12},{12... | collective-permute-start | bytes 786440 | tf_op jit(solution)/shard_map/ppermute | solution.py:53
  60.8 9.5 %collective-permute-start.19 = (bf16[256,512]{1,0:T(8,128)(2,1)S(1)}, bf16[256,512]{1,0:T(8,128)(2,1)S(1)}, u32[]{:S(2)}, u32[]{:S(2)}) collective-permute-start(bf16[256,512]{1,0:T(8,128)(2,1)S(1)} %get-tuple-element.38.refs_1_), channel_id=1, source_target_pairs={{0,112},{16,0},{32,16},{48,32},{64,48},{80,64},{96,80},{112,96},{1... | collective-permute-start | bytes 786440 | tf_op jit(solution)/shard_map/ppermute | solution.py:53
  62.7 7.6 %collective-permute-start.15 = (bf16[256,512]{1,0:T(8,128)(2,1)S(1)}, bf16[256,512]{1,0:T(8,128)(2,1)S(1)}, u32[]{:S(2)}, u32[]{:S(2)}) collective-permute-start(bf16[256,512]{1,0:T(8,128)(2,1)S(1)} %get-tuple-element.37), channel_id=1, source_target_pairs={{0,6},{2,0},{4,2},{6,4},{1,7},{3,1},{5,3},{7,5},{8,14},{10,8},{12,... | collective-permute-start | bytes 786440 | tf_op jit(solution)/shard_map/ppermute | solution.py:53
  63.6 8.5 %collective-permute-start.20 = (bf16[256,512]{1,0:T(8,128)(2,1)S(1)}, bf16[256,512]{1,0:T(8,128)(2,1)S(1)}, u32[]{:S(2)}, u32[]{:S(2)}) collective-permute-start(bf16[256,512]{1,0:T(8,128)(2,1)S(1)} %get-tuple-element.40), channel_id=1, source_target_pairs={{0,18},{2,20},{4,22},{6,16},{16,34},{18,36},{20,38},{22,32},{32,50... | collective-permute-start | bytes 786440 | tf_op jit(solution)/shard_map/ppermute | solution.py:53
  65.9 6.2 %copy-start.5 = (s32[2]{0:T(128)S(1)}, s32[2]{0:T(128)}, u32[]{:S(2)}) copy-start(s32[2]{0:T(128)} %lengths.1) | copy-start | bytes 28
  74.8 33.8 %copy-start.7 = (s32[2,64]{1,0:T(2,128)S(1)}, s32[2,64]{1,0:T(2,128)}, u32[]{:S(2)}) copy-start(s32[2,64]{1,0:T(2,128)} %param.15) | copy-start | bytes 1540
  74.8 42.8 %copy-start.2 = (bf16[2,64,1024]{2,1,0:T(8,128)(2,1)S(1)}, bf16[2,64,1024]{2,1,0:T(8,128)(2,1)}, u32[]{:S(2)}) copy-start(bf16[2,64,1024]{2,1,0:T(8,128)(2,1)} %query.3) | copy-start | bytes 786436
  74.8 42.8 %copy-start.6 = (s32[10]{0:T(128)S(1)}, s32[10]{0:T(128)}, u32[]{:S(2)}) copy-start(s32[10]{0:T(128)} %pages.1) | copy-start | bytes 124
  95.9 38.2 %copy-start.3 = (bf16[2,64,128]{2,1,0:T(8,128)(2,1)S(1)}, bf16[2,64,128]{2,1,0:T(8,128)(2,1)}, u32[]{:S(2)}) copy-start(bf16[2,64,128]{2,1,0:T(8,128)(2,1)} %new_key.1) | copy-start | bytes 98308
  95.9 38.2 %copy-start.4 = (bf16[2,64,128]{2,1,0:T(8,128)(2,1)S(1)}, bf16[2,64,128]{2,1,0:T(8,128)(2,1)}, u32[]{:S(2)}) copy-start(bf16[2,64,128]{2,1,0:T(8,128)(2,1)} %new_value.1) | copy-start | bytes 98308
  97.0 13.3 %collective-permute-start.23 = (bf16[1280,128]{1,0:T(8,128)(2,1)S(1)}, bf16[1280,128]{1,0:T(8,128)(2,1)S(1)}, u32[]{:S(2)}, u32[]{:S(2)}) collective-permute-start(bf16[1280,128]{1,0:T(8,128)(2,1)S(1)} %get-tuple-element.44), channel_id=1, source_target_pairs={{0,0},{2,2},{4,12},{6,14},{8,4},{10,6},{12,8},{14,10},{1,1},{3,3},... | collective-permute-start | bytes 983048 | tf_op jit(solution)/shard_map/ppermute | solution.py:555
  101.8 10.3 %collective-permute-start.24 = (bf16[1280,128]{1,0:T(8,128)(2,1)S(1)}, bf16[1280,128]{1,0:T(8,128)(2,1)S(1)}, u32[]{:S(2)}, u32[]{:S(2)}) collective-permute-start(bf16[1280,128]{1,0:T(8,128)(2,1)S(1)} %get-tuple-element.45), channel_id=1, source_target_pairs={{0,2},{2,4},{4,14},{6,8},{8,6},{10,0},{12,10},{14,12},{1,3},{3,5},... | collective-permute-start | bytes 983048 | tf_op jit(solution)/shard_map/ppermute | solution.py:555
  103.6 10.6 %collective-permute-start.25 = (bf16[1280,128]{1,0:T(8,128)(2,1)S(1)}, bf16[1280,128]{1,0:T(8,128)(2,1)S(1)}, u32[]{:S(2)}, u32[]{:S(2)}) collective-permute-start(bf16[1280,128]{1,0:T(8,128)(2,1)S(1)} %get-tuple-element.46), channel_id=1, source_target_pairs={{0,4},{2,6},{4,8},{6,10},{8,0},{10,2},{12,12},{14,14},{1,5},{3,7},... | collective-permute-start | bytes 983048 | tf_op jit(solution)/shard_map/ppermute | solution.py:555
  105.5 12.0 %collective-permute-start.26 = (bf16[1280,128]{1,0:T(8,128)(2,1)S(1)}, bf16[1280,128]{1,0:T(8,128)(2,1)S(1)}, u32[]{:S(2)}, u32[]{:S(2)}) collective-permute-start(bf16[1280,128]{1,0:T(8,128)(2,1)S(1)} %get-tuple-element.47), channel_id=1, source_target_pairs={{0,6},{2,0},{4,10},{6,12},{8,2},{10,4},{12,14},{14,8},{1,7},{3,1},... | collective-permute-start | bytes 983048 | tf_op jit(solution)/shard_map/ppermute | solution.py:555
  105.6 4.7 %collective-permute-start.27 = (f32[1,512]{1,0:T(1,128)S(1)}, f32[1,512]{1,0:T(1,128)S(1)}, u32[]{:S(2)}, u32[]{:S(2)}) collective-permute-start(f32[1,512]{1,0:T(1,128)S(1)} %get-tuple-element.48.own_scale), channel_id=1, source_target_pairs={{0,8},{8,0},{1,9},{9,1},{2,10},{10,2},{3,11},{11,3},{4,12},{12,4},... | collective-permute-start | bytes 6152 | tf_op jit(solution)/shard_map/ppermute | solution.py:53
  135.2 16.3 %all-to-all-start.2 = ((bf16[32,32,128]{2,1,0:T(8,128)(2,1)}), bf16[32,32,128]{2,1,0:T(8,128)(2,1)S(1)}, u32[]{:S(2)}, u32[]{:S(2)}) async-start(bf16[32,32,128]{2,1,0:T(8,128)(2,1)} %shard_map.117), calls=%async_computation.2 | async-start | bytes 524288 | tf_op jit(solution)/shard_map/all_to_all | solution.py:566
  139.1 1.3 collective-permute-start.28
